TPU v7x, 1024 devices: a whole 8x8x8 slice. The times are simulated.
1024 devices in a mesh: row: 64 (over y_hi, x, core), col: 16 (over z, y_lo).
Axes of the slice: x: 8, y: 8 (y_hi: 4, y_lo: 2; y = y_hi * 2 + y_lo), z: 8, core: 2. Of those that a mesh axis runs over, the one named last changes fastest.
Arguments:
- picture_vectors: bfloat16 [16384, 1152], P(('row', 'col')), may hold values from -50 to 50
- caption_vectors: bfloat16 [16384, 1152], P(('row', 'col')), may hold values from -50 to 50
- caption_partner_position: int32 [16384], replicated, may hold values from 0 to 16383, as said below
- sharpness_factor: float32 [1], replicated, may hold values from 9 to 12
- affine_offset_array: float32 [1], replicated, may hold values from -10 to -7
Outputs:
- image_grad: float32 [16384, 1152], P(('row', 'col'))
- text_grad: float32 [16384, 1152], P(('row', 'col'))
- loss_rows: float32 [16384], P(('row', 'col'))
Inputs may be any that keep to these rules, and one draw needn't show every extreme that they name: `caption_partner_position`: each text index appears exactly once.
All inputs are finite; a program needn't handle non-finite values.
Results may differ from a plain program's by a relative error of at most 0.0023.
Values may be sent and summed in bfloat16 or wider, within the bound.
No kernel may reach another device: no remote copies, remote signals or barrier semaphores. Data moves between devices by JAX's collectives and lax.ppermute only.
A program may use at most 32 MiB of HBM per device.

v0:
```python
import jax
import jax.numpy as jnp
from jax import lax
from jax.sharding import PartitionSpec as P


def normalize(raw):
    values = raw.astype(jnp.float32)
    return values * lax.rsqrt(jnp.sum(values * values, axis=1, keepdims=True) + 1e-06)


def per_device(
    picture_vectors,
    caption_vectors,
    caption_partner_position,
    sharpness_factor,
    affine_offset_array,
):
    own_rows = picture_vectors.shape[0]
    col_count = lax.axis_size("col")
    row_count = lax.axis_size("row")
    row_place = lax.axis_index("row")
    col_place = lax.axis_index("col")
    similarity_multiplier = sharpness_factor[0]
    shift = affine_offset_array[0]
    img_block = lax.all_gather(
        normalize(picture_vectors).astype(jnp.bfloat16), "col", axis=0, tiled=True
    )
    txt_block = lax.all_gather(
        normalize(caption_vectors).astype(jnp.bfloat16), "row", axis=0, tiled=True
    )
    first_image = row_place * own_rows * col_count
    my_pairs = lax.dynamic_slice_in_dim(
        caption_partner_position, first_image, own_rows * col_count, 0
    )
    column = jnp.arange(own_rows * row_count, dtype=jnp.int32)
    text_ids = (
        column // own_rows * (own_rows * col_count) + col_place * own_rows + column % own_rows
    )
    logits = (
        similarity_multiplier
        * lax.dot_general(
            img_block, txt_block, (((1,), (1,)), ((), ())), preferred_element_type=jnp.float32
        )
        + shift
    )
    positive = (my_pairs[:, None] == text_ids[None, :]).astype(jnp.float32)
    sign = 2.0 * positive - 1.0
    partial_loss = jnp.sum(jax.nn.softplus(-sign * logits), axis=1)
    slope = (jax.nn.sigmoid(logits) - positive).astype(jnp.bfloat16)
    img_part = similarity_multiplier * jnp.dot(slope, txt_block, preferred_element_type=jnp.float32)
    img_dir, loss_rows = (
        lax.psum_scatter(img_part, "col", scatter_dimension=0, tiled=True),
        lax.psum_scatter(partial_loss, "col", scatter_dimension=0, tiled=True),
    )
    txt_dir = lax.psum_scatter(
        similarity_multiplier
        * lax.dot_general(
            slope, img_block, (((0,), (0,)), ((), ())), preferred_element_type=jnp.float32
        ),
        "row",
        scatter_dimension=0,
        tiled=True,
    )
    unused, image_back = jax.vjp(normalize, picture_vectors.astype(jnp.float32))
    unused2, text_backward = jax.vjp(normalize, caption_vectors.astype(jnp.float32))
    return (image_back(img_dir)[0], text_backward(txt_dir)[0], loss_rows)


def solution(mesh):
    in_specs = (P(("row", "col"), None), P(("row", "col"), None), P(), P(), P())
    out_specs = (P(("row", "col"), None), P(("row", "col"), None), P(("row", "col")))
    return jax.shard_map(
        per_device, mesh=mesh, in_specs=in_specs, out_specs=out_specs, check_vma=False
    )
```

profile of v0, /device:TPU:4, one launch (start us, length us, event | category | flops | bytes accessed | tf_op | source)
XLA Modules:
  0.0 376.2 jit_solution(21394224933026652)
XLA Ops:
  7.2 0.0 all-gather.2.cloned.1.call-start
  7.2 0.9 fusion.10
  8.1 1.5 fusion.11
  9.6 0.0 all-gather.2.cloned.1.call-update
  9.6 0.0 reduce-scatter.3.cloned.1.call-start
  10.9 0.8 dynamic_slice.3
  11.7 0.9 fusion.7
  12.6 0.8 fusion.8
  13.5 51.7 %all_gather.6 = bf16[256,1152]{1,0:T(8,128)(2,1)S(1)} all-gather(bf16[16,1152]{1,0:T(8,128)(2,1)S(1)} %fusion.8), channel_id=1, replica_groups=mesh['row'=64,'col'=16] {'col'}, dimensions={0}, use_global_device_ids=true | all-gather | bytes 626688 | tf_op jit(solution)/shard_map/all_gather | solution.py:26
  65.2 49.2 %all-gather.2.cloned.1.call-done = bf16[1024,1152]{1,0:T(8,128)(2,1)} async-done(((bf16[16,1152]{1,0:T(8,128)(2,1)}), bf16[1024,1152]{1,0:T(8,128)(2,1)}) %all-gather.2.cloned.1.call-update) | async-done | bytes 2359312 | tf_op jit(solution)/shard_map/all_gather | solution.py:29
  114.4 0.0 copy-start.2
  114.4 3.3 fusion.6
  117.8 0.0 copy-done.2
  117.8 2.0 convolution_multiply_fusion.1
  119.7 0.0 reduce-scatter.3.cloned.1.call-update
  119.7 0.0 reduce-scatter.5.cloned.1.call-start
  119.8 3.2 convolution_multiply_fusion
  123.0 0.0 copy-start
  123.0 0.0 copy-start.1
  123.0 0.0 reduce-scatter.5.cloned.1.call-update
  123.0 1.3 dynamic-slice
  124.9 36.2 %all-reduce = f32[256]{0:T(256)S(1)} all-reduce(f32[256]{0:T(256)S(1)} %get-tuple-element.3), channel_id=4, replica_groups=mesh['row'=64,'col'=16] {'col'}, use_global_device_ids=true, to_apply=%region_7.8.clone | all-reduce | flops 256 | bytes 2048
  161.2 0.6 dynamic-slice.1
  161.8 36.8 %reduce-scatter.3.cloned.1.call-done = f32[16,1152]{1,0:T(8,128)} async-done(((f32[256,1152]{1,0:T(8,128)}), f32[16,1152]{1,0:T(8,128)}) %reduce-scatter.3.cloned.1.call-update) | async-done | bytes 73744 | tf_op jit(solution)/shard_map/reduce_scatter | solution.py:53
  198.5 0.0 copy-done
  198.5 1.0 fusion.9
  199.5 1.6 add_add_fusion.1
  201.2 165.9 %reduce-scatter.5.cloned.1.call-done = f32[16,1152]{1,0:T(8,128)} async-done(((f32[1024,1152]{1,0:T(8,128)}), f32[16,1152]{1,0:T(8,128)}) %reduce-scatter.5.cloned.1.call-update) | async-done | bytes 73744 | tf_op jit(solution)/shard_map/reduce_scatter | solution.py:56
  367.0 0.0 copy-done.1
  367.1 1.0 fusion.12
  368.1 1.6 add_add_fusion
  (5 shorter events, 0.0 us)
Async XLA Ops:
  7.2 107.3 %all-gather.2.cloned.1.call-start = ((), (), s32[]{:S(2)}) async-start(), calls=%async_computation.2 | async-start | bytes 2396160 | tf_op jit(solution)/shard_map/all_gather | solution.py:29
  9.6 188.9 %reduce-scatter.3.cloned.1.call-start = ((), (), s32[]{:S(2)}) async-start(), calls=%async_computation.3 | async-start | bytes 1253376 | tf_op jit(solution)/shard_map/reduce_scatter | solution.py:53
  114.4 3.3 copy-start.2
  119.7 247.3 %reduce-scatter.5.cloned.1.call-start = ((), (), s32[]{:S(2)}) async-start(), calls=%async_computation.4 | async-start | bytes 4792320 | tf_op jit(solution)/shard_map/reduce_scatter | solution.py:56
  123.0 75.5 %copy-start = (bf16[16,1152]{1,0:T(8,128)(2,1)S(1)}, bf16[16,1152]{1,0:T(8,128)(2,1)}, u32[]{:S(2)}) copy-start(bf16[16,1152]{1,0:T(8,128)(2,1)} %param.5) | copy-start | bytes 110596
  123.0 244.1 %copy-start.1 = (bf16[16,1152]{1,0:T(8,128)(2,1)S(1)}, bf16[16,1152]{1,0:T(8,128)(2,1)}, u32[]{:S(2)}) copy-start(bf16[16,1152]{1,0:T(8,128)(2,1)} %param.6) | copy-start | bytes 110596
Sparse Core Ops, SparseCore 0:
  12.9 101.4 all-gather.1
  119.9 78.6 reduce-scatter.2
  204.4 162.5 reduce-scatter.4
where the time goes:
time: 377 us; the launch traced here: 376 us
  waiting for transfers between devices  252 us (67%)
  blocking collectives  87.9 us (23%)
  between operations  15.7 us (4%)
  other arithmetic  9.36 us (2%)
  matrix products  8.49 us (2%)
    reduce_scatter x1, waiting for transfers between devices, per_device(): lax.psum_scatter(similarity_multiplier * lax.dot_general(slope, img_block...  166 us
    all_gather x1, blocking collectives, per_device(): lax.all_gather(normalize(picture_vectors).astype(jnp.bfloat16), 'col', ax...  51.7 us
    all_gather x1, waiting for transfers between devices, per_device(): lax.all_gather(normalize(caption_vectors).astype(jnp.bfloat16), 'row', ax...  49.2 us
    reduce_scatter x1, waiting for transfers between devices, per_device(): lax.psum_scatter(img_part, 'col', scatter_dimension=0, tiled=True)  36.8 us
    unnamed x1, blocking collectives  36.2 us
  transfers between devices with their start and end apart: 3, of which 3 were waited for; matrix products, arithmetic and copies ran while one was open for 3% of the time, Pallas kernels for 0%

commit v1 on v0

v1 whole, which is shorter than its diff:
```python
import jax
import jax.numpy as jnp
from jax import lax
from jax.sharding import Mesh, PartitionSpec as P

FINE = ("yhi", "x", "core", "z", "ylo")
FINE_SIZES = (4, 8, 2, 8, 2)
IMAGE_GROUP = ("core", "z", "ylo")
TEXT_GROUP = ("yhi", "x")
SEND_SCALE = 32.0


def normalize(raw):
    values = raw.astype(jnp.float32)
    return values * lax.rsqrt(jnp.sum(values * values, axis=1, keepdims=True) + 1e-06)


def gather(block, axes):
    copies = jnp.broadcast_to(block[None], (lax.axis_size(axes),) + block.shape)
    return lax.all_to_all(copies, axes, 0, 0, tiled=True)


def scatter(parts, axes):
    count = lax.axis_size(axes)
    return lax.all_to_all(
        parts.reshape(count, parts.shape[0] // count, parts.shape[1]), axes, 0, 0, tiled=True
    )


def per_device(
    picture_vectors,
    caption_vectors,
    caption_partner_position,
    sharpness_factor,
    affine_offset_array,
):
    own_rows, width = picture_vectors.shape
    image_devices = lax.axis_size(IMAGE_GROUP)
    text_devices = lax.axis_size(TEXT_GROUP)
    similarity_multiplier = sharpness_factor[0]
    shift = affine_offset_array[0]
    txt_block = gather(normalize(caption_vectors).astype(jnp.bfloat16), TEXT_GROUP).reshape(-1, width)
    img_block = gather(normalize(picture_vectors).astype(jnp.bfloat16), IMAGE_GROUP).reshape(-1, width)
    group_rows = own_rows * image_devices
    my_pairs = lax.dynamic_slice_in_dim(
        caption_partner_position, lax.axis_index(TEXT_GROUP) * group_rows, group_rows, 0
    )
    column = jnp.arange(own_rows * text_devices, dtype=jnp.int32)
    text_ids = (
        column // own_rows * group_rows + lax.axis_index(IMAGE_GROUP) * own_rows + column % own_rows
    )
    logits = (
        similarity_multiplier
        * lax.dot_general(
            img_block, txt_block, (((1,), (1,)), ((), ())), preferred_element_type=jnp.float32
        )
        + shift
    )
    positive = (my_pairs[:, None] == text_ids[None, :]).astype(jnp.float32)
    sign = 2.0 * positive - 1.0
    partial_loss = jnp.sum(jax.nn.softplus(-sign * logits), axis=1)
    slope = (jax.nn.sigmoid(logits) - positive).astype(jnp.bfloat16)
    txt_part = lax.dot_general(
        slope, img_block, (((0,), (0,)), ((), ())), preferred_element_type=jnp.float32
    )
    txt_terms = scatter((SEND_SCALE * txt_part).astype(jnp.float16), TEXT_GROUP)
    img_part = jnp.dot(slope, txt_block, preferred_element_type=jnp.float32)
    loss_high = partial_loss.astype(jnp.float16)
    loss_low = (partial_loss - loss_high.astype(jnp.float32)).astype(jnp.float16)
    lane = jnp.arange(128)[None, :]
    losses = jnp.where(lane == 0, loss_high[:, None], jnp.where(lane == 1, loss_low[:, None], 0))
    img_terms = scatter(
        jnp.concatenate([(SEND_SCALE * img_part).astype(jnp.float16), losses], axis=1), IMAGE_GROUP
    )
    img_sum = jnp.sum(img_terms.astype(jnp.float32), axis=0)
    img_dir = (similarity_multiplier / SEND_SCALE) * img_sum[:, :width]
    loss_rows = img_sum[:, width] + img_sum[:, width + 1]
    txt_dir = (similarity_multiplier / SEND_SCALE) * jnp.sum(txt_terms.astype(jnp.float32), axis=0)
    unused, image_back = jax.vjp(normalize, picture_vectors.astype(jnp.float32))
    unused2, text_backward = jax.vjp(normalize, caption_vectors.astype(jnp.float32))
    return (image_back(img_dir)[0], text_backward(txt_dir)[0], loss_rows)


def solution(mesh):
    fine = Mesh(mesh.devices.reshape(FINE_SIZES), FINE)
    in_specs = (P(FINE, None), P(FINE, None), P(), P(), P())
    out_specs = (P(FINE, None), P(FINE, None), P(FINE))
    return jax.shard_map(
        per_device, mesh=fine, in_specs=in_specs, out_specs=out_specs, check_vma=False
    )
```

time: 377 us -> 187 us (0.50)
  the two profiles are of different devices: /device:TPU:4 before, /device:TPU:2 now
where the time goes in v1:
time: 187 us; the launch traced here: 186 us
  waiting for transfers between devices  127 us (68%)
  starting transfers between devices  42.1 us (23%)
  other arithmetic  6.33 us (3%)
  matrix products  5.85 us (3%)
  local copies, waits for them, and re-layouts  2.96 us (2%)
  between operations  2.04 us (1%)
    all_to_all x2, waiting for transfers between devices, scatter(): lax.all_to_all(parts.reshape(count, parts.shape[0] // count, parts.shape[...  63.4 us
    all_to_all x2, waiting for transfers between devices, gather(): return lax.all_to_all(copies, axes, 0, 0, tiled=True)  63.3 us
    all_to_all x2, starting transfers between devices, gather(): return lax.all_to_all(copies, axes, 0, 0, tiled=True)  30.6 us
    all_to_all x2, starting transfers between devices, scatter(): lax.all_to_all(parts.reshape(count, parts.shape[0] // count, parts.shape[...  11.5 us
  transfers between devices with their start and end apart: 4, of which 4 were waited for; matrix products, arithmetic and copies ran while one was open for 3% of the time, Pallas kernels for 0%

profile of v1, /device:TPU:2, one launch (start us, length us, event | category | flops | bytes accessed | tf_op | source)
XLA Modules:
  0.0 186.0 jit_solution(14574928538277158660)
XLA Ops:
  0.6 0.9 fusion.9
  1.5 0.8 fusion.10
  2.4 1.1 broadcast_in_dim.44
  3.5 0.0 copy-start
  3.5 18.3 %all-to-all-start = ((bf16[32,16,1152]{2,1,0:T(8,128)(2,1)}), bf16[32,16,1152]{2,1,0:T(8,128)(2,1)S(1)}, u32[]{:S(2)}, u32[]{:S(2)}) async-start(bf16[32,16,1152]{2,1,0:T(8,128)(2,1)} %broadcast_in_dim.44), calls=%async_computation | async-start | bytes 2359296 | tf_op jit(solution)/shard_map/all_to_all | solution.py:20
  21.8 0.0 copy-done
  21.8 0.1 fusion.12
  21.9 0.1 fusion.13
  22.0 31.5 %all-to-all-done = bf16[32,16,1152]{2,1,0:T(8,128)(2,1)S(1)} async-done(((bf16[32,16,1152]{2,1,0:T(8,128)(2,1)}), bf16[32,16,1152]{2,1,0:T(8,128)(2,1)S(1)}, u32[]{:S(2)}, u32[]{:S(2)}) %all-to-all-start) | async-done | bytes 1179680 | tf_op jit(solution)/shard_map/all_to_all | solution.py:20
  53.5 1.1 broadcast_in_dim.64
  54.6 12.3 %all-to-all-start.1 = ((bf16[32,16,1152]{2,1,0:T(8,128)(2,1)}), bf16[32,16,1152]{2,1,0:T(8,128)(2,1)S(1)}, u32[]{:S(2)}, u32[]{:S(2)}) async-start(bf16[32,16,1152]{2,1,0:T(8,128)(2,1)} %broadcast_in_dim.64), calls=%async_computation.1 | async-start | bytes 2359296 | tf_op jit(solution)/shard_map/all_to_all | solution.py:20
  68.2 0.8 dynamic_slice.3
  69.0 31.8 %all-to-all-done.1 = bf16[32,16,1152]{2,1,0:T(8,128)(2,1)S(1)} async-done(((bf16[32,16,1152]{2,1,0:T(8,128)(2,1)}), bf16[32,16,1152]{2,1,0:T(8,128)(2,1)S(1)}, u32[]{:S(2)}, u32[]{:S(2)}) %all-to-all-start.1) | async-done | bytes 1179680 | tf_op jit(solution)/shard_map/all_to_all | solution.py:20
  100.8 1.6 fusion.8
  102.4 0.0 copy-start.2
  102.4 2.1 %fusion.1 = f16[512,1152]{1,0:T(8,128)(2,1)} fusion(bf16[512,1152]{1,0:T(8,128)(2,1)S(1)} %bitcast.16, f32[512,512]{0,1:T(8,128)S(1)} %get-tuple-element.6, s32[512]{0:T(512)S(1)} %dynamic_slice.3, s32[512]{0:T(512)S(1)} %fusion.22), kind=kOutput, calls=%fused_computation.4 | convolution fusion | flops 606994432 | bytes 3411968 | tf_op jit(solution)/shard_map/dot_general | solution.py:63
  104.5 0.0 copy-done.2
  104.5 7.5 %all-to-all-start.3 = ((f16[32,16,1152]{2,1,0:T(8,128)(2,1)}), f16[32,16,1152]{2,1,0:T(8,128)(2,1)S(1)}, u32[]{:S(2)}, u32[]{:S(2)}) async-start(f16[32,16,1152]{2,1,0:T(8,128)(2,1)} %bitcast.17), calls=%async_computation.3 | async-start | bytes 2359296 | tf_op jit(solution)/shard_map/all_to_all | solution.py:25
  112.0 0.2 select_select_fusion
  112.3 2.2 %fusion = f16[512,1152]{1,0:T(8,128)(2,1)S(1)} fusion(bf16[512,1152]{1,0:T(8,128)(2,1)S(1)} %bitcast.14, f32[512,512]{0,1:T(8,128)} %copy-done.2, s32[512]{0:T(512)S(1)} %dynamic_slice.3, s32[512]{0:T(512)S(1)} %fusion.22), kind=kOutput, calls=%fused_computation.3 | convolution fusion | flops 606994432 | bytes 3411968 | tf_op jit(solution)/shard_map/dot_general | solution.py:67
  114.5 1.4 pad_maximum_fusion
  115.8 29.8 %all-to-all-done.3 = f16[32,16,1152]{2,1,0:T(8,128)(2,1)S(1)} async-done(((f16[32,16,1152]{2,1,0:T(8,128)(2,1)}), f16[32,16,1152]{2,1,0:T(8,128)(2,1)S(1)}, u32[]{:S(2)}, u32[]{:S(2)}) %all-to-all-start.3) | async-done | bytes 1179680 | tf_op jit(solution)/shard_map/all_to_all | solution.py:25
  145.7 4.0 %all-to-all-start.2 = ((f16[32,16,1280]{2,1,0:T(8,128)(2,1)}), f16[32,16,1280]{2,1,0:T(8,128)(2,1)S(1)}, u32[]{:S(2)}, u32[]{:S(2)}) async-start(f16[32,16,1280]{2,1,0:T(8,128)(2,1)} %bitcast.4), calls=%async_computation.2 | async-start | bytes 2621440 | tf_op jit(solution)/shard_map/all_to_all | solution.py:25
  149.6 0.0 copy-start.1
  149.6 0.2 convert_reduce_fusion.1
  149.8 0.1 fusion.14
  149.9 0.7 add_add_fusion
  150.7 33.5 %all-to-all-done.2 = f16[32,16,1280]{2,1,0:T(8,128)(2,1)S(1)} async-done(((f16[32,16,1280]{2,1,0:T(8,128)(2,1)}), f16[32,16,1280]{2,1,0:T(8,128)(2,1)S(1)}, u32[]{:S(2)}, u32[]{:S(2)}) %all-to-all-start.2) | async-done | bytes 1310752 | tf_op jit(solution)/shard_map/all_to_all | solution.py:25
  184.2 0.2 convert_reduce_fusion
  184.4 0.7 fusion.15
  185.1 0.0 copy-done.1
  185.1 0.1 fusion.11
  185.2 0.7 add_add_fusion.1
  (7 shorter events, 0.1 us)
Async XLA Ops:
  3.5 18.3 %copy-start = (bf16[16,1152]{1,0:T(8,128)(2,1)S(1)}, bf16[16,1152]{1,0:T(8,128)(2,1)}, u32[]{:S(2)}) copy-start(bf16[16,1152]{1,0:T(8,128)(2,1)} %param.6) | copy-start | bytes 110596
  3.5 50.1 %all-to-all-start = ((bf16[32,16,1152]{2,1,0:T(8,128)(2,1)}), bf16[32,16,1152]{2,1,0:T(8,128)(2,1)S(1)}, u32[]{:S(2)}, u32[]{:S(2)}) async-start(bf16[32,16,1152]{2,1,0:T(8,128)(2,1)} %broadcast_in_dim.44), calls=%async_computation | async-start | bytes 2359296 | tf_op jit(solution)/shard_map/all_to_all | solution.py:20
  54.6 46.2 %all-to-all-start.1 = ((bf16[32,16,1152]{2,1,0:T(8,128)(2,1)}), bf16[32,16,1152]{2,1,0:T(8,128)(2,1)S(1)}, u32[]{:S(2)}, u32[]{:S(2)}) async-start(bf16[32,16,1152]{2,1,0:T(8,128)(2,1)} %broadcast_in_dim.64), calls=%async_computation.1 | async-start | bytes 2359296 | tf_op jit(solution)/shard_map/all_to_all | solution.py:20
  102.4 2.1 %copy-start.2 = (f32[512,512]{0,1:T(8,128)}, f32[512,512]{0,1:T(8,128)S(1)}, u32[]{:S(2)}) copy-start(f32[512,512]{0,1:T(8,128)S(1)} %get-tuple-element.6) | copy-start | bytes 3145732
  104.5 41.2 %all-to-all-start.3 = ((f16[32,16,1152]{2,1,0:T(8,128)(2,1)}), f16[32,16,1152]{2,1,0:T(8,128)(2,1)S(1)}, u32[]{:S(2)}, u32[]{:S(2)}) async-start(f16[32,16,1152]{2,1,0:T(8,128)(2,1)} %bitcast.17), calls=%async_computation.3 | async-start | bytes 2359296 | tf_op jit(solution)/shard_map/all_to_all | solution.py:25
  145.7 38.5 %all-to-all-start.2 = ((f16[32,16,1280]{2,1,0:T(8,128)(2,1)}), f16[32,16,1280]{2,1,0:T(8,128)(2,1)S(1)}, u32[]{:S(2)}, u32[]{:S(2)}) async-start(f16[32,16,1280]{2,1,0:T(8,128)(2,1)} %bitcast.4), calls=%async_computation.2 | async-start | bytes 2621440 | tf_op jit(solution)/shard_map/all_to_all | solution.py:25
  149.6 35.5 %copy-start.1 = (bf16[16,1152]{1,0:T(8,128)(2,1)S(1)}, bf16[16,1152]{1,0:T(8,128)(2,1)}, u32[]{:S(2)}) copy-start(bf16[16,1152]{1,0:T(8,128)(2,1)} %param.5) | copy-start | bytes 110596

commit v2 on v1

v2 whole, which is shorter than its diff:
```python
import jax
import jax.numpy as jnp
from jax import lax
from jax.sharding import Mesh, PartitionSpec as P

FINE = ("y2", "y1", "x", "core", "z2", "z1", "z0", "y0")
FINE_SIZES = (2, 2, 8, 2, 2, 2, 2, 2)
IMAGE_GROUP = ("core", "z2", "z1", "z0", "y2")
TEXT_GROUP = ("y1", "x", "y0")
SEND_SCALE = 2.0
LOSS_SCALE = 0.125


def normalize(raw):
    values = raw.astype(jnp.float32)
    return values * lax.rsqrt(jnp.sum(values * values, axis=1, keepdims=True) + 1e-06)


def gather(block, axes):
    copies = jnp.broadcast_to(block[None], (lax.axis_size(axes),) + block.shape)
    return lax.all_to_all(copies, axes, 0, 0, tiled=True)


def scatter(parts, axes):
    count = lax.axis_size(axes)
    return lax.all_to_all(
        parts.reshape(count, parts.shape[0] // count, parts.shape[1]), axes, 0, 0, tiled=True
    )


def halve(total, axis, place, tie=None):
    mine = lax.axis_index(axis)
    sent = lax.dynamic_index_in_dim(total, 1 - mine, place, keepdims=False).astype(jnp.float16)
    if tie is not None:
        sent = sent + jnp.minimum(jnp.abs(tie), 0).astype(jnp.float16)
    came = lax.ppermute(sent, axis, [(0, 1), (1, 0)])
    return lax.dynamic_index_in_dim(total, mine, place, keepdims=False) + came.astype(jnp.float32)


def per_device(
    picture_vectors,
    caption_vectors,
    caption_partner_position,
    sharpness_factor,
    affine_offset_array,
):
    own_rows, width = picture_vectors.shape
    similarity_multiplier = sharpness_factor[0]
    shift = affine_offset_array[0]
    txt_block = gather(normalize(caption_vectors).astype(jnp.bfloat16), TEXT_GROUP).reshape(-1, width)
    img_block = normalize(picture_vectors).astype(jnp.bfloat16)
    for axes in (("y2",), ("z2", "z1", "z0")):
        img_block = lax.all_gather(img_block, axes, axis=0, tiled=True)
    img_block = jnp.concatenate([img_block, lax.ppermute(img_block, "core", [(0, 1), (1, 0)])])
    ids = jnp.arange(caption_partner_position.shape[0], dtype=jnp.int32)

    def of_group(array, group):
        rows = array.reshape(FINE_SIZES + (own_rows,))
        for place, axis in enumerate(FINE):
            if axis not in group:
                rows = lax.dynamic_slice_in_dim(rows, lax.axis_index(axis), 1, place)
        order = [FINE.index(axis) for axis in group]
        order = order + [i for i in range(len(FINE) + 1) if i not in order]
        return rows.transpose(order).reshape(-1)

    my_pairs = of_group(caption_partner_position, IMAGE_GROUP)
    half = my_pairs.shape[0] // 2
    my_pairs = lax.dynamic_slice_in_dim(
        jnp.concatenate([my_pairs, my_pairs]), lax.axis_index("core") * half, 2 * half, 0
    )
    text_ids = of_group(ids, TEXT_GROUP)
    logits = (
        similarity_multiplier
        * lax.dot_general(
            img_block, txt_block, (((1,), (1,)), ((), ())), preferred_element_type=jnp.float32
        )
        + shift
    )
    positive = (my_pairs[:, None] == text_ids[None, :]).astype(jnp.float32)
    sign = 2.0 * positive - 1.0
    loss = jnp.sum(jax.nn.softplus(-sign * logits), axis=1)
    slope = (jax.nn.sigmoid(logits) - positive).astype(jnp.bfloat16)
    txt_part = lax.dot_general(
        slope, img_block, (((0,), (0,)), ((), ())), preferred_element_type=jnp.float32
    )
    txt_terms = scatter((SEND_SCALE * txt_part).astype(jnp.float16), TEXT_GROUP)
    img_part = SEND_SCALE * jnp.dot(slope, txt_block, preferred_element_type=jnp.float32)
    img_part = jnp.concatenate(
        [img_part, jnp.broadcast_to(loss[:, None] * LOSS_SCALE, (2 * half, 128))], axis=1
    )
    came = lax.ppermute(img_part[half:].astype(jnp.float16), "core", [(0, 1), (1, 0)])
    img_sum = img_part[:half] + came.astype(jnp.float32)
    img_sum = img_sum.reshape(2, 2, 2, 2, own_rows, width + 128)
    img_sum = halve(img_sum, "z0", 2)
    img_sum = halve(img_sum, "z1", 1)
    img_sum = halve(img_sum, "z2", 0)
    img_sum = halve(img_sum, "y2", 0, txt_terms[0, 0, 0])
    loss = img_sum[:, width] / LOSS_SCALE
    img_sum = img_sum[:, :width]
    img_dir = (similarity_multiplier / SEND_SCALE) * img_sum
    txt_dir = (similarity_multiplier / SEND_SCALE) * jnp.sum(txt_terms.astype(jnp.float32), axis=0)
    unused, image_back = jax.vjp(normalize, picture_vectors.astype(jnp.float32))
    unused2, text_backward = jax.vjp(normalize, caption_vectors.astype(jnp.float32))
    return (image_back(img_dir)[0], text_backward(txt_dir)[0], loss)


def solution(mesh):
    fine = Mesh(mesh.devices.reshape(FINE_SIZES), FINE)
    in_specs = (P(FINE, None), P(FINE, None), P(), P(), P())
    out_specs = (P(FINE, None), P(FINE, None), P(FINE))
    return jax.shard_map(
        per_device, mesh=fine, in_specs=in_specs, out_specs=out_specs, check_vma=False
    )
```

time: 187 us -> 155 us (0.83)
  waiting for transfers between devices: 127 us -> 32.5 us
  blocking collectives: 0 us -> 43.1 us
  starting transfers between devices: 42.1 us -> 61.5 us
    all_to_all x2 -> x1, waiting for transfers between devices: 63.3 us -> 0.01 us  [gather(): return lax.all_to_all(copies, axes, 0, 0, tiled=True)]
    all_to_all x2 -> x1, waiting for transfers between devices: 63.4 us -> 9.16 us  [scatter(): lax.all_to_all(parts.reshape(count, parts.shape[0] // count, parts.shape[...]
    all_gather x0 -> x2, blocking collectives: none -> 43.1 us  [per_device(): img_block = lax.all_gather(img_block, axes, axis=0, tiled=True)]
    ppermute x0 -> x6, waiting for transfers between devices: none -> 23.3 us  [the longest x4 21.4 us: halve(): came = lax.ppermute(sent, axis, [(0, 1), (1, 0)])]
    ppermute x0 -> x6, starting transfers between devices: none -> 18.8 us  [the longest x4 14.5 us: halve(): came = lax.ppermute(sent, axis, [(0, 1), (1, 0)])]
    all_to_all x2 -> x1, starting transfers between devices: 11.5 us -> 25.8 us  [scatter(): lax.all_to_all(parts.reshape(count, parts.shape[0] // count, parts.shape[...]
    all_to_all x2 -> x1, starting transfers between devices: 30.6 us -> 16.9 us  [gather(): return lax.all_to_all(copies, axes, 0, 0, tiled=True)]
  transfers between devices with their start and end apart: 4 -> 8, of which waited for: 4 -> 5; matrix products, arithmetic and copies ran while one was open for 3% -> 3% of each run, Pallas kernels for 0% -> 0%
where the time goes in v2:
time: 155 us
  starting transfers between devices  61.5 us (40%)
  blocking collectives  43.1 us (28%)
  waiting for transfers between devices  32.5 us (21%)
  other arithmetic  6.27 us (4%)
  matrix products  4.63 us (3%)
  local copies, waits for them, and re-layouts  3.56 us (2%)
  between operations  3.05 us (2%)
    all_gather x2, blocking collectives, per_device(): img_block = lax.all_gather(img_block, axes, axis=0, tiled=True)  43.1 us
    all_to_all x1, starting transfers between devices, scatter(): lax.all_to_all(parts.reshape(count, parts.shape[0] // count, parts.shape[...  25.8 us
    ppermute x4, waiting for transfers between devices, halve(): came = lax.ppermute(sent, axis, [(0, 1), (1, 0)])  21.4 us
    all_to_all x1, starting transfers between devices, gather(): return lax.all_to_all(copies, axes, 0, 0, tiled=True)  16.9 us
    ppermute x4, starting transfers between devices, halve(): came = lax.ppermute(sent, axis, [(0, 1), (1, 0)])  14.5 us
    all_to_all x1, waiting for transfers between devices, scatter(): lax.all_to_all(parts.reshape(count, parts.shape[0] // count, parts.shape[...  9.16 us
  transfers between devices with their start and end apart: 8, of which 5 were waited for; matrix products, arithmetic and copies ran while one was open for 3% of the time, Pallas kernels for 0%

profile of v2, /device:TPU:2, one launch (start us, length us, event | category | flops | bytes accessed | tf_op | source)
XLA Modules:
  0.0 154.7 jit_solution(16041028248697888857)
XLA Ops:
  0.6 0.9 fusion.17
  1.5 0.5 copy-done.8
  2.1 0.8 fusion.18
  2.9 1.1 broadcast_in_dim.8
  4.0 16.9 %all-to-all-start = ((bf16[32,16,1152]{2,1,0:T(8,128)(2,1)}), bf16[32,16,1152]{2,1,0:T(8,128)(2,1)S(1)}, u32[]{:S(2)}, u32[]{:S(2)}) async-start(bf16[32,16,1152]{2,1,0:T(8,128)(2,1)} %broadcast_in_dim.8), calls=%async_computation | async-start | bytes 2359296 | tf_op jit(solution)/shard_map/all_to_all | solution.py:21
  21.0 0.1 fusion.14
  21.1 0.1 fusion.15
  21.2 11.9 %all_gather.6 = bf16[32,1152]{1,0:T(8,128)(2,1)S(1)} all-gather(bf16[16,1152]{1,0:T(8,128)(2,1)S(1)} %fusion.15), channel_id=1, replica_groups=mesh['y2'=2,'y1'=2,'x'=8,'core'=2,'z2'=2,'z1'=2,'z0'=2,'y0'=2] {'y2'}, dimensions={0}, use_global_device_ids=true | all-gather | bytes 110592 | tf_op jit(solution)/shard_map/all_gather | solution.py:53
  33.0 31.3 %all_gather.7 = bf16[256,1152]{1,0:T(8,128)(2,1)S(1)} all-gather(bf16[32,1152]{1,0:T(8,128)(2,1)S(1)} %all_gather.6), channel_id=1, replica_groups=mesh['y2'=2,'y1'=2,'x'=8,'core'=2,'z2'=2,'z1'=2,'z0'=2,'y0'=2] {'z2','z1..., dimensions={0}, use_global_device_ids=true | all-gather | bytes 663552 | tf_op jit(solution)/shard_map/all_gather | solution.py:53
  64.3 1.9 %collective-permute-start = (bf16[256,1152]{1,0:T(8,128)(2,1)S(1)}, bf16[256,1152]{1,0:T(8,128)(2,1)S(1)}, u32[]{:S(2)}, u32[]{:S(2)}) collective-permute-start(bf16[256,1152]{1,0:T(8,128)(2,1)S(1)} %all_gather.7), channel_id=1, source_target_pairs={{0,16},{16,0},{1,17},{17,1},{2,18},{18,2},{3,19},{19,3},{4,20},{20... | collective-permute-start | bytes 1769480 | tf_op jit(solution)/shard_map/ppermute | solution.py:54
  67.6 0.7 reshape.115
  68.3 0.1 reshape.116
  68.4 0.5 iota_multiply_fusion
  69.0 0.1 eq.16
  69.1 0.1 dynamic_slice.46
  69.2 0.0 collective-permute-done
  69.2 0.1 constant_dynamic-update-slice_fusion
  69.3 0.0 all-to-all-done
  69.3 1.6 %fusion.10 = (f32[512]{0:T(512)S(1)}, f32[512,512]{0,1:T(8,128)S(1)}) fusion(s32[512]{0:T(512)S(1)} %dynamic_slice.46, s32[512]{0:T(512)S(1)} %eq.16, f32[]{:T(128)} %bitcast.32, bf16[512,1152]{1,0:T(8,128)(2,1)S(1)} %constant_dynamic-update-slice_fusion, bf16[512,1152]{1,0:T(8,128)(2,1)S(1)} %bitcast.34, f32[]{:T(128)} %bitcast.31), kind=kOutput, calls=%fused_computation.20 | convolution fusion | flops 607649280 | bytes 3414024 | tf_op jit(solution)/shard_map/dot_general | solution.py:74
  70.9 1.0 convolution_multiply_fusion.1
  71.9 0.1 broadcast_in_dim.9
  72.0 0.9 fusion.4
  72.9 2.4 %collective-permute-start.1 = (f16[256,1280]{1,0:T(8,128)(2,1)}, f16[256,1280]{1,0:T(8,128)(2,1)S(1)}, u32[]{:S(2)}, u32[]{:S(2)}) collective-permute-start(f16[256,1280]{1,0:T(8,128)(2,1)} %fusion.4), channel_id=1, source_target_pairs={{0,16},{16,0},{1,17},{17,1},{2,18},{18,2},{3,19},{19,3},{4,20},{20... | collective-permute-start | bytes 1966088 | tf_op jit(solution)/shard_map/ppermute | solution.py:91
  75.3 1.9 %collective-permute-done.1 = f16[256,1280]{1,0:T(8,128)(2,1)S(1)} collective-permute-done((f16[256,1280]{1,0:T(8,128)(2,1)}, f16[256,1280]{1,0:T(8,128)(2,1)S(1)}, u32[]{:S(2)}, u32[]{:S(2)}) %collective-permute-start.1) | collective-permute-done | bytes 655392 | tf_op jit(solution)/shard_map/ppermute | solution.py:91
  77.3 0.1 fusion.3
  77.4 0.1 constant_dynamic-slice_fusion
  77.6 3.8 %collective-permute-start.2 = (f16[2,2,2,16,1280]{4,3,2,0,1:T(8,128)(2,1)S(1)}, f16[2,2,2,16,1280]{4,3,2,0,1:T(8,128)(2,1)S(1)}, u32[]{:S(2)}, u32[]{:S(2)}) collective-permute-start(f16[2,2,2,16,1280]{4,3,2,0,1:T(8,128)(2,1)S(1)} %fusion.11), channel_id=1, source_target_pairs={{0,2},{2,0},{1,3},{3,1},{4,6},{6,4},{5,7},{7,5},{8,10},{10,8},{9,1... | collective-permute-start | bytes 983048 | tf_op jit(solution)/shard_map/ppermute | solution.py:36
  81.4 2.1 %fusion = f16[512,1152]{1,0:T(8,128)(2,1)} fusion(bf16[512,1152]{1,0:T(8,128)(2,1)S(1)} %copy-done.4, f32[512,512]{0,1:T(8,128)S(1)} %copy-done.11, s32[512]{0:T(512)S(1)} %dynamic_slice.46, s32[512]{0:T(512)S(1)} %eq.16), kind=kOutput, calls=%fused_computation.3 | convolution fusion | flops 606994432 | bytes 3411968 | tf_op jit(solution)/shard_map/dot_general | solution.py:83
  83.5 25.8 %all-to-all-start.1 = ((f16[32,16,1152]{2,1,0:T(8,128)(2,1)}), f16[32,16,1152]{2,1,0:T(8,128)(2,1)S(1)}, u32[]{:S(2)}, u32[]{:S(2)}) async-start(f16[32,16,1152]{2,1,0:T(8,128)(2,1)} %bitcast.12), calls=%async_computation.1 | async-start | bytes 2359296 | tf_op jit(solution)/shard_map/all_to_all | solution.py:26
  109.3 0.0 collective-permute-done.2
  109.3 0.1 bitcast_add_fusion
  109.4 2.2 %collective-permute-start.3 = (f16[2,2,16,1280]{3,2,1,0:T(8,128)(2,1)S(1)}, f16[2,2,16,1280]{3,2,1,0:T(8,128)(2,1)S(1)}, u32[]{:S(2)}, u32[]{:S(2)}) collective-permute-start(f16[2,2,16,1280]{3,2,1,0:T(8,128)(2,1)S(1)} %fusion.12), channel_id=1, source_target_pairs={{0,4},{4,0},{1,5},{5,1},{2,6},{6,2},{3,7},{7,3},{8,12},{12,8},{9,1... | collective-permute-start | bytes 491528 | tf_op jit(solution)/shard_map/ppermute | solution.py:36
  111.6 0.0 copy-start
  111.6 9.4 %collective-permute-done.3 = f16[2,2,16,1280]{3,2,1,0:T(8,128)(2,1)S(1)} collective-permute-done((f16[2,2,16,1280]{3,2,1,0:T(8,128)(2,1)S(1)}, f16[2,2,16,1280]{3,2,1,0:T(8,128)(2,1)S(1)}, u32[]{:S(2)}, u32[]{:S(2)}) %collective-permute-start.3) | collective-permute-done | bytes 163872 | tf_op jit(solution)/shard_map/ppermute | solution.py:36
  121.1 0.0 copy-start.2
  121.2 4.3 %collective-permute-start.4 = (f16[2,16,1280]{2,1,0:T(8,128)(2,1)S(1)}, f16[2,16,1280]{2,1,0:T(8,128)(2,1)S(1)}, u32[]{:S(2)}, u32[]{:S(2)}) collective-permute-start(f16[2,16,1280]{2,1,0:T(8,128)(2,1)S(1)} %fusion.13), channel_id=1, source_target_pairs={{0,8},{8,0},{1,9},{9,1},{2,10},{10,2},{3,11},{11,3},{4,12},{12,4},... | collective-permute-start | bytes 245768 | tf_op jit(solution)/shard_map/ppermute | solution.py:36
  125.5 0.0 copy-start.7
  125.5 6.7 %collective-permute-done.4 = f16[2,16,1280]{2,1,0:T(8,128)(2,1)S(1)} collective-permute-done((f16[2,16,1280]{2,1,0:T(8,128)(2,1)S(1)}, f16[2,16,1280]{2,1,0:T(8,128)(2,1)S(1)}, u32[]{:S(2)}, u32[]{:S(2)}) %collective-permute-start.4) | collective-permute-done | bytes 81952 | tf_op jit(solution)/shard_map/ppermute | solution.py:36
  132.2 9.2 %all-to-all-done.1 = f16[32,16,1152]{2,1,0:T(8,128)(2,1)S(1)} async-done(((f16[32,16,1152]{2,1,0:T(8,128)(2,1)}), f16[32,16,1152]{2,1,0:T(8,128)(2,1)S(1)}, u32[]{:S(2)}, u32[]{:S(2)}) %all-to-all-start.1) | async-done | bytes 1179680 | tf_op jit(solution)/shard_map/all_to_all | solution.py:26
  141.4 0.5 slice.23
  142.5 0.2 convert_reduce_fusion
  142.7 0.1 fusion.19
  142.9 4.2 %collective-permute-start.5 = (f16[16,1280]{1,0:T(8,128)(2,1)S(1)}, f16[16,1280]{1,0:T(8,128)(2,1)S(1)}, u32[]{:S(2)}, u32[]{:S(2)}) collective-permute-start(f16[16,1280]{1,0:T(8,128)(2,1)S(1)} %fusion.21), channel_id=1, source_target_pairs={{0,512},{512,0},{1,513},{513,1},{2,514},{514,2},{3,515},{515,3},{4... | collective-permute-start | bytes 122888 | tf_op jit(solution)/shard_map/ppermute | solution.py:36
  147.1 0.7 add_add_fusion
  147.8 5.3 %collective-permute-done.5 = f16[16,1280]{1,0:T(8,128)(2,1)S(1)} collective-permute-done((f16[16,1280]{1,0:T(8,128)(2,1)S(1)}, f16[16,1280]{1,0:T(8,128)(2,1)S(1)}, u32[]{:S(2)}, u32[]{:S(2)}) %collective-permute-start.5) | collective-permute-done | bytes 40992 | tf_op jit(solution)/shard_map/ppermute | solution.py:36
  153.2 0.1 fusion.16
  153.3 0.6 fusion.27
  153.9 0.7 add_add_fusion.1
  (37 shorter events, 0.4 us)
Async XLA Ops:
  1.5 0.5 copy-start.8
  4.0 16.9 %copy-start.1 = (bf16[16,1152]{1,0:T(8,128)(2,1)S(1)}, bf16[16,1152]{1,0:T(8,128)(2,1)}, u32[]{:S(2)}) copy-start(bf16[16,1152]{1,0:T(8,128)(2,1)} %param.5) | copy-start | bytes 110596
  4.0 63.5 %copy-start.5 = (s32[16384]{0:T(1024)S(1)}, s32[16384]{0:T(1024)}, u32[]{:S(2)}) copy-start(s32[16384]{0:T(1024)} %param.7) | copy-start | bytes 196612
  4.0 65.3 %all-to-all-start = ((bf16[32,16,1152]{2,1,0:T(8,128)(2,1)}), bf16[32,16,1152]{2,1,0:T(8,128)(2,1)S(1)}, u32[]{:S(2)}, u32[]{:S(2)}) async-start(bf16[32,16,1152]{2,1,0:T(8,128)(2,1)} %broadcast_in_dim.8), calls=%async_computation | async-start | bytes 2359296 | tf_op jit(solution)/shard_map/all_to_all | solution.py:21
  21.1 47.8 %copy-start.6 = (f32[16]{0:T(128)}, f32[16]{0:T(128)S(1)}, u32[]{:S(2)}) copy-start(f32[16]{0:T(128)S(1)} %fusion.14) | copy-start | bytes 196
  64.3 4.9 %collective-permute-start = (bf16[256,1152]{1,0:T(8,128)(2,1)S(1)}, bf16[256,1152]{1,0:T(8,128)(2,1)S(1)}, u32[]{:S(2)}, u32[]{:S(2)}) collective-permute-start(bf16[256,1152]{1,0:T(8,128)(2,1)S(1)} %all_gather.7), channel_id=1, source_target_pairs={{0,16},{16,0},{1,17},{17,1},{2,18},{18,2},{3,19},{19,3},{4,20},{20... | collective-permute-start | bytes 1769480 | tf_op jit(solution)/shard_map/ppermute | solution.py:54
  69.3 1.6 %copy-start.3 = (bf16[512,1152]{1,0:T(8,128)(2,1)}, bf16[512,1152]{1,0:T(8,128)(2,1)S(1)}, u32[]{:S(2)}) copy-start(bf16[512,1152]{1,0:T(8,128)(2,1)S(1)} %constant_dynamic-update-slice_fusion) | copy-start | bytes 3538948
  70.9 1.0 copy-start.10
  72.9 4.3 %collective-permute-start.1 = (f16[256,1280]{1,0:T(8,128)(2,1)}, f16[256,1280]{1,0:T(8,128)(2,1)S(1)}, u32[]{:S(2)}, u32[]{:S(2)}) collective-permute-start(f16[256,1280]{1,0:T(8,128)(2,1)} %fusion.4), channel_id=1, source_target_pairs={{0,16},{16,0},{1,17},{17,1},{2,18},{18,2},{3,19},{19,3},{4,20},{20... | collective-permute-start | bytes 1966088 | tf_op jit(solution)/shard_map/ppermute | solution.py:91
  77.4 4.0 %copy-start.4 = (bf16[512,1152]{1,0:T(8,128)(2,1)S(1)}, bf16[512,1152]{1,0:T(8,128)(2,1)}, u32[]{:S(2)}) copy-start(bf16[512,1152]{1,0:T(8,128)(2,1)} %copy-done.3) | copy-start | bytes 3538948
  77.4 4.0 %copy-start.11 = (f32[512,512]{0,1:T(8,128)S(1)}, f32[512,512]{0,1:T(8,128)}, u32[]{:S(2)}) copy-start(f32[512,512]{0,1:T(8,128)} %copy-done.10) | copy-start | bytes 3145732
  77.6 31.7 %collective-permute-start.2 = (f16[2,2,2,16,1280]{4,3,2,0,1:T(8,128)(2,1)S(1)}, f16[2,2,2,16,1280]{4,3,2,0,1:T(8,128)(2,1)S(1)}, u32[]{:S(2)}, u32[]{:S(2)}) collective-permute-start(f16[2,2,2,16,1280]{4,3,2,0,1:T(8,128)(2,1)S(1)} %fusion.11), channel_id=1, source_target_pairs={{0,2},{2,0},{1,3},{3,1},{4,6},{6,4},{5,7},{7,5},{8,10},{10,8},{9,1... | collective-permute-start | bytes 983048 | tf_op jit(solution)/shard_map/ppermute | solution.py:36
  83.5 57.9 %all-to-all-start.1 = ((f16[32,16,1152]{2,1,0:T(8,128)(2,1)}), f16[32,16,1152]{2,1,0:T(8,128)(2,1)S(1)}, u32[]{:S(2)}, u32[]{:S(2)}) async-start(f16[32,16,1152]{2,1,0:T(8,128)(2,1)} %bitcast.12), calls=%async_computation.1 | async-start | bytes 2359296 | tf_op jit(solution)/shard_map/all_to_all | solution.py:26
  109.4 11.7 %collective-permute-start.3 = (f16[2,2,16,1280]{3,2,1,0:T(8,128)(2,1)S(1)}, f16[2,2,16,1280]{3,2,1,0:T(8,128)(2,1)S(1)}, u32[]{:S(2)}, u32[]{:S(2)}) collective-permute-start(f16[2,2,16,1280]{3,2,1,0:T(8,128)(2,1)S(1)} %fusion.12), channel_id=1, source_target_pairs={{0,4},{4,0},{1,5},{5,1},{2,6},{6,2},{3,7},{7,3},{8,12},{12,8},{9,1... | collective-permute-start | bytes 491528 | tf_op jit(solution)/shard_map/ppermute | solution.py:36
  111.6 31.1 %copy-start = (bf16[16,1152]{1,0:T(8,128)(2,1)S(1)}, bf16[16,1152]{1,0:T(8,128)(2,1)}, u32[]{:S(2)}) copy-start(bf16[16,1152]{1,0:T(8,128)(2,1)} %param.6) | copy-start | bytes 110596
  121.1 21.7 %copy-start.9 = (f32[16]{0:T(128)S(1)}, f32[16]{0:T(128)}, u32[]{:S(2)}) copy-start(f32[16]{0:T(128)} %copy-done.8) | copy-start | bytes 196
  121.1 32.0 %copy-start.2 = (bf16[16,1152]{1,0:T(8,128)(2,1)S(1)}, bf16[16,1152]{1,0:T(8,128)(2,1)}, u32[]{:S(2)}) copy-start(bf16[16,1152]{1,0:T(8,128)(2,1)} %param.5) | copy-start | bytes 110596
  121.2 11.0 %collective-permute-start.4 = (f16[2,16,1280]{2,1,0:T(8,128)(2,1)S(1)}, f16[2,16,1280]{2,1,0:T(8,128)(2,1)S(1)}, u32[]{:S(2)}, u32[]{:S(2)}) collective-permute-start(f16[2,16,1280]{2,1,0:T(8,128)(2,1)S(1)} %fusion.13), channel_id=1, source_target_pairs={{0,8},{8,0},{1,9},{9,1},{2,10},{10,2},{3,11},{11,3},{4,12},{12,4},... | collective-permute-start | bytes 245768 | tf_op jit(solution)/shard_map/ppermute | solution.py:36
  125.5 28.5 %copy-start.7 = (f32[16]{0:T(128)S(1)}, f32[16]{0:T(128)}, u32[]{:S(2)}) copy-start(f32[16]{0:T(128)} %copy-done.6) | copy-start | bytes 196
  142.9 10.2 %collective-permute-start.5 = (f16[16,1280]{1,0:T(8,128)(2,1)S(1)}, f16[16,1280]{1,0:T(8,128)(2,1)S(1)}, u32[]{:S(2)}, u32[]{:S(2)}) collective-permute-start(f16[16,1280]{1,0:T(8,128)(2,1)S(1)} %fusion.21), channel_id=1, source_target_pairs={{0,512},{512,0},{1,513},{513,1},{2,514},{514,2},{3,515},{515,3},{4... | collective-permute-start | bytes 122888 | tf_op jit(solution)/shard_map/ppermute | solution.py:36

commit v3 on v2

v3 whole, which is shorter than its diff:
```python
import jax
import jax.numpy as jnp
from jax import lax
from jax.sharding import Mesh, PartitionSpec as P

FINE = ("y2", "y1", "x", "core", "z", "y0")
FINE_SIZES = (2, 2, 8, 2, 8, 2)
IMAGE_GROUP = ("core", "z", "y2")
TEXT_GROUP = ("y1", "x", "y0")
SEND_SCALE = 2.0
LOSS_SCALE = 0.125


def normalize(raw):
    values = raw.astype(jnp.float32)
    return values * lax.rsqrt(jnp.sum(values * values, axis=1, keepdims=True) + 1e-06)


def shift_by(block, axis, step):
    count = lax.axis_size(axis)
    return lax.ppermute(block, axis, [(i, (i + step) % count) for i in range(count)])


def from_own(array, axis):
    return lax.dynamic_slice_in_dim(
        jnp.concatenate([array, array]), lax.axis_index(axis), array.shape[0], 0
    )


def gather(block, axes):
    copies = jnp.broadcast_to(block[None], (lax.axis_size(axes),) + block.shape)
    return lax.all_to_all(copies, axes, 0, 0, tiled=True)


def scatter(parts, axes):
    count = lax.axis_size(axes)
    return lax.all_to_all(
        parts.reshape(count, parts.shape[0] // count, parts.shape[1]), axes, 0, 0, tiled=True
    )


def half(total):
    return total.astype(jnp.float16)


def full(total):
    return total.astype(jnp.float32)


def per_device(
    picture_vectors,
    caption_vectors,
    caption_partner_position,
    sharpness_factor,
    affine_offset_array,
):
    own_rows, width = picture_vectors.shape
    similarity_multiplier = sharpness_factor[0]
    shift = affine_offset_array[0]
    own_images = normalize(picture_vectors).astype(jnp.bfloat16)
    txt_block = gather(normalize(caption_vectors).astype(jnp.bfloat16), TEXT_GROUP).reshape(-1, width)
    own_images = jnp.concatenate([own_images, shift_by(own_images, "y2", 1)])
    z_images = from_own(lax.all_gather(own_images, "z", axis=0, tiled=False), "z")
    z_images = z_images.reshape(-1, width)
    img_block = jnp.concatenate([z_images, shift_by(z_images, "core", 1)])
    image_count = img_block.shape[0]

    def of_group(array, group):
        rows = array.reshape(FINE_SIZES + (own_rows,))
        for place, axis in enumerate(FINE):
            if axis not in group:
                rows = lax.dynamic_slice_in_dim(rows, lax.axis_index(axis), 1, place)
        order = [FINE.index(axis) for axis in group]
        order = order + [i for i in range(len(FINE) + 1) if i not in order]
        return rows.transpose(order).reshape([lax.axis_size(axis) for axis in group] + [own_rows])

    ids = jnp.arange(caption_partner_position.shape[0], dtype=jnp.int32)
    text_ids = of_group(ids, TEXT_GROUP).reshape(-1)
    my_pairs = of_group(caption_partner_position, IMAGE_GROUP)
    for place, axis in enumerate(IMAGE_GROUP):
        my_pairs = jnp.moveaxis(from_own(jnp.moveaxis(my_pairs, place, 0), axis), 0, place)
    my_pairs = my_pairs.reshape(-1)
    logits = (
        similarity_multiplier
        * lax.dot_general(
            img_block, txt_block, (((1,), (1,)), ((), ())), preferred_element_type=jnp.float32
        )
        + shift
    )
    positive = (my_pairs[:, None] == text_ids[None, :]).astype(jnp.float32)
    sign = 2.0 * positive - 1.0
    loss = jnp.sum(jax.nn.softplus(-sign * logits), axis=1)
    slope = (jax.nn.sigmoid(logits) - positive).astype(jnp.bfloat16)
    txt_part = lax.dot_general(
        slope, img_block, (((0,), (0,)), ((), ())), preferred_element_type=jnp.float32
    )
    txt_terms = scatter(half(SEND_SCALE * txt_part), TEXT_GROUP)
    img_part = SEND_SCALE * jnp.dot(slope, txt_block, preferred_element_type=jnp.float32)
    img_part = jnp.concatenate(
        [img_part, jnp.broadcast_to(loss[:, None] * LOSS_SCALE, (image_count, 128))], axis=1
    ).reshape(2, 8, 2 * own_rows, width + 128)
    total = img_part[0] + full(shift_by(half(img_part[1]), "core", 1))
    far = shift_by(half(total[4]), "z", 4)
    ahead = full(shift_by(half(jnp.stack([total[1], total[3]])), "z", 1))
    back = full(shift_by(half(jnp.stack([total[7], total[5]])), "z", -1))
    near = total[0] + ahead[0] + back[0]
    near = near + full(shift_by(half(total[2] + ahead[1]), "z", 2))
    near = near + full(shift_by(half(total[6] + back[1]), "z", -2))
    near = near + full(far)
    tie = jnp.minimum(jnp.abs(txt_terms[0, 0, 0]), 0)
    total = near[:own_rows] + full(shift_by(half(near[own_rows:]) + tie, "y2", 1))
    loss = total[:, width] / LOSS_SCALE
    img_dir = (similarity_multiplier / SEND_SCALE) * total[:, :width]
    txt_dir = (similarity_multiplier / SEND_SCALE) * jnp.sum(full(txt_terms), axis=0)
    unused, image_back = jax.vjp(normalize, picture_vectors.astype(jnp.float32))
    unused2, text_backward = jax.vjp(normalize, caption_vectors.astype(jnp.float32))
    return (image_back(img_dir)[0], text_backward(txt_dir)[0], loss)


def solution(mesh):
    fine = Mesh(mesh.devices.reshape(FINE_SIZES), FINE)
    in_specs = (P(FINE, None), P(FINE, None), P(), P(), P())
    out_specs = (P(FINE, None), P(FINE, None), P(FINE))
    return jax.shard_map(
        per_device, mesh=fine, in_specs=in_specs, out_specs=out_specs, check_vma=False
    )
```

time: 155 us -> 148 us (0.955)
  blocking collectives: 43.1 us -> 25.8 us
  starting transfers between devices: 61.5 us -> 70.6 us
    all_gather x2 -> x1, blocking collectives: 43.1 us -> 25.8 us  [per_device(): lax.all_gather(own_images, 'z', axis=0, tiled=False)]
    ppermute x6 -> x9, starting transfers between devices: 18.8 us -> 29.4 us  [shift_by(): lax.ppermute(block, axis, [(i, (i + step) % count) for i in range(count)])]
    all_to_all x1, waiting for transfers between devices: 9.16 us -> 7.58 us  [scatter(): lax.all_to_all(parts.reshape(count, parts.shape[0] // count, parts.shape[...]
    ppermute x6 -> x9, waiting for transfers between devices: 23.3 us -> 24.9 us  [shift_by(): lax.ppermute(block, axis, [(i, (i + step) % count) for i in range(count)])]
  transfers between devices with their start and end apart: 8 -> 11, of which waited for: 5 -> 6; matrix products, arithmetic and copies ran while one was open for 3% -> 4% of each run, Pallas kernels for 0% -> 0%
where the time goes in v3:
time: 148 us; the launch traced here: 147 us
  starting transfers between devices  70.6 us (48%)
  waiting for transfers between devices  32.5 us (22%)
  blocking collectives  25.8 us (17%)
  other arithmetic  7.62 us (5%)
  matrix products  4.63 us (3%)
  between operations  3.04 us (2%)
  local copies, waits for them, and re-layouts  2.77 us (2%)
    ppermute x9, starting transfers between devices, shift_by(): lax.ppermute(block, axis, [(i, (i + step) % count) for i in range(count)])  29.4 us
    all_gather x1, blocking collectives, per_device(): lax.all_gather(own_images, 'z', axis=0, tiled=False)  25.8 us
    ppermute x9, waiting for transfers between devices, shift_by(): lax.ppermute(block, axis, [(i, (i + step) % count) for i in range(count)])  24.9 us
    all_to_all x1, starting transfers between devices, scatter(): lax.all_to_all(parts.reshape(count, parts.shape[0] // count, parts.shape[...  24.3 us
    all_to_all x1, starting transfers between devices, gather(): return lax.all_to_all(copies, axes, 0, 0, tiled=True)  16.9 us
    all_to_all x1, waiting for transfers between devices, scatter(): lax.all_to_all(parts.reshape(count, parts.shape[0] // count, parts.shape[...  7.58 us
  transfers between devices with their start and end apart: 11, of which 6 were waited for; matrix products, arithmetic and copies ran while one was open for 4% of the time, Pallas kernels for 0%

profile of v3, /device:TPU:2, one launch (start us, length us, event | category | flops | bytes accessed | tf_op | source)
XLA Modules:
  0.0 147.0 jit_solution(18277348878687186961)
XLA Ops:
  0.6 0.9 fusion.22
  1.5 0.9 fusion.23
  2.4 1.1 broadcast_in_dim.8
  3.5 16.9 %all-to-all-start = ((bf16[32,16,1152]{2,1,0:T(8,128)(2,1)}), bf16[32,16,1152]{2,1,0:T(8,128)(2,1)S(1)}, u32[]{:S(2)}, u32[]{:S(2)}) async-start(bf16[32,16,1152]{2,1,0:T(8,128)(2,1)} %broadcast_in_dim.8), calls=%async_computation | async-start | bytes 2359296 | tf_op jit(solution)/shard_map/all_to_all | solution.py:32
  20.4 0.1 fusion.19
  20.6 0.1 fusion.20
  20.6 1.9 %collective-permute-start = (bf16[16,1152]{1,0:T(8,128)(2,1)S(1)}, bf16[16,1152]{1,0:T(8,128)(2,1)S(1)}, u32[]{:S(2)}, u32[]{:S(2)}) collective-permute-start(bf16[16,1152]{1,0:T(8,128)(2,1)S(1)} %fusion.20), channel_id=1, source_target_pairs={{0,512},{512,0},{1,513},{513,1},{2,514},{514,2},{3,515},{515,3},{4... | collective-permute-start | bytes 110600 | tf_op jit(solution)/shard_map/ppermute | solution.py:21
  22.6 0.7 reshape.111
  23.3 16.1 %collective-permute-done = bf16[16,1152]{1,0:T(8,128)(2,1)S(1)} collective-permute-done((bf16[16,1152]{1,0:T(8,128)(2,1)S(1)}, bf16[16,1152]{1,0:T(8,128)(2,1)S(1)}, u32[]{:S(2)}, u32[]{:S(2)}) %collective-permute-start) | collective-permute-done | bytes 36896 | tf_op jit(solution)/shard_map/ppermute | solution.py:21
  39.4 25.8 %all-gather = bf16[256,1152]{1,0:T(8,128)(2,1)S(1)} all-gather(bf16[32,1152]{1,0:T(8,128)(2,1)S(1)} %pad_maximum_fusion.6), channel_id=2, replica_groups=mesh['y2'=2,'y1'=2,'x'=8,'core'=2,'z'=8,'y0'=2] {'z'}, dimensions={0}, use_global_device_ids=true | all-gather | bytes 663552 | tf_op jit(solution)/shard_map/all_gather | solution.py:63
  65.2 0.2 fusion.10
  65.4 1.9 %collective-permute-start.1 = (bf16[256,1152]{1,0:T(8,128)(2,1)S(1)}, bf16[256,1152]{1,0:T(8,128)(2,1)S(1)}, u32[]{:S(2)}, u32[]{:S(2)}) collective-permute-start(bf16[256,1152]{1,0:T(8,128)(2,1)S(1)} %bitcast.43), channel_id=1, source_target_pairs={{0,16},{16,0},{1,17},{17,1},{2,18},{18,2},{3,19},{19,3},{4,20},{20... | collective-permute-start | bytes 1769480 | tf_op jit(solution)/shard_map/ppermute | solution.py:21
  68.8 0.1 eq.17
  68.9 0.2 iota_multiply_fusion
  69.2 0.1 eq.19
  69.3 0.1 collective-permute-done.1
  69.3 0.0 all-to-all-done
  69.3 1.6 %fusion.9 = (f32[512]{0:T(512)S(1)}, f32[512,512]{0,1:T(8,128)S(1)}) fusion(s32[512]{0:T(512)S(1)} %eq.17, s32[512]{0:T(512)S(1)} %eq.19, f32[]{:T(128)} %bitcast.36, bf16[512,1152]{1,0:T(8,128)(2,1)S(1)} %bitcast.39, bf16[256,1152]{1,0:T(8,128)(2,1)S(1)} %collective-permute-done.1, bf16[256,1152]{1,0:T(8,128)(2,1)S(1)} %bitcast.44, f32[]{:T(128)} %bitcast.35), kind=kOutput, calls=%fused_computation.23 | convolution fusion | flops 610008576 | bytes 3414024 | tf_op jit(solution)/shard_map/dot_general | solution.py:85
  70.9 1.0 convolution_multiply_fusion.1
  71.9 0.1 broadcast_in_dim.9
  72.1 0.2 fusion.3
  72.2 2.5 %collective-permute-start.2 = (f16[8,32,1280]{2,1,0:T(8,128)(2,1)S(1)}, f16[8,32,1280]{2,1,0:T(8,128)(2,1)}, u32[]{:S(2)}, u32[]{:S(2)}) collective-permute-start(f16[8,32,1280]{2,1,0:T(8,128)(2,1)S(1)} %bitcast.42), channel_id=1, source_target_pairs={{0,16},{16,0},{1,17},{17,1},{2,18},{18,2},{3,19},{19,3},{4,20},{20... | collective-permute-start | bytes 1966088 | tf_op jit(solution)/shard_map/ppermute | solution.py:21
  74.8 2.1 %fusion = f16[512,1152]{1,0:T(8,128)(2,1)} fusion(bf16[256,1152]{1,0:T(8,128)(2,1)S(1)} %copy-done.7, bf16[256,1152]{1,0:T(8,128)(2,1)S(1)} %bitcast.45, f32[512,512]{0,1:T(8,128)S(1)} %get-tuple-element.15, s32[512]{0:T(512)S(1)} %eq.17, s32[512]{0:T(512)S(1)} %eq.19), kind=kOutput, calls=%fused_computation.3 | convolution fusion | flops 609353728 | bytes 3411968 | tf_op jit(solution)/shard_map/dot_general | solution.py:94
  76.8 24.3 %all-to-all-start.1 = ((f16[32,16,1152]{2,1,0:T(8,128)(2,1)}), f16[32,16,1152]{2,1,0:T(8,128)(2,1)S(1)}, u32[]{:S(2)}, u32[]{:S(2)}) async-start(f16[32,16,1152]{2,1,0:T(8,128)(2,1)} %bitcast.41), calls=%async_computation.1 | async-start | bytes 2359296 | tf_op jit(solution)/shard_map/all_to_all | solution.py:37
  101.1 0.0 collective-permute-done.2
  101.2 1.3 fusion.42
  102.4 0.1 slice_bitcast_fusion
  102.6 3.8 %collective-permute-start.3 = (f16[2,32,1280]{2,1,0:T(8,128)(2,1)S(1)}, f16[2,32,1280]{2,1,0:T(8,128)(2,1)S(1)}, u32[]{:S(2)}, u32[]{:S(2)}) collective-permute-start(f16[2,32,1280]{2,1,0:T(8,128)(2,1)S(1)} %pad_maximum_fusion.4), channel_id=1, source_target_pairs={{0,2},{2,4},{4,6},{6,8},{8,10},{10,12},{12,14},{14,0},{1,3},{3,5},... | collective-permute-start | bytes 491528 | tf_op jit(solution)/shard_map/ppermute | solution.py:21
  106.4 3.2 %collective-permute-start.4 = (f16[2,32,1280]{2,1,0:T(8,128)(2,1)S(1)}, f16[2,32,1280]{2,1,0:T(8,128)(2,1)S(1)}, u32[]{:S(2)}, u32[]{:S(2)}) collective-permute-start(f16[2,32,1280]{2,1,0:T(8,128)(2,1)S(1)} %pad_maximum_fusion.5), channel_id=1, source_target_pairs={{0,14},{2,0},{4,2},{6,4},{8,6},{10,8},{12,10},{14,12},{1,15},{3,1}... | collective-permute-start | bytes 491528 | tf_op jit(solution)/shard_map/ppermute | solution.py:21
  109.7 4.0 %collective-permute-start.7 = (f16[32,1280]{1,0:T(8,128)(2,1)S(1)}, f16[32,1280]{1,0:T(8,128)(2,1)S(1)}, u32[]{:S(2)}, u32[]{:S(2)}) collective-permute-start(f16[32,1280]{1,0:T(8,128)(2,1)S(1)} %get-tuple-element.9), channel_id=1, source_target_pairs={{0,8},{2,10},{4,12},{6,14},{8,0},{10,2},{12,4},{14,6},{1,9},{3,11}... | collective-permute-start | bytes 245768 | tf_op jit(solution)/shard_map/ppermute | solution.py:21
  113.7 0.0 collective-permute-done.3
  113.8 0.0 collective-permute-done.4
  113.9 0.0 copy-start.2
  113.9 3.5 %collective-permute-start.5 = (f16[32,1280]{1,0:T(8,128)(2,1)S(1)}, f16[32,1280]{1,0:T(8,128)(2,1)S(1)}, u32[]{:S(2)}, u32[]{:S(2)}) collective-permute-start(f16[32,1280]{1,0:T(8,128)(2,1)S(1)} %get-tuple-element.7), channel_id=1, source_target_pairs={{0,4},{2,6},{4,8},{6,10},{8,12},{10,14},{12,0},{14,2},{1,5},{3,7},... | collective-permute-start | bytes 245768 | tf_op jit(solution)/shard_map/ppermute | solution.py:21
  117.4 4.5 %collective-permute-start.6 = (f16[32,1280]{1,0:T(8,128)(2,1)S(1)}, f16[32,1280]{1,0:T(8,128)(2,1)S(1)}, u32[]{:S(2)}, u32[]{:S(2)}) collective-permute-start(f16[32,1280]{1,0:T(8,128)(2,1)S(1)} %get-tuple-element.8), channel_id=1, source_target_pairs={{0,12},{2,14},{4,0},{6,2},{8,4},{10,6},{12,8},{14,10},{1,13},{3,15... | collective-permute-start | bytes 245768 | tf_op jit(solution)/shard_map/ppermute | solution.py:21
  121.9 0.0 collective-permute-done.7
  121.9 1.4 collective-permute-done.5
  123.3 1.4 collective-permute-done.6
  124.6 1.0 fusion.16
  125.6 7.6 %all-to-all-done.1 = f16[32,16,1152]{2,1,0:T(8,128)(2,1)S(1)} async-done(((f16[32,16,1152]{2,1,0:T(8,128)(2,1)}), f16[32,16,1152]{2,1,0:T(8,128)(2,1)S(1)}, u32[]{:S(2)}, u32[]{:S(2)}) %all-to-all-start.1) | async-done | bytes 1179680 | tf_op jit(solution)/shard_map/all_to_all | solution.py:37
  133.2 0.5 slice.101
  134.4 4.1 %collective-permute-start.8 = (f16[16,1280]{1,0:T(8,128)(2,1)S(1)}, f16[16,1280]{1,0:T(8,128)(2,1)S(1)}, u32[]{:S(2)}, u32[]{:S(2)}) collective-permute-start(f16[16,1280]{1,0:T(8,128)(2,1)S(1)} %fusion.25), channel_id=1, source_target_pairs={{0,512},{512,0},{1,513},{513,1},{2,514},{514,2},{3,515},{515,3},{4... | collective-permute-start | bytes 122888 | tf_op jit(solution)/shard_map/ppermute | solution.py:21
  138.5 0.2 convert_reduce_fusion
  138.7 6.0 %collective-permute-done.8 = f16[16,1280]{1,0:T(8,128)(2,1)S(1)} collective-permute-done((f16[16,1280]{1,0:T(8,128)(2,1)S(1)}, f16[16,1280]{1,0:T(8,128)(2,1)S(1)}, u32[]{:S(2)}, u32[]{:S(2)}) %collective-permute-start.8) | collective-permute-done | bytes 40992 | tf_op jit(solution)/shard_map/ppermute | solution.py:21
  144.7 0.6 fusion.37
  145.3 0.1 fusion.21
  145.4 0.8 add_add_fusion.1
  146.3 0.7 add_add_fusion
  (34 shorter events, 0.4 us)
Async XLA Ops:
  3.5 16.9 %copy-start.1 = (bf16[16,1152]{1,0:T(8,128)(2,1)S(1)}, bf16[16,1152]{1,0:T(8,128)(2,1)}, u32[]{:S(2)}) copy-start(bf16[16,1152]{1,0:T(8,128)(2,1)} %param.5) | copy-start | bytes 110596
  3.5 19.1 %copy-start.5 = (s32[16384]{0:T(1024)S(1)}, s32[16384]{0:T(1024)}, u32[]{:S(2)}) copy-start(s32[16384]{0:T(1024)} %param.7) | copy-start | bytes 196612
  3.5 65.9 %all-to-all-start = ((bf16[32,16,1152]{2,1,0:T(8,128)(2,1)}), bf16[32,16,1152]{2,1,0:T(8,128)(2,1)S(1)}, u32[]{:S(2)}, u32[]{:S(2)}) async-start(bf16[32,16,1152]{2,1,0:T(8,128)(2,1)} %broadcast_in_dim.8), calls=%async_computation | async-start | bytes 2359296 | tf_op jit(solution)/shard_map/all_to_all | solution.py:32
  20.6 18.8 %collective-permute-start = (bf16[16,1152]{1,0:T(8,128)(2,1)S(1)}, bf16[16,1152]{1,0:T(8,128)(2,1)S(1)}, u32[]{:S(2)}, u32[]{:S(2)}) collective-permute-start(bf16[16,1152]{1,0:T(8,128)(2,1)S(1)} %fusion.20), channel_id=1, source_target_pairs={{0,512},{512,0},{1,513},{513,1},{2,514},{514,2},{3,515},{515,3},{4... | collective-permute-start | bytes 110600 | tf_op jit(solution)/shard_map/ppermute | solution.py:21
  65.4 5.5 %copy-start.3 = (bf16[8,32,1152]{2,1,0:T(8,128)(2,1)}, bf16[8,32,1152]{2,1,0:T(8,128)(2,1)S(1)}, u32[]{:S(2)}) copy-start(bf16[8,32,1152]{2,1,0:T(8,128)(2,1)S(1)} %fusion.10) | copy-start | bytes 1769476
  65.4 3.9 %collective-permute-start.1 = (bf16[256,1152]{1,0:T(8,128)(2,1)S(1)}, bf16[256,1152]{1,0:T(8,128)(2,1)S(1)}, u32[]{:S(2)}, u32[]{:S(2)}) collective-permute-start(bf16[256,1152]{1,0:T(8,128)(2,1)S(1)} %bitcast.43), channel_id=1, source_target_pairs={{0,16},{16,0},{1,17},{17,1},{2,18},{18,2},{3,19},{19,3},{4,20},{20... | collective-permute-start | bytes 1769480 | tf_op jit(solution)/shard_map/ppermute | solution.py:21
  69.3 1.6 %copy-start.6 = (bf16[256,1152]{1,0:T(8,128)(2,1)}, bf16[256,1152]{1,0:T(8,128)(2,1)S(1)}, u32[]{:S(2)}) copy-start(bf16[256,1152]{1,0:T(8,128)(2,1)S(1)} %collective-permute-done.1) | copy-start | bytes 1769476
  72.1 2.7 %copy-start.4 = (bf16[8,32,1152]{2,1,0:T(8,128)(2,1)S(1)}, bf16[8,32,1152]{2,1,0:T(8,128)(2,1)}, u32[]{:S(2)}) copy-start(bf16[8,32,1152]{2,1,0:T(8,128)(2,1)} %copy-done.3) | copy-start | bytes 1769476
  72.1 2.7 %copy-start.7 = (bf16[256,1152]{1,0:T(8,128)(2,1)S(1)}, bf16[256,1152]{1,0:T(8,128)(2,1)}, u32[]{:S(2)}) copy-start(bf16[256,1152]{1,0:T(8,128)(2,1)} %copy-done.6) | copy-start | bytes 1769476
  72.2 28.9 %collective-permute-start.2 = (f16[8,32,1280]{2,1,0:T(8,128)(2,1)S(1)}, f16[8,32,1280]{2,1,0:T(8,128)(2,1)}, u32[]{:S(2)}, u32[]{:S(2)}) collective-permute-start(f16[8,32,1280]{2,1,0:T(8,128)(2,1)S(1)} %bitcast.42), channel_id=1, source_target_pairs={{0,16},{16,0},{1,17},{17,1},{2,18},{18,2},{3,19},{19,3},{4,20},{20... | collective-permute-start | bytes 1966088 | tf_op jit(solution)/shard_map/ppermute | solution.py:21
  76.8 56.4 %all-to-all-start.1 = ((f16[32,16,1152]{2,1,0:T(8,128)(2,1)}), f16[32,16,1152]{2,1,0:T(8,128)(2,1)S(1)}, u32[]{:S(2)}, u32[]{:S(2)}) async-start(f16[32,16,1152]{2,1,0:T(8,128)(2,1)} %bitcast.41), calls=%async_computation.1 | async-start | bytes 2359296 | tf_op jit(solution)/shard_map/all_to_all | solution.py:37
  102.4 11.4 %copy-start = (f32[8,32,1280]{2,1,0:T(8,128)}, f32[8,32,1280]{2,1,0:T(8,128)S(1)}, u32[]{:S(2)}) copy-start(f32[8,32,1280]{2,1,0:T(8,128)S(1)} %get-tuple-element.4) | copy-start | bytes 3932164
  102.6 11.2 %collective-permute-start.3 = (f16[2,32,1280]{2,1,0:T(8,128)(2,1)S(1)}, f16[2,32,1280]{2,1,0:T(8,128)(2,1)S(1)}, u32[]{:S(2)}, u32[]{:S(2)}) collective-permute-start(f16[2,32,1280]{2,1,0:T(8,128)(2,1)S(1)} %pad_maximum_fusion.4), channel_id=1, source_target_pairs={{0,2},{2,4},{4,6},{6,8},{8,10},{10,12},{12,14},{14,0},{1,3},{3,5},... | collective-permute-start | bytes 491528 | tf_op jit(solution)/shard_map/ppermute | solution.py:21
  106.4 7.3 %collective-permute-start.4 = (f16[2,32,1280]{2,1,0:T(8,128)(2,1)S(1)}, f16[2,32,1280]{2,1,0:T(8,128)(2,1)S(1)}, u32[]{:S(2)}, u32[]{:S(2)}) collective-permute-start(f16[2,32,1280]{2,1,0:T(8,128)(2,1)S(1)} %pad_maximum_fusion.5), channel_id=1, source_target_pairs={{0,14},{2,0},{4,2},{6,4},{8,6},{10,8},{12,10},{14,12},{1,15},{3,1}... | collective-permute-start | bytes 491528 | tf_op jit(solution)/shard_map/ppermute | solution.py:21
  109.7 12.2 %collective-permute-start.7 = (f16[32,1280]{1,0:T(8,128)(2,1)S(1)}, f16[32,1280]{1,0:T(8,128)(2,1)S(1)}, u32[]{:S(2)}, u32[]{:S(2)}) collective-permute-start(f16[32,1280]{1,0:T(8,128)(2,1)S(1)} %get-tuple-element.9), channel_id=1, source_target_pairs={{0,8},{2,10},{4,12},{6,14},{8,0},{10,2},{12,4},{14,6},{1,9},{3,11}... | collective-permute-start | bytes 245768 | tf_op jit(solution)/shard_map/ppermute | solution.py:21
  113.9 31.6 %copy-start.2 = (bf16[16,1152]{1,0:T(8,128)(2,1)S(1)}, bf16[16,1152]{1,0:T(8,128)(2,1)}, u32[]{:S(2)}) copy-start(bf16[16,1152]{1,0:T(8,128)(2,1)} %param.6) | copy-start | bytes 110596
  113.9 9.4 %collective-permute-start.5 = (f16[32,1280]{1,0:T(8,128)(2,1)S(1)}, f16[32,1280]{1,0:T(8,128)(2,1)S(1)}, u32[]{:S(2)}, u32[]{:S(2)}) collective-permute-start(f16[32,1280]{1,0:T(8,128)(2,1)S(1)} %get-tuple-element.7), channel_id=1, source_target_pairs={{0,4},{2,6},{4,8},{6,10},{8,12},{10,14},{12,0},{14,2},{1,5},{3,7},... | collective-permute-start | bytes 245768 | tf_op jit(solution)/shard_map/ppermute | solution.py:21
  117.4 7.3 %collective-permute-start.6 = (f16[32,1280]{1,0:T(8,128)(2,1)S(1)}, f16[32,1280]{1,0:T(8,128)(2,1)S(1)}, u32[]{:S(2)}, u32[]{:S(2)}) collective-permute-start(f16[32,1280]{1,0:T(8,128)(2,1)S(1)} %get-tuple-element.8), channel_id=1, source_target_pairs={{0,12},{2,14},{4,0},{6,2},{8,4},{10,6},{12,8},{14,10},{1,13},{3,15... | collective-permute-start | bytes 245768 | tf_op jit(solution)/shard_map/ppermute | solution.py:21
  134.4 10.2 %collective-permute-start.8 = (f16[16,1280]{1,0:T(8,128)(2,1)S(1)}, f16[16,1280]{1,0:T(8,128)(2,1)S(1)}, u32[]{:S(2)}, u32[]{:S(2)}) collective-permute-start(f16[16,1280]{1,0:T(8,128)(2,1)S(1)} %fusion.25), channel_id=1, source_target_pairs={{0,512},{512,0},{1,513},{513,1},{2,514},{514,2},{3,515},{515,3},{4... | collective-permute-start | bytes 122888 | tf_op jit(solution)/shard_map/ppermute | solution.py:21

commit v4 on v3

--- a/solution.py
+++ b/solution.py
@@ -3,10 +3,10 @@
 from jax import lax
 from jax.sharding import Mesh, PartitionSpec as P
 
-FINE = ("y2", "y1", "x", "core", "z", "y0")
-FINE_SIZES = (2, 2, 8, 2, 8, 2)
-IMAGE_GROUP = ("core", "z", "y2")
-TEXT_GROUP = ("y1", "x", "y0")
+FINE = ("yhi", "x", "core", "z", "ylo")
+FINE_SIZES = (4, 8, 2, 8, 2)
+IMAGE_GROUP = ("core", "z", "ylo")
+TEXT_GROUP = ("yhi", "x")
 SEND_SCALE = 2.0
 LOSS_SCALE = 0.125
 
@@ -58,8 +58,10 @@
     similarity_multiplier = sharpness_factor[0]
     shift = affine_offset_array[0]
     own_images = normalize(picture_vectors).astype(jnp.bfloat16)
-    txt_block = gather(normalize(caption_vectors).astype(jnp.bfloat16), TEXT_GROUP).reshape(-1, width)
-    own_images = jnp.concatenate([own_images, shift_by(own_images, "y2", 1)])
+    neighbour_images = shift_by(own_images, "ylo", 1)
+    own_images = jnp.concatenate([own_images, neighbour_images])
+    own_texts = normalize(caption_vectors).astype(jnp.bfloat16)
+    txt_block = gather(own_texts, TEXT_GROUP).reshape(-1, width)
     z_images = from_own(lax.all_gather(own_images, "z", axis=0, tiled=False), "z")
     z_images = z_images.reshape(-1, width)
     img_block = jnp.concatenate([z_images, shift_by(z_images, "core", 1)])
@@ -107,8 +109,7 @@
     near = near + full(shift_by(half(total[2] + ahead[1]), "z", 2))
     near = near + full(shift_by(half(total[6] + back[1]), "z", -2))
     near = near + full(far)
-    tie = jnp.minimum(jnp.abs(txt_terms[0, 0, 0]), 0)
-    total = near[:own_rows] + full(shift_by(half(near[own_rows:]) + tie, "y2", 1))
+    total = near[:own_rows] + full(shift_by(half(near[own_rows:]), "ylo", 1))
     loss = total[:, width] / LOSS_SCALE
     img_dir = (similarity_multiplier / SEND_SCALE) * total[:, :width]
     txt_dir = (similarity_multiplier / SEND_SCALE) * jnp.sum(full(txt_terms), axis=0)

time: 148 us -> 142 us (0.959)
  the two profiles are of different devices: /device:TPU:2 before, /device:TPU:18 now
where the time goes in v4:
time: 142 us; the launch traced here: 141 us
  starting transfers between devices  58.2 us (41%)
  blocking collectives  35.8 us (25%)
  waiting for transfers between devices  31.2 us (22%)
  other arithmetic  6.46 us (5%)
  matrix products  4.63 us (3%)
  between operations  2.32 us (2%)
  local copies, waits for them, and re-layouts  2.22 us (2%)
    all_gather x1, blocking collectives, per_device(): lax.all_gather(own_images, 'z', axis=0, tiled=False)  35.8 us
    ppermute x9, starting transfers between devices, shift_by(): lax.ppermute(block, axis, [(i, (i + step) % count) for i in range(count)])  32 us
    ppermute x9, waiting for transfers between devices, shift_by(): lax.ppermute(block, axis, [(i, (i + step) % count) for i in range(count)])  28.4 us
    all_to_all x1, starting transfers between devices, scatter(): lax.all_to_all(parts.reshape(count, parts.shape[0] // count, parts.shape[...  13.8 us
    all_to_all x1, starting transfers between devices, gather(): return lax.all_to_all(copies, axes, 0, 0, tiled=True)  12.4 us
  transfers between devices with their start and end apart: 11, of which 7 were waited for; matrix products, arithmetic and copies ran while one was open for 4% of the time, Pallas kernels for 0%

profile of v4, /device:TPU:18, one launch (start us, length us, event | category | flops | bytes accessed | tf_op | source)
XLA Modules:
  0.0 140.9 jit_solution(3251992895304908582)
XLA Ops:
  0.6 0.9 fusion.22
  1.5 0.9 fusion.23
  2.4 1.1 broadcast_in_dim.8
  3.5 12.4 %all-to-all-start = ((bf16[32,16,1152]{2,1,0:T(8,128)(2,1)}), bf16[32,16,1152]{2,1,0:T(8,128)(2,1)S(1)}, u32[]{:S(2)}, u32[]{:S(2)}) async-start(bf16[32,16,1152]{2,1,0:T(8,128)(2,1)} %broadcast_in_dim.8), calls=%async_computation | async-start | bytes 2359296 | tf_op jit(solution)/shard_map/all_to_all | solution.py:32
  15.9 0.0 copy-start.4
  15.9 0.1 fusion.19
  16.0 0.1 fusion.20
  16.1 6.8 %collective-permute-start = (bf16[16,1152]{1,0:T(8,128)(2,1)S(1)}, bf16[16,1152]{1,0:T(8,128)(2,1)S(1)}, u32[]{:S(2)}, u32[]{:S(2)}) collective-permute-start(bf16[16,1152]{1,0:T(8,128)(2,1)S(1)} %fusion.20), channel_id=1, source_target_pairs={{0,1},{1,0},{2,3},{3,2},{4,5},{5,4},{6,7},{7,6},{8,9},{9,8},{10,11... | collective-permute-start | bytes 110600 | tf_op jit(solution)/shard_map/ppermute | solution.py:21
  22.9 20.5 %collective-permute-done = bf16[16,1152]{1,0:T(8,128)(2,1)S(1)} collective-permute-done((bf16[16,1152]{1,0:T(8,128)(2,1)S(1)}, bf16[16,1152]{1,0:T(8,128)(2,1)S(1)}, u32[]{:S(2)}, u32[]{:S(2)}) %collective-permute-start) | collective-permute-done | bytes 36896 | tf_op jit(solution)/shard_map/ppermute | solution.py:21
  43.3 35.8 %all-gather = bf16[256,1152]{1,0:T(8,128)(2,1)S(1)} all-gather(bf16[32,1152]{1,0:T(8,128)(2,1)S(1)} %pad_maximum_fusion.6), channel_id=2, replica_groups=mesh['yhi'=4,'x'=8,'core'=2,'z'=8,'ylo'=2] {'z'}, dimensions={0}, use_global_device_ids=true | all-gather | bytes 663552 | tf_op jit(solution)/shard_map/all_gather | solution.py:65
  79.2 0.2 fusion.10
  79.4 1.9 %collective-permute-start.1 = (bf16[256,1152]{1,0:T(8,128)(2,1)S(1)}, bf16[256,1152]{1,0:T(8,128)(2,1)S(1)}, u32[]{:S(2)}, u32[]{:S(2)}) collective-permute-start(bf16[256,1152]{1,0:T(8,128)(2,1)S(1)} %bitcast.41), channel_id=1, source_target_pairs={{0,16},{16,0},{1,17},{17,1},{2,18},{18,2},{3,19},{19,3},{4,20},{20... | collective-permute-start | bytes 1769480 | tf_op jit(solution)/shard_map/ppermute | solution.py:21
  82.7 0.1 fusion.32
  82.7 0.1 eq.19
  82.8 0.7 reshape.99
  83.7 0.1 eq.17
  83.8 0.0 collective-permute-done.1
  83.8 0.0 all-to-all-done
  83.8 1.6 %fusion.9 = (f32[512]{0:T(512)S(1)}, f32[512,512]{0,1:T(8,128)S(1)}) fusion(s32[512]{0:T(512)S(1)} %eq.17, s32[512]{0:T(512)S(1)} %eq.19, f32[]{:T(128)} %bitcast.34, bf16[512,1152]{1,0:T(8,128)(2,1)S(1)} %bitcast.37, bf16[256,1152]{1,0:T(8,128)(2,1)S(1)} %collective-permute-done.1, bf16[256,1152]{1,0:T(8,128)(2,1)S(1)} %bitcast.42, f32[]{:T(128)} %bitcast.33), kind=kOutput, calls=%fused_computation.23 | convolution fusion | flops 610008576 | bytes 3414024 | tf_op jit(solution)/shard_map/dot_general | solution.py:87
  85.4 1.0 convolution_multiply_fusion.1
  86.4 0.1 broadcast_in_dim.9
  86.5 0.2 fusion.3
  86.7 2.5 %collective-permute-start.2 = (f16[8,32,1280]{2,1,0:T(8,128)(2,1)S(1)}, f16[8,32,1280]{2,1,0:T(8,128)(2,1)}, u32[]{:S(2)}, u32[]{:S(2)}) collective-permute-start(f16[8,32,1280]{2,1,0:T(8,128)(2,1)S(1)} %bitcast.40), channel_id=1, source_target_pairs={{0,16},{16,0},{1,17},{17,1},{2,18},{18,2},{3,19},{19,3},{4,20},{20... | collective-permute-start | bytes 1966088 | tf_op jit(solution)/shard_map/ppermute | solution.py:21
  89.3 2.1 %fusion = f16[512,1152]{1,0:T(8,128)(2,1)} fusion(bf16[256,1152]{1,0:T(8,128)(2,1)S(1)} %copy-done.6, bf16[256,1152]{1,0:T(8,128)(2,1)S(1)} %bitcast.43, f32[512,512]{0,1:T(8,128)S(1)} %get-tuple-element.15, s32[512]{0:T(512)S(1)} %eq.17, s32[512]{0:T(512)S(1)} %eq.19), kind=kOutput, calls=%fused_computation.3 | convolution fusion | flops 609353728 | bytes 3411968 | tf_op jit(solution)/shard_map/dot_general | solution.py:96
  91.3 13.8 %all-to-all-start.1 = ((f16[32,16,1152]{2,1,0:T(8,128)(2,1)}), f16[32,16,1152]{2,1,0:T(8,128)(2,1)S(1)}, u32[]{:S(2)}, u32[]{:S(2)}) async-start(f16[32,16,1152]{2,1,0:T(8,128)(2,1)} %bitcast.39), calls=%async_computation.1 | async-start | bytes 2359296 | tf_op jit(solution)/shard_map/all_to_all | solution.py:37
  105.1 0.0 collective-permute-done.2
  105.1 1.3 fusion.41
  106.4 0.1 slice_bitcast_fusion
  106.5 4.2 %collective-permute-start.3 = (f16[2,32,1280]{2,1,0:T(8,128)(2,1)S(1)}, f16[2,32,1280]{2,1,0:T(8,128)(2,1)S(1)}, u32[]{:S(2)}, u32[]{:S(2)}) collective-permute-start(f16[2,32,1280]{2,1,0:T(8,128)(2,1)S(1)} %pad_maximum_fusion.4), channel_id=1, source_target_pairs={{0,2},{2,4},{4,6},{6,8},{8,10},{10,12},{12,14},{14,0},{1,3},{3,5},... | collective-permute-start | bytes 491528 | tf_op jit(solution)/shard_map/ppermute | solution.py:21
  110.8 3.1 %collective-permute-start.4 = (f16[2,32,1280]{2,1,0:T(8,128)(2,1)S(1)}, f16[2,32,1280]{2,1,0:T(8,128)(2,1)S(1)}, u32[]{:S(2)}, u32[]{:S(2)}) collective-permute-start(f16[2,32,1280]{2,1,0:T(8,128)(2,1)S(1)} %pad_maximum_fusion.5), channel_id=1, source_target_pairs={{0,14},{2,0},{4,2},{6,4},{8,6},{10,8},{12,10},{14,12},{1,15},{3,1}... | collective-permute-start | bytes 491528 | tf_op jit(solution)/shard_map/ppermute | solution.py:21
  113.9 3.6 %collective-permute-start.7 = (f16[32,1280]{1,0:T(8,128)(2,1)S(1)}, f16[32,1280]{1,0:T(8,128)(2,1)S(1)}, u32[]{:S(2)}, u32[]{:S(2)}) collective-permute-start(f16[32,1280]{1,0:T(8,128)(2,1)S(1)} %get-tuple-element.9), channel_id=1, source_target_pairs={{0,8},{2,10},{4,12},{6,14},{8,0},{10,2},{12,4},{14,6},{1,9},{3,11}... | collective-permute-start | bytes 245768 | tf_op jit(solution)/shard_map/ppermute | solution.py:21
  117.6 0.0 collective-permute-done.3
  117.6 0.4 collective-permute-done.4
  118.1 0.0 copy-start.3
  118.1 3.6 %collective-permute-start.5 = (f16[32,1280]{1,0:T(8,128)(2,1)S(1)}, f16[32,1280]{1,0:T(8,128)(2,1)S(1)}, u32[]{:S(2)}, u32[]{:S(2)}) collective-permute-start(f16[32,1280]{1,0:T(8,128)(2,1)S(1)} %get-tuple-element.7), channel_id=1, source_target_pairs={{0,4},{2,6},{4,8},{6,10},{8,12},{10,14},{12,0},{14,2},{1,5},{3,7},... | collective-permute-start | bytes 245768 | tf_op jit(solution)/shard_map/ppermute | solution.py:21
  121.7 4.3 %collective-permute-start.6 = (f16[32,1280]{1,0:T(8,128)(2,1)S(1)}, f16[32,1280]{1,0:T(8,128)(2,1)S(1)}, u32[]{:S(2)}, u32[]{:S(2)}) collective-permute-start(f16[32,1280]{1,0:T(8,128)(2,1)S(1)} %get-tuple-element.8), channel_id=1, source_target_pairs={{0,12},{2,14},{4,0},{6,2},{8,4},{10,6},{12,8},{14,10},{1,13},{3,15... | collective-permute-start | bytes 245768 | tf_op jit(solution)/shard_map/ppermute | solution.py:21
  126.0 1.5 %collective-permute-done.7 = f16[32,1280]{1,0:T(8,128)(2,1)S(1)} collective-permute-done((f16[32,1280]{1,0:T(8,128)(2,1)S(1)}, f16[32,1280]{1,0:T(8,128)(2,1)S(1)}, u32[]{:S(2)}, u32[]{:S(2)}) %collective-permute-start.7) | collective-permute-done | bytes 81952 | tf_op jit(solution)/shard_map/ppermute | solution.py:21
  127.5 0.4 collective-permute-done.5
  127.9 1.1 collective-permute-done.6
  129.0 0.1 fusion.16
  129.1 1.9 %collective-permute-start.8 = (f16[16,1280]{1,0:T(8,128)(2,1)S(1)}, f16[16,1280]{1,0:T(8,128)(2,1)S(1)}, u32[]{:S(2)}, u32[]{:S(2)}) collective-permute-start(f16[16,1280]{1,0:T(8,128)(2,1)S(1)} %slice_convert_fusion), channel_id=1, source_target_pairs={{0,1},{1,0},{2,3},{3,2},{4,5},{5,4},{6,7},{7,6},{8,9},{9,8},{10,11... | collective-permute-start | bytes 122888 | tf_op jit(solution)/shard_map/ppermute | solution.py:21
  131.0 4.6 %collective-permute-done.8 = f16[16,1280]{1,0:T(8,128)(2,1)S(1)} collective-permute-done((f16[16,1280]{1,0:T(8,128)(2,1)S(1)}, f16[16,1280]{1,0:T(8,128)(2,1)S(1)}, u32[]{:S(2)}, u32[]{:S(2)}) %collective-permute-start.8) | collective-permute-done | bytes 40992 | tf_op jit(solution)/shard_map/ppermute | solution.py:21
  135.7 0.6 fusion.36
  136.3 2.8 %all-to-all-done.1 = f16[32,16,1152]{2,1,0:T(8,128)(2,1)S(1)} async-done(((f16[32,16,1152]{2,1,0:T(8,128)(2,1)}), f16[32,16,1152]{2,1,0:T(8,128)(2,1)S(1)}, u32[]{:S(2)}, u32[]{:S(2)}) %all-to-all-start.1) | async-done | bytes 1179680 | tf_op jit(solution)/shard_map/all_to_all | solution.py:37
  139.1 0.2 convert_reduce_fusion
  139.3 0.1 fusion.21
  139.4 0.7 add_add_fusion.1
  140.2 0.7 add_add_fusion
  (29 shorter events, 0.4 us)
Async XLA Ops:
  3.5 12.4 %copy-start.2 = (bf16[16,1152]{1,0:T(8,128)(2,1)S(1)}, bf16[16,1152]{1,0:T(8,128)(2,1)}, u32[]{:S(2)}) copy-start(bf16[16,1152]{1,0:T(8,128)(2,1)} %param.5) | copy-start | bytes 110596
  3.5 80.3 %all-to-all-start = ((bf16[32,16,1152]{2,1,0:T(8,128)(2,1)}), bf16[32,16,1152]{2,1,0:T(8,128)(2,1)S(1)}, u32[]{:S(2)}, u32[]{:S(2)}) async-start(bf16[32,16,1152]{2,1,0:T(8,128)(2,1)} %broadcast_in_dim.8), calls=%async_computation | async-start | bytes 2359296 | tf_op jit(solution)/shard_map/all_to_all | solution.py:32
  15.9 66.9 %copy-start.4 = (s32[16384]{0:T(1024)S(1)}, s32[16384]{0:T(1024)}, u32[]{:S(2)}) copy-start(s32[16384]{0:T(1024)} %param.7) | copy-start | bytes 196612
  16.1 27.2 %collective-permute-start = (bf16[16,1152]{1,0:T(8,128)(2,1)S(1)}, bf16[16,1152]{1,0:T(8,128)(2,1)S(1)}, u32[]{:S(2)}, u32[]{:S(2)}) collective-permute-start(bf16[16,1152]{1,0:T(8,128)(2,1)S(1)} %fusion.20), channel_id=1, source_target_pairs={{0,1},{1,0},{2,3},{3,2},{4,5},{5,4},{6,7},{7,6},{8,9},{9,8},{10,11... | collective-permute-start | bytes 110600 | tf_op jit(solution)/shard_map/ppermute | solution.py:21
  79.4 6.0 %copy-start = (bf16[8,32,1152]{2,1,0:T(8,128)(2,1)}, bf16[8,32,1152]{2,1,0:T(8,128)(2,1)S(1)}, u32[]{:S(2)}) copy-start(bf16[8,32,1152]{2,1,0:T(8,128)(2,1)S(1)} %fusion.10) | copy-start | bytes 1769476
  79.4 4.4 %collective-permute-start.1 = (bf16[256,1152]{1,0:T(8,128)(2,1)S(1)}, bf16[256,1152]{1,0:T(8,128)(2,1)S(1)}, u32[]{:S(2)}, u32[]{:S(2)}) collective-permute-start(bf16[256,1152]{1,0:T(8,128)(2,1)S(1)} %bitcast.41), channel_id=1, source_target_pairs={{0,16},{16,0},{1,17},{17,1},{2,18},{18,2},{3,19},{19,3},{4,20},{20... | collective-permute-start | bytes 1769480 | tf_op jit(solution)/shard_map/ppermute | solution.py:21
  83.8 1.6 %copy-start.5 = (bf16[256,1152]{1,0:T(8,128)(2,1)}, bf16[256,1152]{1,0:T(8,128)(2,1)S(1)}, u32[]{:S(2)}) copy-start(bf16[256,1152]{1,0:T(8,128)(2,1)S(1)} %collective-permute-done.1) | copy-start | bytes 1769476
  86.5 2.7 %copy-start.1 = (bf16[8,32,1152]{2,1,0:T(8,128)(2,1)S(1)}, bf16[8,32,1152]{2,1,0:T(8,128)(2,1)}, u32[]{:S(2)}) copy-start(bf16[8,32,1152]{2,1,0:T(8,128)(2,1)} %copy-done) | copy-start | bytes 1769476
  86.5 2.7 %copy-start.6 = (bf16[256,1152]{1,0:T(8,128)(2,1)S(1)}, bf16[256,1152]{1,0:T(8,128)(2,1)}, u32[]{:S(2)}) copy-start(bf16[256,1152]{1,0:T(8,128)(2,1)} %copy-done.5) | copy-start | bytes 1769476
  86.7 18.4 %collective-permute-start.2 = (f16[8,32,1280]{2,1,0:T(8,128)(2,1)S(1)}, f16[8,32,1280]{2,1,0:T(8,128)(2,1)}, u32[]{:S(2)}, u32[]{:S(2)}) collective-permute-start(f16[8,32,1280]{2,1,0:T(8,128)(2,1)S(1)} %bitcast.40), channel_id=1, source_target_pairs={{0,16},{16,0},{1,17},{17,1},{2,18},{18,2},{3,19},{19,3},{4,20},{20... | collective-permute-start | bytes 1966088 | tf_op jit(solution)/shard_map/ppermute | solution.py:21
  91.3 47.8 %all-to-all-start.1 = ((f16[32,16,1152]{2,1,0:T(8,128)(2,1)}), f16[32,16,1152]{2,1,0:T(8,128)(2,1)S(1)}, u32[]{:S(2)}, u32[]{:S(2)}) async-start(f16[32,16,1152]{2,1,0:T(8,128)(2,1)} %bitcast.39), calls=%async_computation.1 | async-start | bytes 2359296 | tf_op jit(solution)/shard_map/all_to_all | solution.py:37
  106.5 11.0 %collective-permute-start.3 = (f16[2,32,1280]{2,1,0:T(8,128)(2,1)S(1)}, f16[2,32,1280]{2,1,0:T(8,128)(2,1)S(1)}, u32[]{:S(2)}, u32[]{:S(2)}) collective-permute-start(f16[2,32,1280]{2,1,0:T(8,128)(2,1)S(1)} %pad_maximum_fusion.4), channel_id=1, source_target_pairs={{0,2},{2,4},{4,6},{6,8},{8,10},{10,12},{12,14},{14,0},{1,3},{3,5},... | collective-permute-start | bytes 491528 | tf_op jit(solution)/shard_map/ppermute | solution.py:21
  110.8 7.2 %collective-permute-start.4 = (f16[2,32,1280]{2,1,0:T(8,128)(2,1)S(1)}, f16[2,32,1280]{2,1,0:T(8,128)(2,1)S(1)}, u32[]{:S(2)}, u32[]{:S(2)}) collective-permute-start(f16[2,32,1280]{2,1,0:T(8,128)(2,1)S(1)} %pad_maximum_fusion.5), channel_id=1, source_target_pairs={{0,14},{2,0},{4,2},{6,4},{8,6},{10,8},{12,10},{14,12},{1,15},{3,1}... | collective-permute-start | bytes 491528 | tf_op jit(solution)/shard_map/ppermute | solution.py:21
  113.9 13.6 %collective-permute-start.7 = (f16[32,1280]{1,0:T(8,128)(2,1)S(1)}, f16[32,1280]{1,0:T(8,128)(2,1)S(1)}, u32[]{:S(2)}, u32[]{:S(2)}) collective-permute-start(f16[32,1280]{1,0:T(8,128)(2,1)S(1)} %get-tuple-element.9), channel_id=1, source_target_pairs={{0,8},{2,10},{4,12},{6,14},{8,0},{10,2},{12,4},{14,6},{1,9},{3,11}... | collective-permute-start | bytes 245768 | tf_op jit(solution)/shard_map/ppermute | solution.py:21
  118.1 21.2 %copy-start.3 = (bf16[16,1152]{1,0:T(8,128)(2,1)S(1)}, bf16[16,1152]{1,0:T(8,128)(2,1)}, u32[]{:S(2)}) copy-start(bf16[16,1152]{1,0:T(8,128)(2,1)} %param.6) | copy-start | bytes 110596
  118.1 9.8 %collective-permute-start.5 = (f16[32,1280]{1,0:T(8,128)(2,1)S(1)}, f16[32,1280]{1,0:T(8,128)(2,1)S(1)}, u32[]{:S(2)}, u32[]{:S(2)}) collective-permute-start(f16[32,1280]{1,0:T(8,128)(2,1)S(1)} %get-tuple-element.7), channel_id=1, source_target_pairs={{0,4},{2,6},{4,8},{6,10},{8,12},{10,14},{12,0},{14,2},{1,5},{3,7},... | collective-permute-start | bytes 245768 | tf_op jit(solution)/shard_map/ppermute | solution.py:21
  121.7 7.3 %collective-permute-start.6 = (f16[32,1280]{1,0:T(8,128)(2,1)S(1)}, f16[32,1280]{1,0:T(8,128)(2,1)S(1)}, u32[]{:S(2)}, u32[]{:S(2)}) collective-permute-start(f16[32,1280]{1,0:T(8,128)(2,1)S(1)} %get-tuple-element.8), channel_id=1, source_target_pairs={{0,12},{2,14},{4,0},{6,2},{8,4},{10,6},{12,8},{14,10},{1,13},{3,15... | collective-permute-start | bytes 245768 | tf_op jit(solution)/shard_map/ppermute | solution.py:21
  129.1 6.6 %collective-permute-start.8 = (f16[16,1280]{1,0:T(8,128)(2,1)S(1)}, f16[16,1280]{1,0:T(8,128)(2,1)S(1)}, u32[]{:S(2)}, u32[]{:S(2)}) collective-permute-start(f16[16,1280]{1,0:T(8,128)(2,1)S(1)} %slice_convert_fusion), channel_id=1, source_target_pairs={{0,1},{1,0},{2,3},{3,2},{4,5},{5,4},{6,7},{7,6},{8,9},{9,8},{10,11... | collective-permute-start | bytes 122888 | tf_op jit(solution)/shard_map/ppermute | solution.py:21

commit v5 on v4

--- a/solution.py
+++ b/solution.py
@@ -57,10 +57,10 @@
     own_rows, width = picture_vectors.shape
     similarity_multiplier = sharpness_factor[0]
     shift = affine_offset_array[0]
-    own_images = normalize(picture_vectors).astype(jnp.bfloat16)
-    neighbour_images = shift_by(own_images, "ylo", 1)
-    own_images = jnp.concatenate([own_images, neighbour_images])
-    own_texts = normalize(caption_vectors).astype(jnp.bfloat16)
+    near_images = jnp.concatenate([picture_vectors, shift_by(picture_vectors, "ylo", 1)])
+    own_images = normalize(near_images).astype(jnp.bfloat16)
+    tie = jnp.minimum(jnp.abs(near_images[own_rows, 0]), 0)
+    own_texts = normalize(caption_vectors).astype(jnp.bfloat16) + tie
     txt_block = gather(own_texts, TEXT_GROUP).reshape(-1, width)
     z_images = from_own(lax.all_gather(own_images, "z", axis=0, tiled=False), "z")
     z_images = z_images.reshape(-1, width)

time: 142 us -> 122 us (0.86)
  the two profiles are of different devices: /device:TPU:18 before, /device:TPU:2 now
where the time goes in v5:
time: 122 us; the launch traced here: 121 us
  starting transfers between devices  58.7 us (48%)
  blocking collectives  34.4 us (28%)
  waiting for transfers between devices  11.4 us (9%)
  other arithmetic  6.49 us (5%)
  matrix products  4.62 us (4%)
  between operations  2.99 us (2%)
  local copies, waits for them, and re-layouts  2.72 us (2%)
    all_gather x1, blocking collectives, per_device(): lax.all_gather(own_images, 'z', axis=0, tiled=False)  34.4 us
    ppermute x9, starting transfers between devices, shift_by(): lax.ppermute(block, axis, [(i, (i + step) % count) for i in range(count)])  29.6 us
    all_to_all x1, starting transfers between devices, gather(): return lax.all_to_all(copies, axes, 0, 0, tiled=True)  16.9 us
    all_to_all x1, starting transfers between devices, scatter(): lax.all_to_all(parts.reshape(count, parts.shape[0] // count, parts.shape[...  12.2 us
    ppermute x9, waiting for transfers between devices, shift_by(): lax.ppermute(block, axis, [(i, (i + step) % count) for i in range(count)])  8.1 us
    all_to_all x1, waiting for transfers between devices, scatter(): lax.all_to_all(parts.reshape(count, parts.shape[0] // count, parts.shape[...  3.33 us
  transfers between devices with their start and end apart: 11, of which 7 were waited for; matrix products, arithmetic and copies ran while one was open for 6% of the time, Pallas kernels for 0%

profile of v5, /device:TPU:2, one launch (start us, length us, event | category | flops | bytes accessed | tf_op | source)
XLA Modules:
  0.0 121.4 jit_solution(6561222744534472322)
XLA Ops:
  0.6 3.6 %collective-permute-start = (bf16[16,1152]{1,0:T(8,128)(2,1)}, bf16[16,1152]{1,0:T(8,128)(2,1)S(1)}, u32[]{:S(2)}, u32[]{:S(2)}) collective-permute-start(bf16[16,1152]{1,0:T(8,128)(2,1)} %param.5), channel_id=1, source_target_pairs={{0,1},{1,0},{2,3},{3,2},{4,5},{5,4},{6,7},{7,6},{8,9},{9,8},{10,11... | collective-permute-start | bytes 110600 | tf_op jit(solution)/shard_map/ppermute | solution.py:21
  4.2 0.9 fusion.21
  5.1 1.6 %collective-permute-done = bf16[16,1152]{1,0:T(8,128)(2,1)S(1)} collective-permute-done((bf16[16,1152]{1,0:T(8,128)(2,1)}, bf16[16,1152]{1,0:T(8,128)(2,1)S(1)}, u32[]{:S(2)}, u32[]{:S(2)}) %collective-permute-start) | collective-permute-done | bytes 36896 | tf_op jit(solution)/shard_map/ppermute | solution.py:21
  6.7 0.5 slice.85
  7.9 0.8 fusion.24
  8.7 1.1 broadcast_in_dim.8
  9.8 16.9 %all-to-all-start = ((bf16[32,16,1152]{2,1,0:T(8,128)(2,1)}), bf16[32,16,1152]{2,1,0:T(8,128)(2,1)S(1)}, u32[]{:S(2)}, u32[]{:S(2)}) async-start(bf16[32,16,1152]{2,1,0:T(8,128)(2,1)} %broadcast_in_dim.8), calls=%async_computation | async-start | bytes 2359296 | tf_op jit(solution)/shard_map/all_to_all | solution.py:32
  26.7 0.0 copy-start.4
  26.8 0.1 multiply_reduce_fusion
  26.9 0.1 multiply_convert_fusion
  27.0 34.4 %all_gather.4 = bf16[8,32,1152]{2,1,0:T(8,128)(2,1)S(1)} all-gather(bf16[1,32,1152]{2,1,0:T(8,128)(2,1)S(1)} %multiply_convert_fusion), channel_id=1, replica_groups=mesh['yhi'=4,'x'=8,'core'=2,'z'=8,'ylo'=2] {'z'}, dimensions={0}, use_global_device_ids=true | all-gather | bytes 663552 | tf_op jit(solution)/shard_map/all_gather | solution.py:65
  61.4 0.2 fusion.10
  61.7 1.9 %collective-permute-start.1 = (bf16[256,1152]{1,0:T(8,128)(2,1)S(1)}, bf16[256,1152]{1,0:T(8,128)(2,1)S(1)}, u32[]{:S(2)}, u32[]{:S(2)}) collective-permute-start(bf16[256,1152]{1,0:T(8,128)(2,1)S(1)} %bitcast.42), channel_id=1, source_target_pairs={{0,16},{16,0},{1,17},{17,1},{2,18},{18,2},{3,19},{19,3},{4,20},{20... | collective-permute-start | bytes 1769480 | tf_op jit(solution)/shard_map/ppermute | solution.py:21
  64.9 0.1 fusion.32
  65.0 0.1 eq.19
  65.1 0.7 reshape.162
  65.9 0.1 eq.17
  66.0 0.0 collective-permute-done.1
  66.0 0.0 all-to-all-done
  66.0 1.6 %fusion.9 = (f32[512]{0:T(512)S(1)}, f32[512,512]{0,1:T(8,128)S(1)}) fusion(s32[512]{0:T(512)S(1)} %eq.17, s32[512]{0:T(512)S(1)} %eq.19, f32[]{:T(128)} %bitcast.36, bf16[512,1152]{1,0:T(8,128)(2,1)S(1)} %bitcast.38, bf16[256,1152]{1,0:T(8,128)(2,1)S(1)} %collective-permute-done.1, bf16[256,1152]{1,0:T(8,128)(2,1)S(1)} %bitcast.43, f32[]{:T(128)} %bitcast.35), kind=kOutput, calls=%fused_computation.23 | convolution fusion | flops 610008576 | bytes 3414024 | tf_op jit(solution)/shard_map/dot_general | solution.py:87
  67.6 1.0 convolution_multiply_fusion.1
  68.6 0.1 broadcast_in_dim.9
  68.8 0.2 fusion.3
  68.9 2.5 %collective-permute-start.2 = (f16[8,32,1280]{2,1,0:T(8,128)(2,1)S(1)}, f16[8,32,1280]{2,1,0:T(8,128)(2,1)}, u32[]{:S(2)}, u32[]{:S(2)}) collective-permute-start(f16[8,32,1280]{2,1,0:T(8,128)(2,1)S(1)} %bitcast.41), channel_id=1, source_target_pairs={{0,16},{16,0},{1,17},{17,1},{2,18},{18,2},{3,19},{19,3},{4,20},{20... | collective-permute-start | bytes 1966088 | tf_op jit(solution)/shard_map/ppermute | solution.py:21
  71.5 2.1 %fusion = f16[512,1152]{1,0:T(8,128)(2,1)} fusion(bf16[256,1152]{1,0:T(8,128)(2,1)S(1)} %copy-done.6, bf16[256,1152]{1,0:T(8,128)(2,1)S(1)} %bitcast.44, f32[512,512]{0,1:T(8,128)S(1)} %get-tuple-element.19, s32[512]{0:T(512)S(1)} %eq.17, s32[512]{0:T(512)S(1)} %eq.19), kind=kOutput, calls=%fused_computation.3 | convolution fusion | flops 609353728 | bytes 3411968 | tf_op jit(solution)/shard_map/dot_general | solution.py:96
  73.6 12.2 %all-to-all-start.1 = ((f16[32,16,1152]{2,1,0:T(8,128)(2,1)}), f16[32,16,1152]{2,1,0:T(8,128)(2,1)S(1)}, u32[]{:S(2)}, u32[]{:S(2)}) async-start(f16[32,16,1152]{2,1,0:T(8,128)(2,1)} %bitcast.40), calls=%async_computation.1 | async-start | bytes 2359296 | tf_op jit(solution)/shard_map/all_to_all | solution.py:37
  85.8 0.0 collective-permute-done.2
  85.8 1.3 %fusion.41 = (f16[8,32,1280]{2,1,0:T(8,128)(2,1)S(1)}, f32[8,32,1280]{2,1,0:T(8,128)S(1)}) fusion(f32[8,32,1280]{2,1,0:T(8,128)S(1)} %bitcast.37, f16[8,32,1280]{2,1,0:T(8,128)(2,1)} %collective-permute-done.2), kind=kLoop, calls=%fused_computation.94 | loop fusion | flops 983040 | bytes 3932160 | tf_op jit(solution)/shard_map/convert.9
  87.0 0.1 slice_bitcast_fusion
  87.2 3.8 %collective-permute-start.3 = (f16[2,32,1280]{2,1,0:T(8,128)(2,1)S(1)}, f16[2,32,1280]{2,1,0:T(8,128)(2,1)S(1)}, u32[]{:S(2)}, u32[]{:S(2)}) collective-permute-start(f16[2,32,1280]{2,1,0:T(8,128)(2,1)S(1)} %pad_maximum_fusion.4), channel_id=1, source_target_pairs={{0,2},{2,4},{4,6},{6,8},{8,10},{10,12},{12,14},{14,0},{1,3},{3,5},... | collective-permute-start | bytes 491528 | tf_op jit(solution)/shard_map/ppermute | solution.py:21
  91.0 3.2 %collective-permute-start.4 = (f16[2,32,1280]{2,1,0:T(8,128)(2,1)S(1)}, f16[2,32,1280]{2,1,0:T(8,128)(2,1)S(1)}, u32[]{:S(2)}, u32[]{:S(2)}) collective-permute-start(f16[2,32,1280]{2,1,0:T(8,128)(2,1)S(1)} %pad_maximum_fusion.5), channel_id=1, source_target_pairs={{0,14},{2,0},{4,2},{6,4},{8,6},{10,8},{12,10},{14,12},{1,15},{3,1}... | collective-permute-start | bytes 491528 | tf_op jit(solution)/shard_map/ppermute | solution.py:21
  94.3 3.8 %collective-permute-start.7 = (f16[32,1280]{1,0:T(8,128)(2,1)S(1)}, f16[32,1280]{1,0:T(8,128)(2,1)S(1)}, u32[]{:S(2)}, u32[]{:S(2)}) collective-permute-start(f16[32,1280]{1,0:T(8,128)(2,1)S(1)} %get-tuple-element.11), channel_id=1, source_target_pairs={{0,8},{2,10},{4,12},{6,14},{8,0},{10,2},{12,4},{14,6},{1,9},{3,11}... | collective-permute-start | bytes 245768 | tf_op jit(solution)/shard_map/ppermute | solution.py:21
  98.2 0.1 collective-permute-done.4
  98.3 0.0 copy-start.2
  98.3 3.6 %collective-permute-start.5 = (f16[32,1280]{1,0:T(8,128)(2,1)S(1)}, f16[32,1280]{1,0:T(8,128)(2,1)S(1)}, u32[]{:S(2)}, u32[]{:S(2)}) collective-permute-start(f16[32,1280]{1,0:T(8,128)(2,1)S(1)} %get-tuple-element.9), channel_id=1, source_target_pairs={{0,4},{2,6},{4,8},{6,10},{8,12},{10,14},{12,0},{14,2},{1,5},{3,7},... | collective-permute-start | bytes 245768 | tf_op jit(solution)/shard_map/ppermute | solution.py:21
  102.0 4.3 %collective-permute-start.6 = (f16[32,1280]{1,0:T(8,128)(2,1)S(1)}, f16[32,1280]{1,0:T(8,128)(2,1)S(1)}, u32[]{:S(2)}, u32[]{:S(2)}) collective-permute-start(f16[32,1280]{1,0:T(8,128)(2,1)S(1)} %get-tuple-element.10), channel_id=1, source_target_pairs={{0,12},{2,14},{4,0},{6,2},{8,4},{10,6},{12,8},{14,10},{1,13},{3,15... | collective-permute-start | bytes 245768 | tf_op jit(solution)/shard_map/ppermute | solution.py:21
  106.3 1.1 collective-permute-done.7
  107.5 0.5 collective-permute-done.5
  108.0 1.2 %collective-permute-done.6 = f16[32,1280]{1,0:T(8,128)(2,1)S(1)} collective-permute-done((f16[32,1280]{1,0:T(8,128)(2,1)S(1)}, f16[32,1280]{1,0:T(8,128)(2,1)S(1)}, u32[]{:S(2)}, u32[]{:S(2)}) %collective-permute-start.6) | collective-permute-done | bytes 81952 | tf_op jit(solution)/shard_map/ppermute | solution.py:21
  109.2 0.1 fusion.16
  109.3 2.7 %collective-permute-start.8 = (f16[16,1280]{1,0:T(8,128)(2,1)S(1)}, f16[16,1280]{1,0:T(8,128)(2,1)S(1)}, u32[]{:S(2)}, u32[]{:S(2)}) collective-permute-start(f16[16,1280]{1,0:T(8,128)(2,1)S(1)} %slice_convert_fusion), channel_id=1, source_target_pairs={{0,1},{1,0},{2,3},{3,2},{4,5},{5,4},{6,7},{7,6},{8,9},{9,8},{10,11... | collective-permute-start | bytes 122888 | tf_op jit(solution)/shard_map/ppermute | solution.py:21
  112.0 3.5 %collective-permute-done.8 = f16[16,1280]{1,0:T(8,128)(2,1)S(1)} collective-permute-done((f16[16,1280]{1,0:T(8,128)(2,1)S(1)}, f16[16,1280]{1,0:T(8,128)(2,1)S(1)}, u32[]{:S(2)}, u32[]{:S(2)}) %collective-permute-start.8) | collective-permute-done | bytes 40992 | tf_op jit(solution)/shard_map/ppermute | solution.py:21
  115.6 0.6 fusion.36
  116.2 3.3 %all-to-all-done.1 = f16[32,16,1152]{2,1,0:T(8,128)(2,1)S(1)} async-done(((f16[32,16,1152]{2,1,0:T(8,128)(2,1)}), f16[32,16,1152]{2,1,0:T(8,128)(2,1)S(1)}, u32[]{:S(2)}, u32[]{:S(2)}) %all-to-all-start.1) | async-done | bytes 1179680 | tf_op jit(solution)/shard_map/all_to_all | solution.py:37
  119.6 0.2 convert_reduce_fusion
  119.7 0.2 fusion.19
  119.9 0.7 add_add_fusion
  120.6 0.7 add_add_fusion.1
  (29 shorter events, 0.4 us)
Async XLA Ops:
  0.6 6.1 %collective-permute-start = (bf16[16,1152]{1,0:T(8,128)(2,1)}, bf16[16,1152]{1,0:T(8,128)(2,1)S(1)}, u32[]{:S(2)}, u32[]{:S(2)}) collective-permute-start(bf16[16,1152]{1,0:T(8,128)(2,1)} %param.5), channel_id=1, source_target_pairs={{0,1},{1,0},{2,3},{3,2},{4,5},{5,4},{6,7},{7,6},{8,9},{9,8},{10,11... | collective-permute-start | bytes 110600 | tf_op jit(solution)/shard_map/ppermute | solution.py:21
  9.8 16.9 %copy-start.3 = (bf16[16,1152]{1,0:T(8,128)(2,1)S(1)}, bf16[16,1152]{1,0:T(8,128)(2,1)}, u32[]{:S(2)}) copy-start(bf16[16,1152]{1,0:T(8,128)(2,1)} %param.5) | copy-start | bytes 110596
  9.8 56.2 %all-to-all-start = ((bf16[32,16,1152]{2,1,0:T(8,128)(2,1)}), bf16[32,16,1152]{2,1,0:T(8,128)(2,1)S(1)}, u32[]{:S(2)}, u32[]{:S(2)}) async-start(bf16[32,16,1152]{2,1,0:T(8,128)(2,1)} %broadcast_in_dim.8), calls=%async_computation | async-start | bytes 2359296 | tf_op jit(solution)/shard_map/all_to_all | solution.py:32
  26.7 38.3 %copy-start.4 = (s32[16384]{0:T(1024)S(1)}, s32[16384]{0:T(1024)}, u32[]{:S(2)}) copy-start(s32[16384]{0:T(1024)} %param.7) | copy-start | bytes 196612
  61.7 6.0 %copy-start = (bf16[8,32,1152]{2,1,0:T(8,128)(2,1)}, bf16[8,32,1152]{2,1,0:T(8,128)(2,1)S(1)}, u32[]{:S(2)}) copy-start(bf16[8,32,1152]{2,1,0:T(8,128)(2,1)S(1)} %fusion.10) | copy-start | bytes 1769476
  61.7 4.4 %collective-permute-start.1 = (bf16[256,1152]{1,0:T(8,128)(2,1)S(1)}, bf16[256,1152]{1,0:T(8,128)(2,1)S(1)}, u32[]{:S(2)}, u32[]{:S(2)}) collective-permute-start(bf16[256,1152]{1,0:T(8,128)(2,1)S(1)} %bitcast.42), channel_id=1, source_target_pairs={{0,16},{16,0},{1,17},{17,1},{2,18},{18,2},{3,19},{19,3},{4,20},{20... | collective-permute-start | bytes 1769480 | tf_op jit(solution)/shard_map/ppermute | solution.py:21
  66.0 1.6 %copy-start.5 = (bf16[256,1152]{1,0:T(8,128)(2,1)}, bf16[256,1152]{1,0:T(8,128)(2,1)S(1)}, u32[]{:S(2)}) copy-start(bf16[256,1152]{1,0:T(8,128)(2,1)S(1)} %collective-permute-done.1) | copy-start | bytes 1769476
  68.8 2.7 %copy-start.1 = (bf16[8,32,1152]{2,1,0:T(8,128)(2,1)S(1)}, bf16[8,32,1152]{2,1,0:T(8,128)(2,1)}, u32[]{:S(2)}) copy-start(bf16[8,32,1152]{2,1,0:T(8,128)(2,1)} %copy-done) | copy-start | bytes 1769476
  68.8 2.7 %copy-start.6 = (bf16[256,1152]{1,0:T(8,128)(2,1)S(1)}, bf16[256,1152]{1,0:T(8,128)(2,1)}, u32[]{:S(2)}) copy-start(bf16[256,1152]{1,0:T(8,128)(2,1)} %copy-done.5) | copy-start | bytes 1769476
  68.9 16.8 %collective-permute-start.2 = (f16[8,32,1280]{2,1,0:T(8,128)(2,1)S(1)}, f16[8,32,1280]{2,1,0:T(8,128)(2,1)}, u32[]{:S(2)}, u32[]{:S(2)}) collective-permute-start(f16[8,32,1280]{2,1,0:T(8,128)(2,1)S(1)} %bitcast.41), channel_id=1, source_target_pairs={{0,16},{16,0},{1,17},{17,1},{2,18},{18,2},{3,19},{19,3},{4,20},{20... | collective-permute-start | bytes 1966088 | tf_op jit(solution)/shard_map/ppermute | solution.py:21
  73.6 46.0 %all-to-all-start.1 = ((f16[32,16,1152]{2,1,0:T(8,128)(2,1)}), f16[32,16,1152]{2,1,0:T(8,128)(2,1)S(1)}, u32[]{:S(2)}, u32[]{:S(2)}) async-start(f16[32,16,1152]{2,1,0:T(8,128)(2,1)} %bitcast.40), calls=%async_computation.1 | async-start | bytes 2359296 | tf_op jit(solution)/shard_map/all_to_all | solution.py:37
  87.2 11.0 %collective-permute-start.3 = (f16[2,32,1280]{2,1,0:T(8,128)(2,1)S(1)}, f16[2,32,1280]{2,1,0:T(8,128)(2,1)S(1)}, u32[]{:S(2)}, u32[]{:S(2)}) collective-permute-start(f16[2,32,1280]{2,1,0:T(8,128)(2,1)S(1)} %pad_maximum_fusion.4), channel_id=1, source_target_pairs={{0,2},{2,4},{4,6},{6,8},{8,10},{10,12},{12,14},{14,0},{1,3},{3,5},... | collective-permute-start | bytes 491528 | tf_op jit(solution)/shard_map/ppermute | solution.py:21
  91.0 7.2 %collective-permute-start.4 = (f16[2,32,1280]{2,1,0:T(8,128)(2,1)S(1)}, f16[2,32,1280]{2,1,0:T(8,128)(2,1)S(1)}, u32[]{:S(2)}, u32[]{:S(2)}) collective-permute-start(f16[2,32,1280]{2,1,0:T(8,128)(2,1)S(1)} %pad_maximum_fusion.5), channel_id=1, source_target_pairs={{0,14},{2,0},{4,2},{6,4},{8,6},{10,8},{12,10},{14,12},{1,15},{3,1}... | collective-permute-start | bytes 491528 | tf_op jit(solution)/shard_map/ppermute | solution.py:21
  94.3 13.2 %collective-permute-start.7 = (f16[32,1280]{1,0:T(8,128)(2,1)S(1)}, f16[32,1280]{1,0:T(8,128)(2,1)S(1)}, u32[]{:S(2)}, u32[]{:S(2)}) collective-permute-start(f16[32,1280]{1,0:T(8,128)(2,1)S(1)} %get-tuple-element.11), channel_id=1, source_target_pairs={{0,8},{2,10},{4,12},{6,14},{8,0},{10,2},{12,4},{14,6},{1,9},{3,11}... | collective-permute-start | bytes 245768 | tf_op jit(solution)/shard_map/ppermute | solution.py:21
  98.3 21.4 %copy-start.2 = (bf16[16,1152]{1,0:T(8,128)(2,1)S(1)}, bf16[16,1152]{1,0:T(8,128)(2,1)}, u32[]{:S(2)}) copy-start(bf16[16,1152]{1,0:T(8,128)(2,1)} %param.6) | copy-start | bytes 110596
  98.3 9.7 %collective-permute-start.5 = (f16[32,1280]{1,0:T(8,128)(2,1)S(1)}, f16[32,1280]{1,0:T(8,128)(2,1)S(1)}, u32[]{:S(2)}, u32[]{:S(2)}) collective-permute-start(f16[32,1280]{1,0:T(8,128)(2,1)S(1)} %get-tuple-element.9), channel_id=1, source_target_pairs={{0,4},{2,6},{4,8},{6,10},{8,12},{10,14},{12,0},{14,2},{1,5},{3,7},... | collective-permute-start | bytes 245768 | tf_op jit(solution)/shard_map/ppermute | solution.py:21
  102.0 7.3 %collective-permute-start.6 = (f16[32,1280]{1,0:T(8,128)(2,1)S(1)}, f16[32,1280]{1,0:T(8,128)(2,1)S(1)}, u32[]{:S(2)}, u32[]{:S(2)}) collective-permute-start(f16[32,1280]{1,0:T(8,128)(2,1)S(1)} %get-tuple-element.10), channel_id=1, source_target_pairs={{0,12},{2,14},{4,0},{6,2},{8,4},{10,6},{12,8},{14,10},{1,13},{3,15... | collective-permute-start | bytes 245768 | tf_op jit(solution)/shard_map/ppermute | solution.py:21
  109.3 6.2 %collective-permute-start.8 = (f16[16,1280]{1,0:T(8,128)(2,1)S(1)}, f16[16,1280]{1,0:T(8,128)(2,1)S(1)}, u32[]{:S(2)}, u32[]{:S(2)}) collective-permute-start(f16[16,1280]{1,0:T(8,128)(2,1)S(1)} %slice_convert_fusion), channel_id=1, source_target_pairs={{0,1},{1,0},{2,3},{3,2},{4,5},{5,4},{6,7},{7,6},{8,9},{9,8},{10,11... | collective-permute-start | bytes 122888 | tf_op jit(solution)/shard_map/ppermute | solution.py:21

commit v6 on v5

--- a/solution.py
+++ b/solution.py
@@ -1,12 +1,15 @@
 import jax
 import jax.numpy as jnp
 from jax import lax
+from jax.experimental import pallas as pl
+from jax.experimental.pallas import tpu as pltpu
 from jax.sharding import Mesh, PartitionSpec as P
 
-FINE = ("yhi", "x", "core", "z", "ylo")
-FINE_SIZES = (4, 8, 2, 8, 2)
+FINE = ("yhi", "xhi", "xlo", "core", "z", "ylo")
+FINE_SIZES = (4, 4, 2, 2, 8, 2)
+X = ("xhi", "xlo")
 IMAGE_GROUP = ("core", "z", "ylo")
-TEXT_GROUP = ("yhi", "x")
+TEXT_GROUP = ("xlo", "yhi", "xhi")
 SEND_SCALE = 2.0
 LOSS_SCALE = 0.125
 
@@ -27,8 +30,20 @@
     )
 
 
-def gather(block, axes):
-    copies = jnp.broadcast_to(block[None], (lax.axis_size(axes),) + block.shape)
+def copies_kernel(rows_ref, after_ref, copies_ref):
+    for place in range(copies_ref.shape[0]):
+        copies_ref[place] = rows_ref[...]
+
+
+def gather(block, axes, after):
+    count = lax.axis_size(axes)
+    copies = pl.pallas_call(
+        copies_kernel,
+        out_shape=jax.ShapeDtypeStruct((count,) + block.shape, block.dtype),
+        in_specs=[pl.BlockSpec(memory_space=pltpu.VMEM), pl.BlockSpec(memory_space=pl.ANY)],
+        out_specs=pl.BlockSpec(memory_space=pltpu.VMEM),
+        name="copies",
+    )(block, after)
     return lax.all_to_all(copies, axes, 0, 0, tiled=True)
 
 
@@ -59,9 +74,17 @@
     shift = affine_offset_array[0]
     near_images = jnp.concatenate([picture_vectors, shift_by(picture_vectors, "ylo", 1)])
     own_images = normalize(near_images).astype(jnp.bfloat16)
-    tie = jnp.minimum(jnp.abs(near_images[own_rows, 0]), 0)
-    own_texts = normalize(caption_vectors).astype(jnp.bfloat16) + tie
-    txt_block = gather(own_texts, TEXT_GROUP).reshape(-1, width)
+    own_texts = normalize(caption_vectors).astype(jnp.bfloat16)
+    near_texts = gather(own_texts, ("yhi", "xhi"), near_images[own_rows:]).reshape(-1, width)
+    split = near_texts.shape[0] // 2
+    xlo = lax.axis_index("xlo")
+    txt_block = jnp.zeros((4 * split, width), jnp.bfloat16)
+    for rows, place in (
+        (near_texts, 2 * split * xlo),
+        (shift_by(near_texts[:split], X, -1), 2 * split * (1 - xlo)),
+        (shift_by(near_texts[split:], X, 1), 2 * split * (1 - xlo) + split),
+    ):
+        txt_block = lax.dynamic_update_slice_in_dim(txt_block, rows, place, 0)
     z_images = from_own(lax.all_gather(own_images, "z", axis=0, tiled=False), "z")
     z_images = z_images.reshape(-1, width)
     img_block = jnp.concatenate([z_images, shift_by(z_images, "core", 1)])

time: 122 us -> 136 us (1.11)
  the two profiles are of different devices: /device:TPU:2 before, /device:TPU:1 now
where the time goes in v6:
time: 136 us; the launch traced here: 135 us
  starting transfers between devices  63.1 us (46%)
  blocking collectives  32.7 us (24%)
  waiting for transfers between devices  20.7 us (15%)
  other arithmetic  7.19 us (5%)
  matrix products  4.64 us (3%)
  local copies, waits for them, and re-layouts  2.84 us (2%)
  between operations  2.35 us (2%)
  Pallas kernels  1.63 us (1%)
    ppermute x11, starting transfers between devices, shift_by(): lax.ppermute(block, axis, [(i, (i + step) % count) for i in range(count)])  42.6 us
    all_gather x1, blocking collectives, per_device(): lax.all_gather(own_images, 'z', axis=0, tiled=False)  32.7 us
    ppermute x11, waiting for transfers between devices, shift_by(): lax.ppermute(block, axis, [(i, (i + step) % count) for i in range(count)])  16.9 us
    all_to_all x1, starting transfers between devices, gather(): return lax.all_to_all(copies, axes, 0, 0, tiled=True)  11.5 us
    all_to_all x1, starting transfers between devices, scatter(): lax.all_to_all(parts.reshape(count, parts.shape[0] // count, parts.shape[...  8.98 us
    all_to_all x1, waiting for transfers between devices, scatter(): lax.all_to_all(parts.reshape(count, parts.shape[0] // count, parts.shape[...  3.82 us
  transfers between devices with their start and end apart: 13, of which 6 were waited for; matrix products, arithmetic and copies ran while one was open for 7% of the time, Pallas kernels for 0%

profile of v6, /device:TPU:1, one launch (start us, length us, event | category | flops | bytes accessed | tf_op | source)
XLA Modules:
  0.0 135.1 jit_solution(17103693987911087242)
XLA Ops:
  0.6 4.2 %collective-permute-start = (bf16[16,1152]{1,0:T(8,128)(2,1)}, bf16[16,1152]{1,0:T(8,128)(2,1)S(1)}, u32[]{:S(2)}, u32[]{:S(2)}) collective-permute-start(bf16[16,1152]{1,0:T(8,128)(2,1)} %param.5), channel_id=1, source_target_pairs={{0,1},{1,0},{2,3},{3,2},{4,5},{5,4},{6,7},{7,6},{8,9},{9,8},{10,11... | collective-permute-start | bytes 110600 | tf_op jit(solution)/shard_map/ppermute | solution.py:24
  4.8 0.1 iota_multiply_fusion
  4.9 0.9 fusion.21
  5.8 1.5 %fusion.22.rows_ref = bf16[16,1152]{1,0:T(8,128)(2,1)} fusion(bf16[16,1152]{1,0:T(8,128)(2,1)} %param.6, f32[16]{0:T(128)S(1)} %add_rsqrt_fusion.2), kind=kLoop, calls=%fused_computation.57 | loop fusion | flops 55296 | bytes 73792 | tf_op jit(solution)/shard_map/convert_element_type | solution.py:77
  7.3 1.6 %reshape.166 = s32[4,4,2,2,8,2,16]{6,5,4,3,2,1,0:T(2,128)S(1)} reshape(s32[16384]{0:T(1024)} %param.7) | data formatting | bytes 131072 | tf_op jit(solution)/shard_map/reshape | solution.py:94
  9.0 0.0 copy-start.2
  9.0 0.6 copy-done.2
  9.6 1.6 %copies.1 = bf16[16,16,1152]{2,1,0:T(8,128)(2,1)} custom-call(bf16[16,1152]{1,0:T(8,128)(2,1)} %fusion.22.rows_ref, bf16[16,1152]{1,0:T(8,128)(2,1)} %copy-done.2), custom_call_target="tpu_custom_call" | custom-call | tf_op jit(solution)/shard_map/copies/pallas_call | solution.py:40
  11.2 11.5 %all-to-all-start = ((bf16[16,16,1152]{2,1,0:T(8,128)(2,1)}), bf16[16,16,1152]{2,1,0:T(8,128)(2,1)S(1)}, u32[]{:S(2)}, u32[]{:S(2)}) async-start(bf16[16,16,1152]{2,1,0:T(8,128)(2,1)} %copies.1), calls=%async_computation | async-start | bytes 1179648 | tf_op jit(solution)/shard_map/all_to_all | solution.py:47
  24.1 0.1 eq.17
  24.2 0.1 eq.19
  24.3 0.1 multiply_reduce_fusion
  24.5 0.1 multiply_convert_fusion
  24.6 32.7 %all_gather.4 = bf16[8,32,1152]{2,1,0:T(8,128)(2,1)S(1)} all-gather(bf16[1,32,1152]{2,1,0:T(8,128)(2,1)S(1)} %multiply_convert_fusion), channel_id=1, replica_groups=mesh['yhi'=4,'xhi'=4,'xlo'=2,'core'=2,'z'=8,'ylo'=2] {'z'}, dimensions={0}, use_global_device_ids=true | all-gather | bytes 663552 | tf_op jit(solution)/shard_map/all_gather | solution.py:88
  57.3 4.7 %collective-permute-start.2 = (bf16[128,1152]{1,0:T(8,128)(2,1)S(1)}, bf16[128,1152]{1,0:T(8,128)(2,1)S(1)}, u32[]{:S(2)}, u32[]{:S(2)}) collective-permute-start(bf16[128,1152]{1,0:T(8,128)(2,1)S(1)} %bitcast.52), channel_id=1, source_target_pairs={{0,224},{32,0},{64,32},{96,64},{128,96},{160,128},{192,160},{224,1... | collective-permute-start | bytes 884744 | tf_op jit(solution)/shard_map/ppermute | solution.py:24
  62.0 0.3 fusion.10
  62.2 8.8 %collective-permute-start.1 = (bf16[256,1152]{1,0:T(8,128)(2,1)S(1)}, bf16[256,1152]{1,0:T(8,128)(2,1)S(1)}, u32[]{:S(2)}, u32[]{:S(2)}) collective-permute-start(bf16[256,1152]{1,0:T(8,128)(2,1)S(1)} %bitcast.46), channel_id=1, source_target_pairs={{0,16},{16,0},{1,17},{17,1},{2,18},{18,2},{3,19},{19,3},{4,20},{20... | collective-permute-start | bytes 1769480 | tf_op jit(solution)/shard_map/ppermute | solution.py:24
  71.0 1.9 %collective-permute-start.3 = (bf16[128,1152]{1,0:T(8,128)(2,1)S(1)}, bf16[128,1152]{1,0:T(8,128)(2,1)S(1)}, u32[]{:S(2)}, u32[]{:S(2)}) collective-permute-start(bf16[128,1152]{1,0:T(8,128)(2,1)S(1)} %bitcast.51), channel_id=1, source_target_pairs={{0,32},{32,64},{64,96},{96,128},{128,160},{160,192},{192,224},{224... | collective-permute-start | bytes 884744 | tf_op jit(solution)/shard_map/ppermute | solution.py:24
  73.0 0.1 broadcast_in_dim.8
  73.1 0.1 constant_dynamic-update-slice_fusion.2
  73.2 9.6 %collective-permute-done.3 = bf16[128,1152]{1,0:T(8,128)(2,1)S(1)} collective-permute-done((bf16[128,1152]{1,0:T(8,128)(2,1)S(1)}, bf16[128,1152]{1,0:T(8,128)(2,1)S(1)}, u32[]{:S(2)}, u32[]{:S(2)}) %collective-permute-start.3) | collective-permute-done | bytes 294944 | tf_op jit(solution)/shard_map/ppermute | solution.py:24
  82.8 1.6 %fusion.9 = (f32[512]{0:T(512)S(1)}, f32[512,512]{0,1:T(8,128)S(1)}) fusion(s32[512]{0:T(512)S(1)} %eq.17, s32[512]{0:T(512)S(1)} %eq.19, f32[]{:T(128)} %bitcast.41, bf16[512,1152]{1,0:T(8,128)(2,1)S(1)} %constant_dynamic-update-slice_fusion, bf16[256,1152]{1,0:T(8,128)(2,1)S(1)} %collective-permute-done.1, bf16[256,1152]{1,0:T(8,128)(2,1)S(1)} %bitcast.47, ...), kind=kOutput, calls=%fused_computation.23 | convolution fusion | flops 610008576 | bytes 3414024 | tf_op jit(solution)/shard_map/dot_general | solution.py:110
  84.4 1.0 convolution_multiply_fusion.1
  85.4 0.1 broadcast_in_dim.9
  85.5 0.2 fusion.3
  85.7 2.7 %collective-permute-start.4 = (f16[8,32,1280]{2,1,0:T(8,128)(2,1)S(1)}, f16[8,32,1280]{2,1,0:T(8,128)(2,1)}, u32[]{:S(2)}, u32[]{:S(2)}) collective-permute-start(f16[8,32,1280]{2,1,0:T(8,128)(2,1)S(1)} %bitcast.45), channel_id=1, source_target_pairs={{0,16},{16,0},{1,17},{17,1},{2,18},{18,2},{3,19},{19,3},{4,20},{20... | collective-permute-start | bytes 1966088 | tf_op jit(solution)/shard_map/ppermute | solution.py:24
  88.4 2.1 %fusion = f16[512,1152]{1,0:T(8,128)(2,1)} fusion(bf16[256,1152]{1,0:T(8,128)(2,1)S(1)} %collective-permute-done.1, bf16[256,1152]{1,0:T(8,128)(2,1)S(1)} %bitcast.48, f32[512,512]{0,1:T(8,128)S(1)} %get-tuple-element.21, s32[512]{0:T(512)S(1)} %eq.17, s32[512]{0:T(512)S(1)} %eq.19), kind=kOutput, calls=%fused_computation.3 | convolution fusion | flops 609353728 | bytes 3411968 | tf_op jit(solution)/shard_map/dot_general | solution.py:119
  90.5 9.0 %all-to-all-start.1 = ((f16[32,16,1152]{2,1,0:T(8,128)(2,1)}), f16[32,16,1152]{2,1,0:T(8,128)(2,1)S(1)}, u32[]{:S(2)}, u32[]{:S(2)}) async-start(f16[32,16,1152]{2,1,0:T(8,128)(2,1)} %bitcast.44), calls=%async_computation.1 | async-start | bytes 2359296 | tf_op jit(solution)/shard_map/all_to_all | solution.py:52
  99.5 1.3 fusion.41
  100.7 0.1 slice_bitcast_fusion
  100.9 3.2 %collective-permute-start.5 = (f16[2,32,1280]{2,1,0:T(8,128)(2,1)S(1)}, f16[2,32,1280]{2,1,0:T(8,128)(2,1)S(1)}, u32[]{:S(2)}, u32[]{:S(2)}) collective-permute-start(f16[2,32,1280]{2,1,0:T(8,128)(2,1)S(1)} %pad_maximum_fusion.4), channel_id=1, source_target_pairs={{0,2},{2,4},{4,6},{6,8},{8,10},{10,12},{12,14},{14,0},{1,3},{3,5},... | collective-permute-start | bytes 491528 | tf_op jit(solution)/shard_map/ppermute | solution.py:24
  104.2 3.3 %collective-permute-start.6 = (f16[2,32,1280]{2,1,0:T(8,128)(2,1)S(1)}, f16[2,32,1280]{2,1,0:T(8,128)(2,1)S(1)}, u32[]{:S(2)}, u32[]{:S(2)}) collective-permute-start(f16[2,32,1280]{2,1,0:T(8,128)(2,1)S(1)} %pad_maximum_fusion.5), channel_id=1, source_target_pairs={{0,14},{2,0},{4,2},{6,4},{8,6},{10,8},{12,10},{14,12},{1,15},{3,1}... | collective-permute-start | bytes 491528 | tf_op jit(solution)/shard_map/ppermute | solution.py:24
  107.4 3.6 %collective-permute-start.9 = (f16[32,1280]{1,0:T(8,128)(2,1)S(1)}, f16[32,1280]{1,0:T(8,128)(2,1)S(1)}, u32[]{:S(2)}, u32[]{:S(2)}) collective-permute-start(f16[32,1280]{1,0:T(8,128)(2,1)S(1)} %get-tuple-element.11), channel_id=1, source_target_pairs={{0,8},{2,10},{4,12},{6,14},{8,0},{10,2},{12,4},{14,6},{1,9},{3,11}... | collective-permute-start | bytes 245768 | tf_op jit(solution)/shard_map/ppermute | solution.py:24
  111.1 0.2 collective-permute-done.6
  111.3 0.0 copy-start
  111.3 3.2 %collective-permute-start.7 = (f16[32,1280]{1,0:T(8,128)(2,1)S(1)}, f16[32,1280]{1,0:T(8,128)(2,1)S(1)}, u32[]{:S(2)}, u32[]{:S(2)}) collective-permute-start(f16[32,1280]{1,0:T(8,128)(2,1)S(1)} %get-tuple-element.9), channel_id=1, source_target_pairs={{0,4},{2,6},{4,8},{6,10},{8,12},{10,14},{12,0},{14,2},{1,5},{3,7},... | collective-permute-start | bytes 245768 | tf_op jit(solution)/shard_map/ppermute | solution.py:24
  114.5 4.2 %collective-permute-start.8 = (f16[32,1280]{1,0:T(8,128)(2,1)S(1)}, f16[32,1280]{1,0:T(8,128)(2,1)S(1)}, u32[]{:S(2)}, u32[]{:S(2)}) collective-permute-start(f16[32,1280]{1,0:T(8,128)(2,1)S(1)} %get-tuple-element.10), channel_id=1, source_target_pairs={{0,12},{2,14},{4,0},{6,2},{8,4},{10,6},{12,8},{14,10},{1,13},{3,15... | collective-permute-start | bytes 245768 | tf_op jit(solution)/shard_map/ppermute | solution.py:24
  118.7 0.4 collective-permute-done.7
  119.2 1.9 %collective-permute-done.8 = f16[32,1280]{1,0:T(8,128)(2,1)S(1)} collective-permute-done((f16[32,1280]{1,0:T(8,128)(2,1)S(1)}, f16[32,1280]{1,0:T(8,128)(2,1)S(1)}, u32[]{:S(2)}, u32[]{:S(2)}) %collective-permute-start.8) | collective-permute-done | bytes 81952 | tf_op jit(solution)/shard_map/ppermute | solution.py:24
  121.1 0.1 fusion.16
  121.2 2.9 %collective-permute-start.10 = (f16[16,1280]{1,0:T(8,128)(2,1)S(1)}, f16[16,1280]{1,0:T(8,128)(2,1)S(1)}, u32[]{:S(2)}, u32[]{:S(2)}) collective-permute-start(f16[16,1280]{1,0:T(8,128)(2,1)S(1)} %slice_convert_fusion), channel_id=1, source_target_pairs={{0,1},{1,0},{2,3},{3,2},{4,5},{5,4},{6,7},{7,6},{8,9},{9,8},{10,11... | collective-permute-start | bytes 122888 | tf_op jit(solution)/shard_map/ppermute | solution.py:24
  124.0 4.8 %collective-permute-done.10 = f16[16,1280]{1,0:T(8,128)(2,1)S(1)} collective-permute-done((f16[16,1280]{1,0:T(8,128)(2,1)S(1)}, f16[16,1280]{1,0:T(8,128)(2,1)S(1)}, u32[]{:S(2)}, u32[]{:S(2)}) %collective-permute-start.10) | collective-permute-done | bytes 40992 | tf_op jit(solution)/shard_map/ppermute | solution.py:24
  128.9 0.6 fusion.36
  129.5 3.8 %all-to-all-done.1 = f16[32,16,1152]{2,1,0:T(8,128)(2,1)S(1)} async-done(((f16[32,16,1152]{2,1,0:T(8,128)(2,1)}), f16[32,16,1152]{2,1,0:T(8,128)(2,1)S(1)}, u32[]{:S(2)}, u32[]{:S(2)}) %all-to-all-start.1) | async-done | bytes 1179680 | tf_op jit(solution)/shard_map/all_to_all | solution.py:52
  133.3 0.2 convert_reduce_fusion
  133.5 0.2 fusion.19
  133.7 0.7 add_add_fusion
  134.4 0.7 add_add_fusion.1
  (32 shorter events, 0.5 us)
Async XLA Ops:
  0.6 8.3 %collective-permute-start = (bf16[16,1152]{1,0:T(8,128)(2,1)}, bf16[16,1152]{1,0:T(8,128)(2,1)S(1)}, u32[]{:S(2)}, u32[]{:S(2)}) collective-permute-start(bf16[16,1152]{1,0:T(8,128)(2,1)} %param.5), channel_id=1, source_target_pairs={{0,1},{1,0},{2,3},{3,2},{4,5},{5,4},{6,7},{7,6},{8,9},{9,8},{10,11... | collective-permute-start | bytes 110600 | tf_op jit(solution)/shard_map/ppermute | solution.py:24
  7.3 17.0 %copy-start.1 = (bf16[16,1152]{1,0:T(8,128)(2,1)S(1)}, bf16[16,1152]{1,0:T(8,128)(2,1)}, u32[]{:S(2)}) copy-start(bf16[16,1152]{1,0:T(8,128)(2,1)} %param.5) | copy-start | bytes 110596
  9.0 0.6 copy-start.2
  11.2 13.1 %copy-start.3 = (bf16[16,1152]{1,0:T(8,128)(2,1)S(1)}, bf16[16,1152]{1,0:T(8,128)(2,1)}, u32[]{:S(2)}) copy-start(bf16[16,1152]{1,0:T(8,128)(2,1)} %copy-done.2) | copy-start | bytes 110596
  11.2 46.0 %all-to-all-start = ((bf16[16,16,1152]{2,1,0:T(8,128)(2,1)}), bf16[16,16,1152]{2,1,0:T(8,128)(2,1)S(1)}, u32[]{:S(2)}, u32[]{:S(2)}) async-start(bf16[16,16,1152]{2,1,0:T(8,128)(2,1)} %copies.1), calls=%async_computation | async-start | bytes 1179648 | tf_op jit(solution)/shard_map/all_to_all | solution.py:47
  57.3 15.9 %collective-permute-start.2 = (bf16[128,1152]{1,0:T(8,128)(2,1)S(1)}, bf16[128,1152]{1,0:T(8,128)(2,1)S(1)}, u32[]{:S(2)}, u32[]{:S(2)}) collective-permute-start(bf16[128,1152]{1,0:T(8,128)(2,1)S(1)} %bitcast.52), channel_id=1, source_target_pairs={{0,224},{32,0},{64,32},{96,64},{128,96},{160,128},{192,160},{224,1... | collective-permute-start | bytes 884744 | tf_op jit(solution)/shard_map/ppermute | solution.py:24
  62.2 20.6 %collective-permute-start.1 = (bf16[256,1152]{1,0:T(8,128)(2,1)S(1)}, bf16[256,1152]{1,0:T(8,128)(2,1)S(1)}, u32[]{:S(2)}, u32[]{:S(2)}) collective-permute-start(bf16[256,1152]{1,0:T(8,128)(2,1)S(1)} %bitcast.46), channel_id=1, source_target_pairs={{0,16},{16,0},{1,17},{17,1},{2,18},{18,2},{3,19},{19,3},{4,20},{20... | collective-permute-start | bytes 1769480 | tf_op jit(solution)/shard_map/ppermute | solution.py:24
  71.0 11.7 %collective-permute-start.3 = (bf16[128,1152]{1,0:T(8,128)(2,1)S(1)}, bf16[128,1152]{1,0:T(8,128)(2,1)S(1)}, u32[]{:S(2)}, u32[]{:S(2)}) collective-permute-start(bf16[128,1152]{1,0:T(8,128)(2,1)S(1)} %bitcast.51), channel_id=1, source_target_pairs={{0,32},{32,64},{64,96},{96,128},{128,160},{160,192},{192,224},{224... | collective-permute-start | bytes 884744 | tf_op jit(solution)/shard_map/ppermute | solution.py:24
  85.7 13.8 %collective-permute-start.4 = (f16[8,32,1280]{2,1,0:T(8,128)(2,1)S(1)}, f16[8,32,1280]{2,1,0:T(8,128)(2,1)}, u32[]{:S(2)}, u32[]{:S(2)}) collective-permute-start(f16[8,32,1280]{2,1,0:T(8,128)(2,1)S(1)} %bitcast.45), channel_id=1, source_target_pairs={{0,16},{16,0},{1,17},{17,1},{2,18},{18,2},{3,19},{19,3},{4,20},{20... | collective-permute-start | bytes 1966088 | tf_op jit(solution)/shard_map/ppermute | solution.py:24
  90.5 42.8 %all-to-all-start.1 = ((f16[32,16,1152]{2,1,0:T(8,128)(2,1)}), f16[32,16,1152]{2,1,0:T(8,128)(2,1)S(1)}, u32[]{:S(2)}, u32[]{:S(2)}) async-start(f16[32,16,1152]{2,1,0:T(8,128)(2,1)} %bitcast.44), calls=%async_computation.1 | async-start | bytes 2359296 | tf_op jit(solution)/shard_map/all_to_all | solution.py:52
  100.9 10.2 %collective-permute-start.5 = (f16[2,32,1280]{2,1,0:T(8,128)(2,1)S(1)}, f16[2,32,1280]{2,1,0:T(8,128)(2,1)S(1)}, u32[]{:S(2)}, u32[]{:S(2)}) collective-permute-start(f16[2,32,1280]{2,1,0:T(8,128)(2,1)S(1)} %pad_maximum_fusion.4), channel_id=1, source_target_pairs={{0,2},{2,4},{4,6},{6,8},{8,10},{10,12},{12,14},{14,0},{1,3},{3,5},... | collective-permute-start | bytes 491528 | tf_op jit(solution)/shard_map/ppermute | solution.py:24
  104.2 7.1 %collective-permute-start.6 = (f16[2,32,1280]{2,1,0:T(8,128)(2,1)S(1)}, f16[2,32,1280]{2,1,0:T(8,128)(2,1)S(1)}, u32[]{:S(2)}, u32[]{:S(2)}) collective-permute-start(f16[2,32,1280]{2,1,0:T(8,128)(2,1)S(1)} %pad_maximum_fusion.5), channel_id=1, source_target_pairs={{0,14},{2,0},{4,2},{6,4},{8,6},{10,8},{12,10},{14,12},{1,15},{3,1}... | collective-permute-start | bytes 491528 | tf_op jit(solution)/shard_map/ppermute | solution.py:24
  107.4 11.3 %collective-permute-start.9 = (f16[32,1280]{1,0:T(8,128)(2,1)S(1)}, f16[32,1280]{1,0:T(8,128)(2,1)S(1)}, u32[]{:S(2)}, u32[]{:S(2)}) collective-permute-start(f16[32,1280]{1,0:T(8,128)(2,1)S(1)} %get-tuple-element.11), channel_id=1, source_target_pairs={{0,8},{2,10},{4,12},{6,14},{8,0},{10,2},{12,4},{14,6},{1,9},{3,11}... | collective-permute-start | bytes 245768 | tf_op jit(solution)/shard_map/ppermute | solution.py:24
  111.3 22.2 %copy-start = (bf16[16,1152]{1,0:T(8,128)(2,1)S(1)}, bf16[16,1152]{1,0:T(8,128)(2,1)}, u32[]{:S(2)}) copy-start(bf16[16,1152]{1,0:T(8,128)(2,1)} %param.6) | copy-start | bytes 110596
  111.3 7.9 %collective-permute-start.7 = (f16[32,1280]{1,0:T(8,128)(2,1)S(1)}, f16[32,1280]{1,0:T(8,128)(2,1)S(1)}, u32[]{:S(2)}, u32[]{:S(2)}) collective-permute-start(f16[32,1280]{1,0:T(8,128)(2,1)S(1)} %get-tuple-element.9), channel_id=1, source_target_pairs={{0,4},{2,6},{4,8},{6,10},{8,12},{10,14},{12,0},{14,2},{1,5},{3,7},... | collective-permute-start | bytes 245768 | tf_op jit(solution)/shard_map/ppermute | solution.py:24
  114.5 6.5 %collective-permute-start.8 = (f16[32,1280]{1,0:T(8,128)(2,1)S(1)}, f16[32,1280]{1,0:T(8,128)(2,1)S(1)}, u32[]{:S(2)}, u32[]{:S(2)}) collective-permute-start(f16[32,1280]{1,0:T(8,128)(2,1)S(1)} %get-tuple-element.10), channel_id=1, source_target_pairs={{0,12},{2,14},{4,0},{6,2},{8,4},{10,6},{12,8},{14,10},{1,13},{3,15... | collective-permute-start | bytes 245768 | tf_op jit(solution)/shard_map/ppermute | solution.py:24
  121.2 7.7 %collective-permute-start.10 = (f16[16,1280]{1,0:T(8,128)(2,1)S(1)}, f16[16,1280]{1,0:T(8,128)(2,1)S(1)}, u32[]{:S(2)}, u32[]{:S(2)}) collective-permute-start(f16[16,1280]{1,0:T(8,128)(2,1)S(1)} %slice_convert_fusion), channel_id=1, source_target_pairs={{0,1},{1,0},{2,3},{3,2},{4,5},{5,4},{6,7},{7,6},{8,9},{9,8},{10,11... | collective-permute-start | bytes 122888 | tf_op jit(solution)/shard_map/ppermute | solution.py:24

commit v7 on v5

--- a/solution.py
+++ b/solution.py
@@ -1,6 +1,8 @@
 import jax
 import jax.numpy as jnp
 from jax import lax
+from jax.experimental import pallas as pl
+from jax.experimental.pallas import tpu as pltpu
 from jax.sharding import Mesh, PartitionSpec as P
 
 FINE = ("yhi", "x", "core", "z", "ylo")
@@ -9,6 +11,7 @@
 TEXT_GROUP = ("yhi", "x")
 SEND_SCALE = 2.0
 LOSS_SCALE = 0.125
+WAIT_FLOPS = 100_000_000_000
 
 
 def normalize(raw):
@@ -27,9 +30,38 @@
     )
 
 
-def gather(block, axes):
-    copies = jnp.broadcast_to(block[None], (lax.axis_size(axes),) + block.shape)
+def copies_kernel(raw_ref, copies_ref):
+    rows = normalize(raw_ref[...]).astype(copies_ref.dtype)
+    for place in range(copies_ref.shape[0]):
+        copies_ref[place] = rows
+
+
+def gather(raw, axes):
+    copies = pl.pallas_call(
+        copies_kernel,
+        out_shape=jax.ShapeDtypeStruct((lax.axis_size(axes),) + raw.shape, jnp.bfloat16),
+        in_specs=[pl.BlockSpec(memory_space=pltpu.VMEM)],
+        out_specs=pl.BlockSpec(memory_space=pltpu.VMEM),
+        name="copies",
+    )(raw)
     return lax.all_to_all(copies, axes, 0, 0, tiled=True)
+
+
+def rows_kernel(first_ref, second_ref, rows_ref):
+    count = first_ref.shape[0]
+    rows_ref[:count] = normalize(first_ref[...]).astype(rows_ref.dtype)
+    rows_ref[count:] = normalize(second_ref[...]).astype(rows_ref.dtype)
+
+
+def normalized_rows(first, second):
+    return pl.pallas_call(
+        rows_kernel,
+        out_shape=jax.ShapeDtypeStruct((2 * first.shape[0], first.shape[1]), jnp.bfloat16),
+        in_specs=[pl.BlockSpec(memory_space=pltpu.VMEM)] * 2,
+        out_specs=pl.BlockSpec(memory_space=pltpu.VMEM),
+        cost_estimate=pl.CostEstimate(flops=WAIT_FLOPS, bytes_accessed=0, transcendentals=0),
+        name="rows",
+    )(first, second)
 
 
 def scatter(parts, axes):
@@ -57,11 +89,8 @@
     own_rows, width = picture_vectors.shape
     similarity_multiplier = sharpness_factor[0]
     shift = affine_offset_array[0]
-    near_images = jnp.concatenate([picture_vectors, shift_by(picture_vectors, "ylo", 1)])
-    own_images = normalize(near_images).astype(jnp.bfloat16)
-    tie = jnp.minimum(jnp.abs(near_images[own_rows, 0]), 0)
-    own_texts = normalize(caption_vectors).astype(jnp.bfloat16) + tie
-    txt_block = gather(own_texts, TEXT_GROUP).reshape(-1, width)
+    own_images = normalized_rows(picture_vectors, shift_by(picture_vectors, "ylo", 1))
+    txt_block = gather(caption_vectors, TEXT_GROUP).reshape(-1, width)
     z_images = from_own(lax.all_gather(own_images, "z", axis=0, tiled=False), "z")
     z_images = z_images.reshape(-1, width)
     img_block = jnp.concatenate([z_images, shift_by(z_images, "core", 1)])
@@ -101,7 +130,7 @@
     img_part = jnp.concatenate(
         [img_part, jnp.broadcast_to(loss[:, None] * LOSS_SCALE, (image_count, 128))], axis=1
     ).reshape(2, 8, 2 * own_rows, width + 128)
-    total = img_part[0] + full(shift_by(half(img_part[1]), "core", 1))
+    total = img_part[0] + shift_by(img_part[1], "core", 1)
     far = shift_by(half(total[4]), "z", 4)
     ahead = full(shift_by(half(jnp.stack([total[1], total[3]])), "z", 1))
     back = full(shift_by(half(jnp.stack([total[7], total[5]])), "z", -1))

time: 122 us -> 121 us (level)
  Pallas kernels: 0 us -> 3.49 us
  waiting for transfers between devices: 11.4 us -> 9.05 us
  starting transfers between devices: 58.7 us -> 57.2 us
    pallas_call x0 -> x2, Pallas kernels: none -> 3.49 us  [the longest x1 1.96 us: gather(): pl.pallas_call(copies_kernel, out_shape=jax.ShapeDtypeStruct((lax.axis_si...]
    all_to_all x1, starting transfers between devices: 16.9 us -> 15.1 us  [gather(): return lax.all_to_all(copies, axes, 0, 0, tiled=True)]
    ppermute x9, waiting for transfers between devices: 8.1 us -> 6.49 us  [shift_by(): lax.ppermute(block, axis, [(i, (i + step) % count) for i in range(count)])]
    concatenate x0 -> x1, other arithmetic: none -> 1.25 us  [per_device(): jnp.concatenate([img_part, jnp.broadcast_to(loss[:, None] * LOSS_SCALE, (...]
  transfers between devices with their start and end apart: 11 -> 11, of which waited for: 7 -> 5; matrix products, arithmetic and copies ran while one was open for 6% -> 5% of each run, Pallas kernels for 0% -> 3%
where the time goes in v7:
time: 121 us; the launch traced here: 120 us
  starting transfers between devices  57.2 us (47%)
  blocking collectives  35.4 us (29%)
  waiting for transfers between devices  9.05 us (7%)
  other arithmetic  5.87 us (5%)
  matrix products  4.65 us (4%)
  Pallas kernels  3.49 us (3%)
  between operations  2.31 us (2%)
  local copies, waits for them, and re-layouts  1.72 us (1%)
    all_gather x1, blocking collectives, per_device(): lax.all_gather(own_images, 'z', axis=0, tiled=False)  35.4 us
    ppermute x9, starting transfers between devices, shift_by(): lax.ppermute(block, axis, [(i, (i + step) % count) for i in range(count)])  30 us
    all_to_all x1, starting transfers between devices, gather(): return lax.all_to_all(copies, axes, 0, 0, tiled=True)  15.1 us
    all_to_all x1, starting transfers between devices, scatter(): lax.all_to_all(parts.reshape(count, parts.shape[0] // count, parts.shape[...  12.1 us
    ppermute x9, waiting for transfers between devices, shift_by(): lax.ppermute(block, axis, [(i, (i + step) % count) for i in range(count)])  6.49 us
    all_to_all x1, waiting for transfers between devices, scatter(): lax.all_to_all(parts.reshape(count, parts.shape[0] // count, parts.shape[...  2.56 us
  transfers between devices with their start and end apart: 11, of which 5 were waited for; matrix products, arithmetic and copies ran while one was open for 5% of the time, Pallas kernels for 3%

profile of v7, /device:TPU:2, one launch (start us, length us, event | category | flops | bytes accessed | tf_op | source)
XLA Modules:
  0.0 119.7 jit_solution(10181612315356249845)
XLA Ops:
  0.6 3.6 %collective-permute-start = (bf16[16,1152]{1,0:T(8,128)(2,1)}, bf16[16,1152]{1,0:T(8,128)(2,1)S(1)}, u32[]{:S(2)}, u32[]{:S(2)}) collective-permute-start(bf16[16,1152]{1,0:T(8,128)(2,1)} %first_ref.1), channel_id=1, source_target_pairs={{0,1},{1,0},{2,3},{3,2},{4,5},{5,4},{6,7},{7,6},{8,9},{9,8},{10,11... | collective-permute-start | bytes 110600 | tf_op jit(solution)/shard_map/ppermute | solution.py:24
  4.2 2.0 %copies.1 = bf16[32,16,1152]{2,1,0:T(8,128)(2,1)} custom-call(bf16[16,1152]{1,0:T(8,128)(2,1)} %raw_ref.1), custom_call_target="tpu_custom_call" | custom-call | tf_op jit(solution)/shard_map/copies/pallas_call | solution.py:40
  6.2 15.1 %all-to-all-start = ((bf16[32,16,1152]{2,1,0:T(8,128)(2,1)}), bf16[32,16,1152]{2,1,0:T(8,128)(2,1)S(1)}, u32[]{:S(2)}, u32[]{:S(2)}) async-start(bf16[32,16,1152]{2,1,0:T(8,128)(2,1)} %copies.1), calls=%async_computation | async-start | bytes 2359296 | tf_op jit(solution)/shard_map/all_to_all | solution.py:47
  21.3 0.0 collective-permute-done.second_ref
  21.3 0.0 copy-start.5
  21.3 0.6 copy-done.5
  21.9 1.5 %rows.1 = bf16[32,1152]{1,0:T(8,128)(2,1)} custom-call(bf16[16,1152]{1,0:T(8,128)(2,1)} %first_ref.1, bf16[16,1152]{1,0:T(8,128)(2,1)} %copy-done.5), custom_call_target="tpu_custom_call" | custom-call | flops 99999997952 | tf_op jit(solution)/shard_map/rows/pallas_call | solution.py:57
  23.5 35.4 %all-gather = bf16[256,1152]{1,0:T(8,128)(2,1)S(1)} all-gather(bf16[32,1152]{1,0:T(8,128)(2,1)} %rows.1), channel_id=2, replica_groups=mesh['yhi'=4,'x'=8,'core'=2,'z'=8,'ylo'=2] {'z'}, dimensions={0}, use_global_device_ids=true | all-gather | bytes 663552 | tf_op jit(solution)/shard_map/all_gather | solution.py:94
  58.9 0.2 fusion.9
  59.1 1.9 %collective-permute-start.1 = (bf16[256,1152]{1,0:T(8,128)(2,1)S(1)}, bf16[256,1152]{1,0:T(8,128)(2,1)S(1)}, u32[]{:S(2)}, u32[]{:S(2)}) collective-permute-start(bf16[256,1152]{1,0:T(8,128)(2,1)S(1)} %bitcast.40), channel_id=1, source_target_pairs={{0,16},{16,0},{1,17},{17,1},{2,18},{18,2},{3,19},{19,3},{4,20},{20... | collective-permute-start | bytes 1769480 | tf_op jit(solution)/shard_map/ppermute | solution.py:24
  62.4 0.1 fusion.29
  62.5 0.1 eq.19
  62.5 0.0 copy-done.2
  62.5 0.7 reshape.97
  63.4 0.1 eq.17
  63.5 0.0 collective-permute-done.1
  63.5 0.0 all-to-all-done
  63.5 1.6 %fusion.8 = (f32[512]{0:T(512)S(1)}, f32[512,512]{0,1:T(8,128)S(1)}) fusion(s32[512]{0:T(512)S(1)} %eq.17, s32[512]{0:T(512)S(1)} %eq.19, f32[]{:T(128)} %bitcast.34, bf16[512,1152]{1,0:T(8,128)(2,1)S(1)} %bitcast.37, bf16[256,1152]{1,0:T(8,128)(2,1)S(1)} %collective-permute-done.1, bf16[256,1152]{1,0:T(8,128)(2,1)S(1)} %bitcast.41, f32[]{:T(128)} %bitcast.33), kind=kOutput, calls=%fused_computation.21 | convolution fusion | flops 610008576 | bytes 3414024 | tf_op jit(solution)/shard_map/dot_general | solution.py:116
  65.1 1.0 convolution_multiply_fusion.1
  66.1 0.1 broadcast_in_dim.6
  66.2 1.3 %pad_maximum_fusion = (f32[256,1280]{1,0:T(8,128)}, f32[256,1280]{1,0:T(8,128)S(1)}) fusion(f32[512,128]{1,0:T(8,128)S(1)} %broadcast_in_dim.6, f32[512,1152]{1,0:T(8,128)S(1)} %convolution_multiply_fusion.1), kind=kLoop, calls=%fused_computation.12 | loop fusion | flops 655360 | bytes 5242880 | tf_op jit(solution)/shard_map/concatenate | solution.py:130
  67.5 2.4 %collective-permute-start.2 = (f32[8,32,1280]{2,1,0:T(8,128)}, f32[8,32,1280]{2,1,0:T(8,128)}, u32[]{:S(2)}, u32[]{:S(2)}) collective-permute-start(f32[8,32,1280]{2,1,0:T(8,128)} %bitcast.10), channel_id=1, source_target_pairs={{0,16},{16,0},{1,17},{17,1},{2,18},{18,2},{3,19},{19,3},{4,20},{20... | collective-permute-start | bytes 3932168 | tf_op jit(solution)/shard_map/ppermute | solution.py:24
  69.9 2.1 %fusion = f16[512,1152]{1,0:T(8,128)(2,1)} fusion(bf16[256,1152]{1,0:T(8,128)(2,1)S(1)} %copy-done.4, bf16[256,1152]{1,0:T(8,128)(2,1)S(1)} %bitcast.42, f32[512,512]{0,1:T(8,128)S(1)} %get-tuple-element.23, s32[512]{0:T(512)S(1)} %eq.17, s32[512]{0:T(512)S(1)} %eq.19), kind=kOutput, calls=%fused_computation.3 | convolution fusion | flops 609353728 | bytes 3411968 | tf_op jit(solution)/shard_map/dot_general | solution.py:125
  72.0 12.1 %all-to-all-start.1 = ((f16[32,16,1152]{2,1,0:T(8,128)(2,1)}), f16[32,16,1152]{2,1,0:T(8,128)(2,1)S(1)}, u32[]{:S(2)}, u32[]{:S(2)}) async-start(f16[32,16,1152]{2,1,0:T(8,128)(2,1)} %bitcast.39), calls=%async_computation.1 | async-start | bytes 2359296 | tf_op jit(solution)/shard_map/all_to_all | solution.py:69
  84.1 0.0 collective-permute-done.2
  84.1 1.5 %fusion.38 = (f16[8,32,1280]{2,1,0:T(8,128)(2,1)S(1)}, f32[8,32,1280]{2,1,0:T(8,128)S(1)}) fusion(f32[8,32,1280]{2,1,0:T(8,128)S(1)} %bitcast.35, f32[8,32,1280]{2,1,0:T(8,128)} %collective-permute-done.2), kind=kLoop, calls=%fused_computation.86 | loop fusion | flops 655360 | bytes 4587520 | tf_op jit(solution)/shard_map/convert.9
  85.6 0.1 slice_bitcast_fusion
  85.7 3.6 %collective-permute-start.3 = (f16[2,32,1280]{2,1,0:T(8,128)(2,1)S(1)}, f16[2,32,1280]{2,1,0:T(8,128)(2,1)S(1)}, u32[]{:S(2)}, u32[]{:S(2)}) collective-permute-start(f16[2,32,1280]{2,1,0:T(8,128)(2,1)S(1)} %pad_maximum_fusion.4), channel_id=1, source_target_pairs={{0,2},{2,4},{4,6},{6,8},{8,10},{10,12},{12,14},{14,0},{1,3},{3,5},... | collective-permute-start | bytes 491528 | tf_op jit(solution)/shard_map/ppermute | solution.py:24
  89.4 3.4 %collective-permute-start.4 = (f16[2,32,1280]{2,1,0:T(8,128)(2,1)S(1)}, f16[2,32,1280]{2,1,0:T(8,128)(2,1)S(1)}, u32[]{:S(2)}, u32[]{:S(2)}) collective-permute-start(f16[2,32,1280]{2,1,0:T(8,128)(2,1)S(1)} %pad_maximum_fusion.5), channel_id=1, source_target_pairs={{0,14},{2,0},{4,2},{6,4},{8,6},{10,8},{12,10},{14,12},{1,15},{3,1}... | collective-permute-start | bytes 491528 | tf_op jit(solution)/shard_map/ppermute | solution.py:24
  92.9 3.8 %collective-permute-start.7 = (f16[32,1280]{1,0:T(8,128)(2,1)S(1)}, f16[32,1280]{1,0:T(8,128)(2,1)S(1)}, u32[]{:S(2)}, u32[]{:S(2)}) collective-permute-start(f16[32,1280]{1,0:T(8,128)(2,1)S(1)} %get-tuple-element.13), channel_id=1, source_target_pairs={{0,8},{2,10},{4,12},{6,14},{8,0},{10,2},{12,4},{14,6},{1,9},{3,11}... | collective-permute-start | bytes 245768 | tf_op jit(solution)/shard_map/ppermute | solution.py:24
  96.7 0.0 collective-permute-done.3
  96.8 0.0 collective-permute-done.4
  96.8 0.0 copy-start
  96.9 0.0 copy-start.1
  96.9 3.6 %collective-permute-start.5 = (f16[32,1280]{1,0:T(8,128)(2,1)S(1)}, f16[32,1280]{1,0:T(8,128)(2,1)S(1)}, u32[]{:S(2)}, u32[]{:S(2)}) collective-permute-start(f16[32,1280]{1,0:T(8,128)(2,1)S(1)} %get-tuple-element.11), channel_id=1, source_target_pairs={{0,4},{2,6},{4,8},{6,10},{8,12},{10,14},{12,0},{14,2},{1,5},{3,7},... | collective-permute-start | bytes 245768 | tf_op jit(solution)/shard_map/ppermute | solution.py:24
  100.5 4.4 %collective-permute-start.6 = (f16[32,1280]{1,0:T(8,128)(2,1)S(1)}, f16[32,1280]{1,0:T(8,128)(2,1)S(1)}, u32[]{:S(2)}, u32[]{:S(2)}) collective-permute-start(f16[32,1280]{1,0:T(8,128)(2,1)S(1)} %get-tuple-element.12), channel_id=1, source_target_pairs={{0,12},{2,14},{4,0},{6,2},{8,4},{10,6},{12,8},{14,10},{1,13},{3,15... | collective-permute-start | bytes 245768 | tf_op jit(solution)/shard_map/ppermute | solution.py:24
  105.0 0.9 collective-permute-done.7
  105.9 0.7 collective-permute-done.5
  106.5 1.3 %collective-permute-done.6 = f16[32,1280]{1,0:T(8,128)(2,1)S(1)} collective-permute-done((f16[32,1280]{1,0:T(8,128)(2,1)S(1)}, f16[32,1280]{1,0:T(8,128)(2,1)S(1)}, u32[]{:S(2)}, u32[]{:S(2)}) %collective-permute-start.6) | collective-permute-done | bytes 81952 | tf_op jit(solution)/shard_map/ppermute | solution.py:24
  107.8 0.1 fusion.15
  107.9 3.2 %collective-permute-start.8 = (f16[16,1280]{1,0:T(8,128)(2,1)S(1)}, f16[16,1280]{1,0:T(8,128)(2,1)S(1)}, u32[]{:S(2)}, u32[]{:S(2)}) collective-permute-start(f16[16,1280]{1,0:T(8,128)(2,1)S(1)} %slice_convert_fusion), channel_id=1, source_target_pairs={{0,1},{1,0},{2,3},{3,2},{4,5},{5,4},{6,7},{7,6},{8,9},{9,8},{10,11... | collective-permute-start | bytes 122888 | tf_op jit(solution)/shard_map/ppermute | solution.py:24
  111.1 3.6 %collective-permute-done.8 = f16[16,1280]{1,0:T(8,128)(2,1)S(1)} collective-permute-done((f16[16,1280]{1,0:T(8,128)(2,1)S(1)}, f16[16,1280]{1,0:T(8,128)(2,1)S(1)}, u32[]{:S(2)}, u32[]{:S(2)}) %collective-permute-start.8) | collective-permute-done | bytes 40992 | tf_op jit(solution)/shard_map/ppermute | solution.py:24
  114.7 0.6 fusion.33
  115.3 2.6 %all-to-all-done.1 = f16[32,16,1152]{2,1,0:T(8,128)(2,1)S(1)} async-done(((f16[32,16,1152]{2,1,0:T(8,128)(2,1)}), f16[32,16,1152]{2,1,0:T(8,128)(2,1)S(1)}, u32[]{:S(2)}, u32[]{:S(2)}) %all-to-all-start.1) | async-done | bytes 1179680 | tf_op jit(solution)/shard_map/all_to_all | solution.py:69
  117.9 0.2 convert_reduce_fusion
  118.1 0.2 fusion.18
  118.3 0.7 add_add_fusion.1
  119.0 0.7 add_add_fusion
  (21 shorter events, 0.4 us)
Async XLA Ops:
  0.6 20.7 %collective-permute-start = (bf16[16,1152]{1,0:T(8,128)(2,1)}, bf16[16,1152]{1,0:T(8,128)(2,1)S(1)}, u32[]{:S(2)}, u32[]{:S(2)}) collective-permute-start(bf16[16,1152]{1,0:T(8,128)(2,1)} %first_ref.1), channel_id=1, source_target_pairs={{0,1},{1,0},{2,3},{3,2},{4,5},{5,4},{6,7},{7,6},{8,9},{9,8},{10,11... | collective-permute-start | bytes 110600 | tf_op jit(solution)/shard_map/ppermute | solution.py:24
  6.2 57.3 %all-to-all-start = ((bf16[32,16,1152]{2,1,0:T(8,128)(2,1)}), bf16[32,16,1152]{2,1,0:T(8,128)(2,1)S(1)}, u32[]{:S(2)}, u32[]{:S(2)}) async-start(bf16[32,16,1152]{2,1,0:T(8,128)(2,1)} %copies.1), calls=%async_computation | async-start | bytes 2359296 | tf_op jit(solution)/shard_map/all_to_all | solution.py:47
  21.3 0.6 copy-start.5
  23.5 39.1 %copy-start.2 = (s32[16384]{0:T(1024)S(1)}, s32[16384]{0:T(1024)}, u32[]{:S(2)}) copy-start(s32[16384]{0:T(1024)} %param.7) | copy-start | bytes 196612
  59.1 4.4 %collective-permute-start.1 = (bf16[256,1152]{1,0:T(8,128)(2,1)S(1)}, bf16[256,1152]{1,0:T(8,128)(2,1)S(1)}, u32[]{:S(2)}, u32[]{:S(2)}) collective-permute-start(bf16[256,1152]{1,0:T(8,128)(2,1)S(1)} %bitcast.40), channel_id=1, source_target_pairs={{0,16},{16,0},{1,17},{17,1},{2,18},{18,2},{3,19},{19,3},{4,20},{20... | collective-permute-start | bytes 1769480 | tf_op jit(solution)/shard_map/ppermute | solution.py:24
  63.5 1.6 %copy-start.3 = (bf16[256,1152]{1,0:T(8,128)(2,1)}, bf16[256,1152]{1,0:T(8,128)(2,1)S(1)}, u32[]{:S(2)}) copy-start(bf16[256,1152]{1,0:T(8,128)(2,1)S(1)} %collective-permute-done.1) | copy-start | bytes 1769476
  66.2 3.7 %copy-start.4 = (bf16[256,1152]{1,0:T(8,128)(2,1)S(1)}, bf16[256,1152]{1,0:T(8,128)(2,1)}, u32[]{:S(2)}) copy-start(bf16[256,1152]{1,0:T(8,128)(2,1)} %copy-done.3) | copy-start | bytes 1769476
  67.5 16.6 %collective-permute-start.2 = (f32[8,32,1280]{2,1,0:T(8,128)}, f32[8,32,1280]{2,1,0:T(8,128)}, u32[]{:S(2)}, u32[]{:S(2)}) collective-permute-start(f32[8,32,1280]{2,1,0:T(8,128)} %bitcast.10), channel_id=1, source_target_pairs={{0,16},{16,0},{1,17},{17,1},{2,18},{18,2},{3,19},{19,3},{4,20},{20... | collective-permute-start | bytes 3932168 | tf_op jit(solution)/shard_map/ppermute | solution.py:24
  72.0 45.9 %all-to-all-start.1 = ((f16[32,16,1152]{2,1,0:T(8,128)(2,1)}), f16[32,16,1152]{2,1,0:T(8,128)(2,1)S(1)}, u32[]{:S(2)}, u32[]{:S(2)}) async-start(f16[32,16,1152]{2,1,0:T(8,128)(2,1)} %bitcast.39), calls=%async_computation.1 | async-start | bytes 2359296 | tf_op jit(solution)/shard_map/all_to_all | solution.py:69
  85.7 11.0 %collective-permute-start.3 = (f16[2,32,1280]{2,1,0:T(8,128)(2,1)S(1)}, f16[2,32,1280]{2,1,0:T(8,128)(2,1)S(1)}, u32[]{:S(2)}, u32[]{:S(2)}) collective-permute-start(f16[2,32,1280]{2,1,0:T(8,128)(2,1)S(1)} %pad_maximum_fusion.4), channel_id=1, source_target_pairs={{0,2},{2,4},{4,6},{6,8},{8,10},{10,12},{12,14},{14,0},{1,3},{3,5},... | collective-permute-start | bytes 491528 | tf_op jit(solution)/shard_map/ppermute | solution.py:24
  89.4 7.3 %collective-permute-start.4 = (f16[2,32,1280]{2,1,0:T(8,128)(2,1)S(1)}, f16[2,32,1280]{2,1,0:T(8,128)(2,1)S(1)}, u32[]{:S(2)}, u32[]{:S(2)}) collective-permute-start(f16[2,32,1280]{2,1,0:T(8,128)(2,1)S(1)} %pad_maximum_fusion.5), channel_id=1, source_target_pairs={{0,14},{2,0},{4,2},{6,4},{8,6},{10,8},{12,10},{14,12},{1,15},{3,1}... | collective-permute-start | bytes 491528 | tf_op jit(solution)/shard_map/ppermute | solution.py:24
  92.9 13.0 %collective-permute-start.7 = (f16[32,1280]{1,0:T(8,128)(2,1)S(1)}, f16[32,1280]{1,0:T(8,128)(2,1)S(1)}, u32[]{:S(2)}, u32[]{:S(2)}) collective-permute-start(f16[32,1280]{1,0:T(8,128)(2,1)S(1)} %get-tuple-element.13), channel_id=1, source_target_pairs={{0,8},{2,10},{4,12},{6,14},{8,0},{10,2},{12,4},{14,6},{1,9},{3,11}... | collective-permute-start | bytes 245768 | tf_op jit(solution)/shard_map/ppermute | solution.py:24
  96.8 21.2 %copy-start = (bf16[16,1152]{1,0:T(8,128)(2,1)S(1)}, bf16[16,1152]{1,0:T(8,128)(2,1)}, u32[]{:S(2)}) copy-start(bf16[16,1152]{1,0:T(8,128)(2,1)} %raw_ref.1) | copy-start | bytes 110596
  96.9 21.2 %copy-start.1 = (bf16[16,1152]{1,0:T(8,128)(2,1)S(1)}, bf16[16,1152]{1,0:T(8,128)(2,1)}, u32[]{:S(2)}) copy-start(bf16[16,1152]{1,0:T(8,128)(2,1)} %first_ref.1) | copy-start | bytes 110596
  96.9 9.7 %collective-permute-start.5 = (f16[32,1280]{1,0:T(8,128)(2,1)S(1)}, f16[32,1280]{1,0:T(8,128)(2,1)S(1)}, u32[]{:S(2)}, u32[]{:S(2)}) collective-permute-start(f16[32,1280]{1,0:T(8,128)(2,1)S(1)} %get-tuple-element.11), channel_id=1, source_target_pairs={{0,4},{2,6},{4,8},{6,10},{8,12},{10,14},{12,0},{14,2},{1,5},{3,7},... | collective-permute-start | bytes 245768 | tf_op jit(solution)/shard_map/ppermute | solution.py:24
  100.5 7.3 %collective-permute-start.6 = (f16[32,1280]{1,0:T(8,128)(2,1)S(1)}, f16[32,1280]{1,0:T(8,128)(2,1)S(1)}, u32[]{:S(2)}, u32[]{:S(2)}) collective-permute-start(f16[32,1280]{1,0:T(8,128)(2,1)S(1)} %get-tuple-element.12), channel_id=1, source_target_pairs={{0,12},{2,14},{4,0},{6,2},{8,4},{10,6},{12,8},{14,10},{1,13},{3,15... | collective-permute-start | bytes 245768 | tf_op jit(solution)/shard_map/ppermute | solution.py:24
  107.9 6.8 %collective-permute-start.8 = (f16[16,1280]{1,0:T(8,128)(2,1)S(1)}, f16[16,1280]{1,0:T(8,128)(2,1)S(1)}, u32[]{:S(2)}, u32[]{:S(2)}) collective-permute-start(f16[16,1280]{1,0:T(8,128)(2,1)S(1)} %slice_convert_fusion), channel_id=1, source_target_pairs={{0,1},{1,0},{2,3},{3,2},{4,5},{5,4},{6,7},{7,6},{8,9},{9,8},{10,11... | collective-permute-start | bytes 122888 | tf_op jit(solution)/shard_map/ppermute | solution.py:24

commit v8 on v7

--- a/solution.py
+++ b/solution.py
@@ -47,21 +47,35 @@
     return lax.all_to_all(copies, axes, 0, 0, tiled=True)
 
 
-def rows_kernel(first_ref, second_ref, rows_ref):
-    count = first_ref.shape[0]
-    rows_ref[:count] = normalize(first_ref[...]).astype(rows_ref.dtype)
-    rows_ref[count:] = normalize(second_ref[...]).astype(rows_ref.dtype)
+def pairs_kernel(place_ref, all_ref, pairs_ref):
+    group, core, z, ylo = place_ref[0], place_ref[1], place_ref[2], place_ref[3]
+    lane = lax.broadcasted_iota(jnp.int32, (1, 128), 1)
+    turn = lax.rem(z, 4) * 32
+    for ahead in range(2):
+        first = group * 4 + lax.rem(core + ahead, 2) * 2
+        rows = []
+        for late in range(2):
+            row = all_ref[pl.ds(first + lax.rem(z // 4 + late, 2), 1), :]
+            swapped = jnp.where(lane % 32 < 16, pltpu.roll(row, 112, 1), pltpu.roll(row, 16, 1))
+            rows.append(pltpu.roll(jnp.where(ylo == 0, row, swapped), lax.rem(128 - turn, 128), 1))
+        pairs_ref[2 * ahead : 2 * ahead + 1, :] = jnp.where(lane + turn < 128, rows[0], rows[1])
+        pairs_ref[2 * ahead + 1 : 2 * ahead + 2, :] = jnp.where(lane + turn < 128, rows[1], rows[0])
 
 
-def normalized_rows(first, second):
-    return pl.pallas_call(
-        rows_kernel,
-        out_shape=jax.ShapeDtypeStruct((2 * first.shape[0], first.shape[1]), jnp.bfloat16),
-        in_specs=[pl.BlockSpec(memory_space=pltpu.VMEM)] * 2,
+def image_pairs(caption_partner_position, image_count):
+    place = jnp.stack([lax.axis_index(axes) for axes in (TEXT_GROUP,) + IMAGE_GROUP]).astype(jnp.int32)
+    pairs = pl.pallas_call(
+        pairs_kernel,
+        out_shape=jax.ShapeDtypeStruct((image_count // 128, 128), jnp.int32),
+        in_specs=[
+            pl.BlockSpec(memory_space=pltpu.SMEM),
+            pl.BlockSpec(memory_space=pltpu.VMEM),
+        ],
         out_specs=pl.BlockSpec(memory_space=pltpu.VMEM),
         cost_estimate=pl.CostEstimate(flops=WAIT_FLOPS, bytes_accessed=0, transcendentals=0),
-        name="rows",
-    )(first, second)
+        name="pairs",
+    )(place, caption_partner_position.reshape(-1, 128))
+    return pairs.reshape(-1)
 
 
 def scatter(parts, axes):
@@ -89,28 +103,17 @@
     own_rows, width = picture_vectors.shape
     similarity_multiplier = sharpness_factor[0]
     shift = affine_offset_array[0]
-    own_images = normalized_rows(picture_vectors, shift_by(picture_vectors, "ylo", 1))
+    raw_images = jnp.concatenate([picture_vectors, shift_by(picture_vectors, "ylo", 1)])
     txt_block = gather(caption_vectors, TEXT_GROUP).reshape(-1, width)
-    z_images = from_own(lax.all_gather(own_images, "z", axis=0, tiled=False), "z")
-    z_images = z_images.reshape(-1, width)
+    raw_images = lax.all_gather(raw_images, "z", axis=0, tiled=False)
+    z_images = normalize(from_own(raw_images, "z").reshape(-1, width)).astype(jnp.bfloat16)
     img_block = jnp.concatenate([z_images, shift_by(z_images, "core", 1)])
     image_count = img_block.shape[0]
-
-    def of_group(array, group):
-        rows = array.reshape(FINE_SIZES + (own_rows,))
-        for place, axis in enumerate(FINE):
-            if axis not in group:
-                rows = lax.dynamic_slice_in_dim(rows, lax.axis_index(axis), 1, place)
-        order = [FINE.index(axis) for axis in group]
-        order = order + [i for i in range(len(FINE) + 1) if i not in order]
-        return rows.transpose(order).reshape([lax.axis_size(axis) for axis in group] + [own_rows])
-
-    ids = jnp.arange(caption_partner_position.shape[0], dtype=jnp.int32)
-    text_ids = of_group(ids, TEXT_GROUP).reshape(-1)
-    my_pairs = of_group(caption_partner_position, IMAGE_GROUP)
-    for place, axis in enumerate(IMAGE_GROUP):
-        my_pairs = jnp.moveaxis(from_own(jnp.moveaxis(my_pairs, place, 0), axis), 0, place)
-    my_pairs = my_pairs.reshape(-1)
+    my_pairs = image_pairs(caption_partner_position, image_count)
+    column = jnp.arange(txt_block.shape[0], dtype=jnp.int32)
+    text_ids = (
+        column // own_rows * image_count + lax.axis_index(IMAGE_GROUP) * own_rows + column % own_rows
+    )
     logits = (
         similarity_multiplier
         * lax.dot_general(
@@ -130,7 +133,7 @@
     img_part = jnp.concatenate(
         [img_part, jnp.broadcast_to(loss[:, None] * LOSS_SCALE, (image_count, 128))], axis=1
     ).reshape(2, 8, 2 * own_rows, width + 128)
-    total = img_part[0] + shift_by(img_part[1], "core", 1)
+    total = img_part[0] + full(shift_by(half(img_part[1]), "core", 1))
     far = shift_by(half(total[4]), "z", 4)
     ahead = full(shift_by(half(jnp.stack([total[1], total[3]])), "z", 1))
     back = full(shift_by(half(jnp.stack([total[7], total[5]])), "z", -1))

time: 121 us -> 120 us (level)
  local copies, waits for them, and re-layouts: 1.72 us -> 0.31 us
    concatenate x2 -> x1, other arithmetic: 1.5 us -> 0.01 us  [per_device(): jnp.concatenate([picture_vectors, shift_by(picture_vectors, 'ylo', 1)])]
where the time goes in v8:
time: 120 us; the launch traced here: 119 us
  starting transfers between devices  57.3 us (48%)
  blocking collectives  35 us (29%)
  waiting for transfers between devices  9.69 us (8%)
  matrix products  5.38 us (4%)
  other arithmetic  5.26 us (4%)
  Pallas kernels  3.55 us (3%)
  between operations  2.29 us (2%)
    all_gather x1, blocking collectives, per_device(): raw_images = lax.all_gather(raw_images, 'z', axis=0, tiled=False)  35 us
    ppermute x9, starting transfers between devices, shift_by(): lax.ppermute(block, axis, [(i, (i + step) % count) for i in range(count)])  29.8 us
    all_to_all x1, starting transfers between devices, gather(): return lax.all_to_all(copies, axes, 0, 0, tiled=True)  15.2 us
    all_to_all x1, starting transfers between devices, scatter(): lax.all_to_all(parts.reshape(count, parts.shape[0] // count, parts.shape[...  12.3 us
    ppermute x9, waiting for transfers between devices, shift_by(): lax.ppermute(block, axis, [(i, (i + step) % count) for i in range(count)])  6.67 us
    all_to_all x1, waiting for transfers between devices, scatter(): lax.all_to_all(parts.reshape(count, parts.shape[0] // count, parts.shape[...  3.02 us
  transfers between devices with their start and end apart: 11, of which 5 were waited for; matrix products, arithmetic and copies ran while one was open for 5% of the time, Pallas kernels for 3%

profile of v8, /device:TPU:2, one launch (start us, length us, event | category | flops | bytes accessed | tf_op | source)
XLA Modules:
  0.0 118.7 jit_solution(2054785005151724604)
XLA Ops:
  0.6 3.6 %collective-permute-start = (bf16[16,1152]{1,0:T(8,128)(2,1)}, bf16[16,1152]{1,0:T(8,128)(2,1)S(1)}, u32[]{:S(2)}, u32[]{:S(2)}) collective-permute-start(bf16[16,1152]{1,0:T(8,128)(2,1)} %param.5), channel_id=1, source_target_pairs={{0,1},{1,0},{2,3},{3,2},{4,5},{5,4},{6,7},{7,6},{8,9},{9,8},{10,11... | collective-permute-start | bytes 110600 | tf_op jit(solution)/shard_map/ppermute | solution.py:24
  4.2 2.0 %copies.1 = bf16[32,16,1152]{2,1,0:T(8,128)(2,1)} custom-call(bf16[16,1152]{1,0:T(8,128)(2,1)} %raw_ref.1), custom_call_target="tpu_custom_call" | custom-call | tf_op jit(solution)/shard_map/copies/pallas_call | solution.py:40
  6.2 15.2 %all-to-all-start = ((bf16[32,16,1152]{2,1,0:T(8,128)(2,1)}), bf16[32,16,1152]{2,1,0:T(8,128)(2,1)S(1)}, u32[]{:S(2)}, u32[]{:S(2)}) async-start(bf16[32,16,1152]{2,1,0:T(8,128)(2,1)} %copies.1), calls=%async_computation | async-start | bytes 2359296 | tf_op jit(solution)/shard_map/all_to_all | solution.py:47
  21.4 0.6 pad_add_fusion.place_ref
  22.1 0.0 collective-permute-done
  22.1 0.0 copy-done.3
  22.1 35.0 %all-gather = bf16[256,1152]{1,0:T(8,128)(2,1)S(1)} all-gather(bf16[32,1152]{1,0:T(8,128)(2,1)S(1)} %pad_maximum_fusion.6), channel_id=2, replica_groups=mesh['yhi'=4,'x'=8,'core'=2,'z'=8,'ylo'=2] {'z'}, dimensions={0}, use_global_device_ids=true | all-gather | bytes 663552 | tf_op jit(solution)/shard_map/all_gather | solution.py:108
  57.1 0.3 multiply_reduce_fusion
  57.4 0.1 rsqrt.32
  57.5 0.1 fusion.4
  57.6 0.0 copy-start
  57.7 1.9 %collective-permute-start.1 = (bf16[256,1152]{1,0:T(8,128)(2,1)S(1)}, bf16[256,1152]{1,0:T(8,128)(2,1)S(1)}, u32[]{:S(2)}, u32[]{:S(2)}) collective-permute-start(bf16[256,1152]{1,0:T(8,128)(2,1)S(1)} %fusion.4), channel_id=1, source_target_pairs={{0,16},{16,0},{1,17},{17,1},{2,18},{18,2},{3,19},{19,3},{4,20},{20... | collective-permute-start | bytes 1769480 | tf_op jit(solution)/shard_map/ppermute | solution.py:24
  59.6 1.6 %pairs.1 = s32[4,128]{1,0:T(4,128)} custom-call(s32[4]{0:T(128)} %pad_add_fusion.place_ref, s32[128,128]{1,0:T(8,128)} %bitcast.42), custom_call_target="tpu_custom_call" | custom-call | flops 99999997952 | tf_op jit(solution)/shard_map/pairs/pallas_call | solution.py:67
  62.5 0.0 collective-permute-done.1
  62.5 0.0 copy-start.4
  62.5 0.0 all-to-all-done
  62.5 0.0 copy-done
  62.5 0.0 copy-start.6
  62.5 2.3 %fusion.10 = (f32[512]{0:T(512)S(1)}, f32[512,512]{0,1:T(8,128)S(1)}) fusion(s32[512]{0:T(512)} %bitcast.43, s32[512]{0:T(512)S(1)} %fusion.32, f32[]{:T(128)} %bitcast.35, bf16[512,1152]{1,0:T(8,128)(2,1)S(1)} %bitcast.38, bf16[256,1152]{1,0:T(8,128)(2,1)S(1)} %collective-permute-done.1, bf16[256,1152]{1,0:T(8,128)(2,1)S(1)} %fusion.4, f32[]{:T(128)} %bitcast.34), kind=kOutput, calls=%fused_computation.26 | convolution fusion | flops 610008576 | bytes 3414024 | tf_op jit(solution)/shard_map/dot_general | solution.py:119
  64.9 1.0 convolution_multiply_fusion.1
  65.9 0.1 broadcast_in_dim.6
  66.0 0.2 fusion.3
  66.2 2.5 %collective-permute-start.2 = (f16[8,32,1280]{2,1,0:T(8,128)(2,1)S(1)}, f16[8,32,1280]{2,1,0:T(8,128)(2,1)}, u32[]{:S(2)}, u32[]{:S(2)}) collective-permute-start(f16[8,32,1280]{2,1,0:T(8,128)(2,1)S(1)} %bitcast.41), channel_id=1, source_target_pairs={{0,16},{16,0},{1,17},{17,1},{2,18},{18,2},{3,19},{19,3},{4,20},{20... | collective-permute-start | bytes 1966088 | tf_op jit(solution)/shard_map/ppermute | solution.py:24
  68.7 2.1 %fusion = f16[512,1152]{1,0:T(8,128)(2,1)} fusion(bf16[256,1152]{1,0:T(8,128)(2,1)S(1)} %copy-done.5, bf16[256,1152]{1,0:T(8,128)(2,1)S(1)} %copy-done.1, f32[512,512]{0,1:T(8,128)S(1)} %get-tuple-element.25, s32[512]{0:T(512)S(1)} %bitcast.45, s32[512]{0:T(512)S(1)} %fusion.32), kind=kOutput, calls=%fused_computation.3 | convolution fusion | flops 609353728 | bytes 3411968 | tf_op jit(solution)/shard_map/dot_general | solution.py:128
  70.8 12.3 %all-to-all-start.1 = ((f16[32,16,1152]{2,1,0:T(8,128)(2,1)}), f16[32,16,1152]{2,1,0:T(8,128)(2,1)S(1)}, u32[]{:S(2)}, u32[]{:S(2)}) async-start(f16[32,16,1152]{2,1,0:T(8,128)(2,1)} %bitcast.40), calls=%async_computation.1 | async-start | bytes 2359296 | tf_op jit(solution)/shard_map/all_to_all | solution.py:83
  83.1 0.0 collective-permute-done.2
  83.2 1.3 %fusion.40 = (f16[8,32,1280]{2,1,0:T(8,128)(2,1)S(1)}, f32[8,32,1280]{2,1,0:T(8,128)S(1)}) fusion(f32[8,32,1280]{2,1,0:T(8,128)S(1)} %bitcast.36, f16[8,32,1280]{2,1,0:T(8,128)(2,1)} %collective-permute-done.2), kind=kLoop, calls=%fused_computation.85 | loop fusion | flops 983040 | bytes 3932160 | tf_op jit(solution)/shard_map/convert.10
  84.4 0.1 slice_bitcast_fusion
  84.6 3.5 %collective-permute-start.3 = (f16[2,32,1280]{2,1,0:T(8,128)(2,1)S(1)}, f16[2,32,1280]{2,1,0:T(8,128)(2,1)S(1)}, u32[]{:S(2)}, u32[]{:S(2)}) collective-permute-start(f16[2,32,1280]{2,1,0:T(8,128)(2,1)S(1)} %pad_maximum_fusion.4), channel_id=1, source_target_pairs={{0,2},{2,4},{4,6},{6,8},{8,10},{10,12},{12,14},{14,0},{1,3},{3,5},... | collective-permute-start | bytes 491528 | tf_op jit(solution)/shard_map/ppermute | solution.py:24
  88.1 3.5 %collective-permute-start.4 = (f16[2,32,1280]{2,1,0:T(8,128)(2,1)S(1)}, f16[2,32,1280]{2,1,0:T(8,128)(2,1)S(1)}, u32[]{:S(2)}, u32[]{:S(2)}) collective-permute-start(f16[2,32,1280]{2,1,0:T(8,128)(2,1)S(1)} %pad_maximum_fusion.5), channel_id=1, source_target_pairs={{0,14},{2,0},{4,2},{6,4},{8,6},{10,8},{12,10},{14,12},{1,15},{3,1}... | collective-permute-start | bytes 491528 | tf_op jit(solution)/shard_map/ppermute | solution.py:24
  91.7 3.7 %collective-permute-start.7 = (f16[32,1280]{1,0:T(8,128)(2,1)S(1)}, f16[32,1280]{1,0:T(8,128)(2,1)S(1)}, u32[]{:S(2)}, u32[]{:S(2)}) collective-permute-start(f16[32,1280]{1,0:T(8,128)(2,1)S(1)} %get-tuple-element.15), channel_id=1, source_target_pairs={{0,8},{2,10},{4,12},{6,14},{8,0},{10,2},{12,4},{14,6},{1,9},{3,11}... | collective-permute-start | bytes 245768 | tf_op jit(solution)/shard_map/ppermute | solution.py:24
  95.4 0.0 collective-permute-done.3
  95.5 0.0 collective-permute-done.4
  95.6 0.0 copy-start.2
  95.6 3.5 %collective-permute-start.5 = (f16[32,1280]{1,0:T(8,128)(2,1)S(1)}, f16[32,1280]{1,0:T(8,128)(2,1)S(1)}, u32[]{:S(2)}, u32[]{:S(2)}) collective-permute-start(f16[32,1280]{1,0:T(8,128)(2,1)S(1)} %get-tuple-element.13), channel_id=1, source_target_pairs={{0,4},{2,6},{4,8},{6,10},{8,12},{10,14},{12,0},{14,2},{1,5},{3,7},... | collective-permute-start | bytes 245768 | tf_op jit(solution)/shard_map/ppermute | solution.py:24
  99.1 4.4 %collective-permute-start.6 = (f16[32,1280]{1,0:T(8,128)(2,1)S(1)}, f16[32,1280]{1,0:T(8,128)(2,1)S(1)}, u32[]{:S(2)}, u32[]{:S(2)}) collective-permute-start(f16[32,1280]{1,0:T(8,128)(2,1)S(1)} %get-tuple-element.14), channel_id=1, source_target_pairs={{0,12},{2,14},{4,0},{6,2},{8,4},{10,6},{12,8},{14,10},{1,13},{3,15... | collective-permute-start | bytes 245768 | tf_op jit(solution)/shard_map/ppermute | solution.py:24
  103.5 1.2 %collective-permute-done.7 = f16[32,1280]{1,0:T(8,128)(2,1)S(1)} collective-permute-done((f16[32,1280]{1,0:T(8,128)(2,1)S(1)}, f16[32,1280]{1,0:T(8,128)(2,1)S(1)}, u32[]{:S(2)}, u32[]{:S(2)}) %collective-permute-start.7) | collective-permute-done | bytes 81952 | tf_op jit(solution)/shard_map/ppermute | solution.py:24
  104.7 0.5 collective-permute-done.5
  105.3 1.3 %collective-permute-done.6 = f16[32,1280]{1,0:T(8,128)(2,1)S(1)} collective-permute-done((f16[32,1280]{1,0:T(8,128)(2,1)S(1)}, f16[32,1280]{1,0:T(8,128)(2,1)S(1)}, u32[]{:S(2)}, u32[]{:S(2)}) %collective-permute-start.6) | collective-permute-done | bytes 81952 | tf_op jit(solution)/shard_map/ppermute | solution.py:24
  106.5 0.1 fusion.18
  106.6 3.0 %collective-permute-start.8 = (f16[16,1280]{1,0:T(8,128)(2,1)S(1)}, f16[16,1280]{1,0:T(8,128)(2,1)S(1)}, u32[]{:S(2)}, u32[]{:S(2)}) collective-permute-start(f16[16,1280]{1,0:T(8,128)(2,1)S(1)} %slice_convert_fusion), channel_id=1, source_target_pairs={{0,1},{1,0},{2,3},{3,2},{4,5},{5,4},{6,7},{7,6},{8,9},{9,8},{10,11... | collective-permute-start | bytes 122888 | tf_op jit(solution)/shard_map/ppermute | solution.py:24
  109.6 3.7 %collective-permute-done.8 = f16[16,1280]{1,0:T(8,128)(2,1)S(1)} collective-permute-done((f16[16,1280]{1,0:T(8,128)(2,1)S(1)}, f16[16,1280]{1,0:T(8,128)(2,1)S(1)}, u32[]{:S(2)}, u32[]{:S(2)}) %collective-permute-start.8) | collective-permute-done | bytes 40992 | tf_op jit(solution)/shard_map/ppermute | solution.py:24
  113.3 0.6 fusion.25
  113.9 3.0 %all-to-all-done.1 = f16[32,16,1152]{2,1,0:T(8,128)(2,1)S(1)} async-done(((f16[32,16,1152]{2,1,0:T(8,128)(2,1)}), f16[32,16,1152]{2,1,0:T(8,128)(2,1)S(1)}, u32[]{:S(2)}, u32[]{:S(2)}) %all-to-all-start.1) | async-done | bytes 1179680 | tf_op jit(solution)/shard_map/all_to_all | solution.py:83
  116.9 0.2 convert_reduce_fusion
  117.1 0.2 fusion.21
  117.3 0.7 add_add_fusion.1
  118.0 0.7 add_add_fusion
  (21 shorter events, 0.3 us)
Async XLA Ops:
  0.6 21.5 %collective-permute-start = (bf16[16,1152]{1,0:T(8,128)(2,1)}, bf16[16,1152]{1,0:T(8,128)(2,1)S(1)}, u32[]{:S(2)}, u32[]{:S(2)}) collective-permute-start(bf16[16,1152]{1,0:T(8,128)(2,1)} %param.5), channel_id=1, source_target_pairs={{0,1},{1,0},{2,3},{3,2},{4,5},{5,4},{6,7},{7,6},{8,9},{9,8},{10,11... | collective-permute-start | bytes 110600 | tf_op jit(solution)/shard_map/ppermute | solution.py:24
  6.2 15.9 %copy-start.3 = (bf16[16,1152]{1,0:T(8,128)(2,1)S(1)}, bf16[16,1152]{1,0:T(8,128)(2,1)}, u32[]{:S(2)}) copy-start(bf16[16,1152]{1,0:T(8,128)(2,1)} %param.5) | copy-start | bytes 110596
  6.2 56.3 %all-to-all-start = ((bf16[32,16,1152]{2,1,0:T(8,128)(2,1)}), bf16[32,16,1152]{2,1,0:T(8,128)(2,1)S(1)}, u32[]{:S(2)}, u32[]{:S(2)}) async-start(bf16[32,16,1152]{2,1,0:T(8,128)(2,1)} %copies.1), calls=%async_computation | async-start | bytes 2359296 | tf_op jit(solution)/shard_map/all_to_all | solution.py:47
  57.6 4.9 %copy-start = (bf16[256,1152]{1,0:T(8,128)(2,1)}, bf16[256,1152]{1,0:T(8,128)(2,1)S(1)}, u32[]{:S(2)}) copy-start(bf16[256,1152]{1,0:T(8,128)(2,1)S(1)} %fusion.4) | copy-start | bytes 1769476
  57.7 4.8 %collective-permute-start.1 = (bf16[256,1152]{1,0:T(8,128)(2,1)S(1)}, bf16[256,1152]{1,0:T(8,128)(2,1)S(1)}, u32[]{:S(2)}, u32[]{:S(2)}) collective-permute-start(bf16[256,1152]{1,0:T(8,128)(2,1)S(1)} %fusion.4), channel_id=1, source_target_pairs={{0,16},{16,0},{1,17},{17,1},{2,18},{18,2},{3,19},{19,3},{4,20},{20... | collective-permute-start | bytes 1769480 | tf_op jit(solution)/shard_map/ppermute | solution.py:24
  62.5 2.4 %copy-start.4 = (bf16[256,1152]{1,0:T(8,128)(2,1)}, bf16[256,1152]{1,0:T(8,128)(2,1)S(1)}, u32[]{:S(2)}) copy-start(bf16[256,1152]{1,0:T(8,128)(2,1)S(1)} %collective-permute-done.1) | copy-start | bytes 1769476
  62.5 2.4 %copy-start.6 = (s32[4,128]{1,0:T(4,128)S(1)}, s32[4,128]{1,0:T(4,128)}, u32[]{:S(2)}) copy-start(s32[4,128]{1,0:T(4,128)} %pairs.1) | copy-start | bytes 6148
  66.0 2.7 %copy-start.1 = (bf16[256,1152]{1,0:T(8,128)(2,1)S(1)}, bf16[256,1152]{1,0:T(8,128)(2,1)}, u32[]{:S(2)}) copy-start(bf16[256,1152]{1,0:T(8,128)(2,1)} %copy-done) | copy-start | bytes 1769476
  66.0 2.7 %copy-start.5 = (bf16[256,1152]{1,0:T(8,128)(2,1)S(1)}, bf16[256,1152]{1,0:T(8,128)(2,1)}, u32[]{:S(2)}) copy-start(bf16[256,1152]{1,0:T(8,128)(2,1)} %copy-done.4) | copy-start | bytes 1769476
  66.2 17.0 %collective-permute-start.2 = (f16[8,32,1280]{2,1,0:T(8,128)(2,1)S(1)}, f16[8,32,1280]{2,1,0:T(8,128)(2,1)}, u32[]{:S(2)}, u32[]{:S(2)}) collective-permute-start(f16[8,32,1280]{2,1,0:T(8,128)(2,1)S(1)} %bitcast.41), channel_id=1, source_target_pairs={{0,16},{16,0},{1,17},{17,1},{2,18},{18,2},{3,19},{19,3},{4,20},{20... | collective-permute-start | bytes 1966088 | tf_op jit(solution)/shard_map/ppermute | solution.py:24
  70.8 46.1 %all-to-all-start.1 = ((f16[32,16,1152]{2,1,0:T(8,128)(2,1)}), f16[32,16,1152]{2,1,0:T(8,128)(2,1)S(1)}, u32[]{:S(2)}, u32[]{:S(2)}) async-start(f16[32,16,1152]{2,1,0:T(8,128)(2,1)} %bitcast.40), calls=%async_computation.1 | async-start | bytes 2359296 | tf_op jit(solution)/shard_map/all_to_all | solution.py:83
  84.6 10.9 %collective-permute-start.3 = (f16[2,32,1280]{2,1,0:T(8,128)(2,1)S(1)}, f16[2,32,1280]{2,1,0:T(8,128)(2,1)S(1)}, u32[]{:S(2)}, u32[]{:S(2)}) collective-permute-start(f16[2,32,1280]{2,1,0:T(8,128)(2,1)S(1)} %pad_maximum_fusion.4), channel_id=1, source_target_pairs={{0,2},{2,4},{4,6},{6,8},{8,10},{10,12},{12,14},{14,0},{1,3},{3,5},... | collective-permute-start | bytes 491528 | tf_op jit(solution)/shard_map/ppermute | solution.py:24
  88.1 7.3 %collective-permute-start.4 = (f16[2,32,1280]{2,1,0:T(8,128)(2,1)S(1)}, f16[2,32,1280]{2,1,0:T(8,128)(2,1)S(1)}, u32[]{:S(2)}, u32[]{:S(2)}) collective-permute-start(f16[2,32,1280]{2,1,0:T(8,128)(2,1)S(1)} %pad_maximum_fusion.5), channel_id=1, source_target_pairs={{0,14},{2,0},{4,2},{6,4},{8,6},{10,8},{12,10},{14,12},{1,15},{3,1}... | collective-permute-start | bytes 491528 | tf_op jit(solution)/shard_map/ppermute | solution.py:24
  91.7 13.1 %collective-permute-start.7 = (f16[32,1280]{1,0:T(8,128)(2,1)S(1)}, f16[32,1280]{1,0:T(8,128)(2,1)S(1)}, u32[]{:S(2)}, u32[]{:S(2)}) collective-permute-start(f16[32,1280]{1,0:T(8,128)(2,1)S(1)} %get-tuple-element.15), channel_id=1, source_target_pairs={{0,8},{2,10},{4,12},{6,14},{8,0},{10,2},{12,4},{14,6},{1,9},{3,11}... | collective-permute-start | bytes 245768 | tf_op jit(solution)/shard_map/ppermute | solution.py:24
  95.6 21.6 %copy-start.2 = (bf16[16,1152]{1,0:T(8,128)(2,1)S(1)}, bf16[16,1152]{1,0:T(8,128)(2,1)}, u32[]{:S(2)}) copy-start(bf16[16,1152]{1,0:T(8,128)(2,1)} %raw_ref.1) | copy-start | bytes 110596
  95.6 9.7 %collective-permute-start.5 = (f16[32,1280]{1,0:T(8,128)(2,1)S(1)}, f16[32,1280]{1,0:T(8,128)(2,1)S(1)}, u32[]{:S(2)}, u32[]{:S(2)}) collective-permute-start(f16[32,1280]{1,0:T(8,128)(2,1)S(1)} %get-tuple-element.13), channel_id=1, source_target_pairs={{0,4},{2,6},{4,8},{6,10},{8,12},{10,14},{12,0},{14,2},{1,5},{3,7},... | collective-permute-start | bytes 245768 | tf_op jit(solution)/shard_map/ppermute | solution.py:24
  99.1 7.4 %collective-permute-start.6 = (f16[32,1280]{1,0:T(8,128)(2,1)S(1)}, f16[32,1280]{1,0:T(8,128)(2,1)S(1)}, u32[]{:S(2)}, u32[]{:S(2)}) collective-permute-start(f16[32,1280]{1,0:T(8,128)(2,1)S(1)} %get-tuple-element.14), channel_id=1, source_target_pairs={{0,12},{2,14},{4,0},{6,2},{8,4},{10,6},{12,8},{14,10},{1,13},{3,15... | collective-permute-start | bytes 245768 | tf_op jit(solution)/shard_map/ppermute | solution.py:24
  106.6 6.7 %collective-permute-start.8 = (f16[16,1280]{1,0:T(8,128)(2,1)S(1)}, f16[16,1280]{1,0:T(8,128)(2,1)S(1)}, u32[]{:S(2)}, u32[]{:S(2)}) collective-permute-start(f16[16,1280]{1,0:T(8,128)(2,1)S(1)} %slice_convert_fusion), channel_id=1, source_target_pairs={{0,1},{1,0},{2,3},{3,2},{4,5},{5,4},{6,7},{7,6},{8,9},{9,8},{10,11... | collective-permute-start | bytes 122888 | tf_op jit(solution)/shard_map/ppermute | solution.py:24

commit v9 on v8

--- a/solution.py
+++ b/solution.py
@@ -8,6 +8,7 @@
 FINE = ("yhi", "x", "core", "z", "ylo")
 FINE_SIZES = (4, 8, 2, 8, 2)
 IMAGE_GROUP = ("core", "z", "ylo")
+Z_ORDER = (0, 2, 6, 4, 1, 3, 7, 5)
 TEXT_GROUP = ("yhi", "x")
 SEND_SCALE = 2.0
 LOSS_SCALE = 0.125
@@ -24,10 +25,11 @@
     return lax.ppermute(block, axis, [(i, (i + step) % count) for i in range(count)])
 
 
-def from_own(array, axis):
-    return lax.dynamic_slice_in_dim(
-        jnp.concatenate([array, array]), lax.axis_index(axis), array.shape[0], 0
-    )
+def gather_z(own):
+    two_on, two_back = shift_by(own, "z", -2), shift_by(own, "z", 2)
+    on = shift_by(jnp.concatenate([own, two_on]), "z", -1)
+    back = shift_by(jnp.concatenate([own, two_back]), "z", 1)
+    return jnp.concatenate([own, two_on, two_back, shift_by(own, "z", 4), on, back])
 
 
 def copies_kernel(raw_ref, copies_ref):
@@ -50,16 +52,18 @@
 def pairs_kernel(place_ref, all_ref, pairs_ref):
     group, core, z, ylo = place_ref[0], place_ref[1], place_ref[2], place_ref[3]
     lane = lax.broadcasted_iota(jnp.int32, (1, 128), 1)
-    turn = lax.rem(z, 4) * 32
     for ahead in range(2):
         first = group * 4 + lax.rem(core + ahead, 2) * 2
-        rows = []
-        for late in range(2):
-            row = all_ref[pl.ds(first + lax.rem(z // 4 + late, 2), 1), :]
+        for line in range(2):
+            row = jnp.zeros((1, 128), jnp.int32)
+            for slot, distance in enumerate(Z_ORDER[4 * line : 4 * line + 4]):
+                there = lax.rem(z + distance, 8)
+                held = all_ref[pl.ds(first + there // 4, 1), :]
+                held = pltpu.roll(held, lax.rem(128 + 32 * slot - 32 * lax.rem(there, 4), 128), 1)
+                row = jnp.where(lane // 32 == slot, held, row)
             swapped = jnp.where(lane % 32 < 16, pltpu.roll(row, 112, 1), pltpu.roll(row, 16, 1))
-            rows.append(pltpu.roll(jnp.where(ylo == 0, row, swapped), lax.rem(128 - turn, 128), 1))
-        pairs_ref[2 * ahead : 2 * ahead + 1, :] = jnp.where(lane + turn < 128, rows[0], rows[1])
-        pairs_ref[2 * ahead + 1 : 2 * ahead + 2, :] = jnp.where(lane + turn < 128, rows[1], rows[0])
+            out = 2 * ahead + line
+            pairs_ref[out : out + 1, :] = jnp.where(ylo == 0, row, swapped)
 
 
 def image_pairs(caption_partner_position, image_count):
@@ -103,10 +107,10 @@
     own_rows, width = picture_vectors.shape
     similarity_multiplier = sharpness_factor[0]
     shift = affine_offset_array[0]
-    raw_images = jnp.concatenate([picture_vectors, shift_by(picture_vectors, "ylo", 1)])
+    near_images = jnp.concatenate([picture_vectors, shift_by(picture_vectors, "ylo", 1)])
+    near_images = normalize(near_images).astype(jnp.bfloat16)
     txt_block = gather(caption_vectors, TEXT_GROUP).reshape(-1, width)
-    raw_images = lax.all_gather(raw_images, "z", axis=0, tiled=False)
-    z_images = normalize(from_own(raw_images, "z").reshape(-1, width)).astype(jnp.bfloat16)
+    z_images = gather_z(near_images)
     img_block = jnp.concatenate([z_images, shift_by(z_images, "core", 1)])
     image_count = img_block.shape[0]
     my_pairs = image_pairs(caption_partner_position, image_count)
@@ -134,12 +138,12 @@
         [img_part, jnp.broadcast_to(loss[:, None] * LOSS_SCALE, (image_count, 128))], axis=1
     ).reshape(2, 8, 2 * own_rows, width + 128)
     total = img_part[0] + full(shift_by(half(img_part[1]), "core", 1))
-    far = shift_by(half(total[4]), "z", 4)
-    ahead = full(shift_by(half(jnp.stack([total[1], total[3]])), "z", 1))
-    back = full(shift_by(half(jnp.stack([total[7], total[5]])), "z", -1))
+    far = shift_by(half(total[3]), "z", 4)
+    ahead = full(shift_by(half(total[4:6]), "z", 1))
+    back = full(shift_by(half(total[6:8]), "z", -1))
     near = total[0] + ahead[0] + back[0]
-    near = near + full(shift_by(half(total[2] + ahead[1]), "z", 2))
-    near = near + full(shift_by(half(total[6] + back[1]), "z", -2))
+    near = near + full(shift_by(half(total[1] + ahead[1]), "z", 2))
+    near = near + full(shift_by(half(total[2] + back[1]), "z", -2))
     near = near + full(far)
     total = near[:own_rows] + full(shift_by(half(near[own_rows:]), "ylo", 1))
     loss = total[:, width] / LOSS_SCALE

time: 120 us -> 123 us (1.025)
  blocking collectives: 35 us -> 0 us
  starting transfers between devices: 57.3 us -> 83.3 us
  waiting for transfers between devices: 9.69 us -> 20.2 us
    all_gather x1 -> x0, blocking collectives: 35 us -> none  [per_device(): raw_images = lax.all_gather(raw_images, 'z', axis=0, tiled=False)]
    ppermute x9 -> x14, starting transfers between devices: 29.8 us -> 55.9 us  [shift_by(): lax.ppermute(block, axis, [(i, (i + step) % count) for i in range(count)])]
    ppermute x9 -> x14, waiting for transfers between devices: 6.67 us -> 17.7 us  [shift_by(): lax.ppermute(block, axis, [(i, (i + step) % count) for i in range(count)])]
  transfers between devices with their start and end apart: 11 -> 16, of which waited for: 5 -> 8; matrix products, arithmetic and copies ran while one was open for 5% -> 5% of each run, Pallas kernels for 3% -> 3%
where the time goes in v9:
time: 123 us; the launch traced here: 122 us
  starting transfers between devices  83.3 us (68%)
  waiting for transfers between devices  20.2 us (16%)
  matrix products  5.95 us (5%)
  other arithmetic  4.92 us (4%)
  Pallas kernels  3.63 us (3%)
  between operations  2.31 us (2%)
    ppermute x14, starting transfers between devices, shift_by(): lax.ppermute(block, axis, [(i, (i + step) % count) for i in range(count)])  55.9 us
    ppermute x14, waiting for transfers between devices, shift_by(): lax.ppermute(block, axis, [(i, (i + step) % count) for i in range(count)])  17.7 us
    all_to_all x1, starting transfers between devices, gather(): return lax.all_to_all(copies, axes, 0, 0, tiled=True)  15.2 us
    all_to_all x1, starting transfers between devices, scatter(): lax.all_to_all(parts.reshape(count, parts.shape[0] // count, parts.shape[...  12.2 us
    dot_general x1, matrix products, per_device(): lax.dot_general(img_block, txt_block, (((1,), (1,)), ((), ())), preferred...  2.83 us
    all_to_all x1, waiting for transfers between devices, scatter(): lax.all_to_all(parts.reshape(count, parts.shape[0] // count, parts.shape[...  2.56 us
  transfers between devices with their start and end apart: 16, of which 8 were waited for; matrix products, arithmetic and copies ran while one was open for 5% of the time, Pallas kernels for 3%

profile of v9, /device:TPU:2, one launch (start us, length us, event | category | flops | bytes accessed | tf_op | source)
XLA Modules:
  0.0 121.6 jit_solution(17788581347415679084)
XLA Ops:
  0.6 3.6 %collective-permute-start = (bf16[16,1152]{1,0:T(8,128)(2,1)}, bf16[16,1152]{1,0:T(8,128)(2,1)S(1)}, u32[]{:S(2)}, u32[]{:S(2)}) collective-permute-start(bf16[16,1152]{1,0:T(8,128)(2,1)} %param.5), channel_id=1, source_target_pairs={{0,1},{1,0},{2,3},{3,2},{4,5},{5,4},{6,7},{7,6},{8,9},{9,8},{10,11... | collective-permute-start | bytes 110600 | tf_op jit(solution)/shard_map/ppermute | solution.py:25
  4.2 2.0 %copies.1 = bf16[32,16,1152]{2,1,0:T(8,128)(2,1)} custom-call(bf16[16,1152]{1,0:T(8,128)(2,1)} %raw_ref.1), custom_call_target="tpu_custom_call" | custom-call | tf_op jit(solution)/shard_map/copies/pallas_call | solution.py:42
  6.2 15.2 %all-to-all-start = ((bf16[32,16,1152]{2,1,0:T(8,128)(2,1)}), bf16[32,16,1152]{2,1,0:T(8,128)(2,1)S(1)}, u32[]{:S(2)}, u32[]{:S(2)}) async-start(bf16[32,16,1152]{2,1,0:T(8,128)(2,1)} %copies.1), calls=%async_computation | async-start | bytes 2359296 | tf_op jit(solution)/shard_map/all_to_all | solution.py:49
  21.5 0.6 pad_add_fusion.place_ref
  22.1 0.0 collective-permute-done
  22.1 0.1 fusion.16
  22.2 0.1 constant_dynamic-update-slice_fusion.5
  22.3 11.7 %collective-permute-start.3 = (bf16[32,1152]{1,0:T(8,128)(2,1)S(1)}, bf16[32,1152]{1,0:T(8,128)(2,1)S(1)}, u32[]{:S(2)}, u32[]{:S(2)}) collective-permute-start(bf16[32,1152]{1,0:T(8,128)(2,1)S(1)} %get-tuple-element.10), channel_id=1, source_target_pairs={{0,8},{2,10},{4,12},{6,14},{8,0},{10,2},{12,4},{14,6},{1,9},{3,11}... | collective-permute-start | bytes 221192 | tf_op jit(solution)/shard_map/ppermute | solution.py:25
  34.0 6.1 %collective-permute-start.2 = (bf16[32,1152]{1,0:T(8,128)(2,1)S(1)}, bf16[32,1152]{1,0:T(8,128)(2,1)S(1)}, u32[]{:S(2)}, u32[]{:S(2)}) collective-permute-start(bf16[32,1152]{1,0:T(8,128)(2,1)S(1)} %get-tuple-element.10), channel_id=1, source_target_pairs={{0,4},{2,6},{4,8},{6,10},{8,12},{10,14},{12,0},{14,2},{1,5},{3,7},... | collective-permute-start | bytes 221192 | tf_op jit(solution)/shard_map/ppermute | solution.py:25
  40.2 1.9 %collective-permute-start.1 = (bf16[32,1152]{1,0:T(8,128)(2,1)S(1)}, bf16[32,1152]{1,0:T(8,128)(2,1)S(1)}, u32[]{:S(2)}, u32[]{:S(2)}) collective-permute-start(bf16[32,1152]{1,0:T(8,128)(2,1)S(1)} %get-tuple-element.10), channel_id=1, source_target_pairs={{0,12},{2,14},{4,0},{6,2},{8,4},{10,6},{12,8},{14,10},{1,13},{3,15... | collective-permute-start | bytes 221192 | tf_op jit(solution)/shard_map/ppermute | solution.py:25
  42.1 0.7 collective-permute-done.2
  42.8 4.7 %collective-permute-done.1 = bf16[32,1152]{1,0:T(8,128)(2,1)S(1)} collective-permute-done((bf16[32,1152]{1,0:T(8,128)(2,1)S(1)}, bf16[32,1152]{1,0:T(8,128)(2,1)S(1)}, u32[]{:S(2)}, u32[]{:S(2)}) %collective-permute-start.1) | collective-permute-done | bytes 73760 | tf_op jit(solution)/shard_map/ppermute | solution.py:25
  47.5 4.5 %collective-permute-start.5 = (bf16[64,1152]{1,0:T(8,128)(2,1)S(1)}, bf16[64,1152]{1,0:T(8,128)(2,1)S(1)}, u32[]{:S(2)}, u32[]{:S(2)}) collective-permute-start(bf16[64,1152]{1,0:T(8,128)(2,1)S(1)} %get-tuple-element.27), channel_id=1, source_target_pairs={{0,2},{2,4},{4,6},{6,8},{8,10},{10,12},{12,14},{14,0},{1,3},{3,5},... | collective-permute-start | bytes 442376 | tf_op jit(solution)/shard_map/ppermute | solution.py:25
  52.0 2.6 %collective-permute-start.4 = (bf16[64,1152]{1,0:T(8,128)(2,1)S(1)}, bf16[64,1152]{1,0:T(8,128)(2,1)S(1)}, u32[]{:S(2)}, u32[]{:S(2)}) collective-permute-start(bf16[64,1152]{1,0:T(8,128)(2,1)S(1)} %get-tuple-element.28), channel_id=1, source_target_pairs={{0,14},{2,0},{4,2},{6,4},{8,6},{10,8},{12,10},{14,12},{1,15},{3,1}... | collective-permute-start | bytes 442376 | tf_op jit(solution)/shard_map/ppermute | solution.py:25
  54.6 0.0 collective-permute-done.3
  54.7 4.4 %collective-permute-done.4 = bf16[64,1152]{1,0:T(8,128)(2,1)S(1)} collective-permute-done((bf16[64,1152]{1,0:T(8,128)(2,1)S(1)}, bf16[64,1152]{1,0:T(8,128)(2,1)S(1)}, u32[]{:S(2)}, u32[]{:S(2)}) %collective-permute-start.4) | collective-permute-done | bytes 147488 | tf_op jit(solution)/shard_map/ppermute | solution.py:25
  59.0 0.0 collective-permute-done.5
  59.1 1.9 %collective-permute-start.6 = (bf16[256,1152]{1,0:T(8,128)(2,1)S(1)}, bf16[256,1152]{1,0:T(8,128)(2,1)S(1)}, u32[]{:S(2)}, u32[]{:S(2)}) collective-permute-start(bf16[256,1152]{1,0:T(8,128)(2,1)S(1)} %get-tuple-element.17), channel_id=1, source_target_pairs={{0,16},{16,0},{1,17},{17,1},{2,18},{18,2},{3,19},{19,3},{4,20},{20... | collective-permute-start | bytes 1769480 | tf_op jit(solution)/shard_map/ppermute | solution.py:25
  61.0 1.6 %pairs.1 = s32[4,128]{1,0:T(4,128)} custom-call(s32[4]{0:T(128)} %pad_add_fusion.place_ref, s32[128,128]{1,0:T(8,128)} %bitcast.38), custom_call_target="tpu_custom_call" | custom-call | flops 99999997952 | tf_op jit(solution)/shard_map/pairs/pallas_call | solution.py:71
  64.0 0.0 collective-permute-done.6
  64.0 0.9 constant_dynamic-update-slice_fusion.6
  64.9 2.8 %fusion.9 = (f32[512]{0:T(512)S(1)}, f32[512,512]{0,1:T(8,128)S(1)}) fusion(s32[512]{0:T(512)S(1)} %bitcast.39, s32[512]{0:T(512)S(1)} %fusion.31, f32[]{:T(128)} %bitcast.32, bf16[512,1152]{1,0:T(8,128)(2,1)} %constant_dynamic-update-slice_fusion.6, bf16[512,1152]{1,0:T(8,128)(2,1)S(1)} %bitcast.34, f32[]{:T(128)} %bitcast.31), kind=kOutput, calls=%fused_computation.20 | convolution fusion | flops 607649280 | bytes 3414024 | tf_op jit(solution)/shard_map/dot_general | solution.py:123
  67.7 1.0 convolution_multiply_fusion.1
  68.7 0.1 broadcast_in_dim.6
  68.9 0.2 fusion.3
  69.0 2.5 %collective-permute-start.7 = (f16[8,32,1280]{2,1,0:T(8,128)(2,1)S(1)}, f16[8,32,1280]{2,1,0:T(8,128)(2,1)}, u32[]{:S(2)}, u32[]{:S(2)}) collective-permute-start(f16[8,32,1280]{2,1,0:T(8,128)(2,1)S(1)} %bitcast.37), channel_id=1, source_target_pairs={{0,16},{16,0},{1,17},{17,1},{2,18},{18,2},{3,19},{19,3},{4,20},{20... | collective-permute-start | bytes 1966088 | tf_op jit(solution)/shard_map/ppermute | solution.py:25
  71.6 2.1 %fusion = f16[512,1152]{1,0:T(8,128)(2,1)} fusion(bf16[512,1152]{1,0:T(8,128)(2,1)S(1)} %copy-done.3, f32[512,512]{0,1:T(8,128)S(1)} %get-tuple-element.34, s32[512]{0:T(512)S(1)} %bitcast.41, s32[512]{0:T(512)S(1)} %fusion.31), kind=kOutput, calls=%fused_computation.3 | convolution fusion | flops 606994432 | bytes 3411968 | tf_op jit(solution)/shard_map/dot_general | solution.py:132
  73.7 12.2 %all-to-all-start.1 = ((f16[32,16,1152]{2,1,0:T(8,128)(2,1)}), f16[32,16,1152]{2,1,0:T(8,128)(2,1)S(1)}, u32[]{:S(2)}, u32[]{:S(2)}) async-start(f16[32,16,1152]{2,1,0:T(8,128)(2,1)} %bitcast.36), calls=%async_computation.1 | async-start | bytes 2359296 | tf_op jit(solution)/shard_map/all_to_all | solution.py:87
  85.9 1.3 %fusion.37 = (f16[8,32,1280]{2,1,0:T(8,128)(2,1)S(1)}, f32[8,32,1280]{2,1,0:T(8,128)S(1)}) fusion(f32[8,32,1280]{2,1,0:T(8,128)S(1)} %bitcast.33, f16[8,32,1280]{2,1,0:T(8,128)(2,1)} %collective-permute-done.7), kind=kLoop, calls=%fused_computation.92 | loop fusion | flops 983040 | bytes 3932160 | tf_op jit(solution)/shard_map/convert.3
  87.3 0.1 fusion.39
  87.3 1.9 %collective-permute-start.8 = (f16[2,32,1280]{2,1,0:T(8,128)(2,1)S(1)}, f16[2,32,1280]{2,1,0:T(8,128)(2,1)S(1)}, u32[]{:S(2)}, u32[]{:S(2)}) collective-permute-start(f16[2,32,1280]{2,1,0:T(8,128)(2,1)S(1)} %get-tuple-element.15), channel_id=1, source_target_pairs={{0,2},{2,4},{4,6},{6,8},{8,10},{10,12},{12,14},{14,0},{1,3},{3,5},... | collective-permute-start | bytes 491528 | tf_op jit(solution)/shard_map/ppermute | solution.py:25
  89.2 5.1 %collective-permute-start.9 = (f16[2,32,1280]{2,1,0:T(8,128)(2,1)S(1)}, f16[2,32,1280]{2,1,0:T(8,128)(2,1)S(1)}, u32[]{:S(2)}, u32[]{:S(2)}) collective-permute-start(f16[2,32,1280]{2,1,0:T(8,128)(2,1)S(1)} %get-tuple-element.16), channel_id=1, source_target_pairs={{0,14},{2,0},{4,2},{6,4},{8,6},{10,8},{12,10},{14,12},{1,15},{3,1}... | collective-permute-start | bytes 491528 | tf_op jit(solution)/shard_map/ppermute | solution.py:25
  94.4 2.9 %collective-permute-start.12 = (f16[32,1280]{1,0:T(8,128)(2,1)S(1)}, f16[32,1280]{1,0:T(8,128)(2,1)S(1)}, u32[]{:S(2)}, u32[]{:S(2)}) collective-permute-start(f16[32,1280]{1,0:T(8,128)(2,1)S(1)} %slice_bitcast_fusion), channel_id=1, source_target_pairs={{0,8},{2,10},{4,12},{6,14},{8,0},{10,2},{12,4},{14,6},{1,9},{3,11}... | collective-permute-start | bytes 245768 | tf_op jit(solution)/shard_map/ppermute | solution.py:25
  97.3 0.8 collective-permute-done.9
  98.2 3.0 %collective-permute-start.10 = (f16[32,1280]{1,0:T(8,128)(2,1)S(1)}, f16[32,1280]{1,0:T(8,128)(2,1)S(1)}, u32[]{:S(2)}, u32[]{:S(2)}) collective-permute-start(f16[32,1280]{1,0:T(8,128)(2,1)S(1)} %get-tuple-element.13), channel_id=1, source_target_pairs={{0,4},{2,6},{4,8},{6,10},{8,12},{10,14},{12,0},{14,2},{1,5},{3,7},... | collective-permute-start | bytes 245768 | tf_op jit(solution)/shard_map/ppermute | solution.py:25
  101.2 0.0 copy-start.1
  101.2 5.0 %collective-permute-start.11 = (f16[32,1280]{1,0:T(8,128)(2,1)S(1)}, f16[32,1280]{1,0:T(8,128)(2,1)S(1)}, u32[]{:S(2)}, u32[]{:S(2)}) collective-permute-start(f16[32,1280]{1,0:T(8,128)(2,1)S(1)} %get-tuple-element.14), channel_id=1, source_target_pairs={{0,12},{2,14},{4,0},{6,2},{8,4},{10,6},{12,8},{14,10},{1,13},{3,15... | collective-permute-start | bytes 245768 | tf_op jit(solution)/shard_map/ppermute | solution.py:25
  106.2 1.7 %collective-permute-done.12 = f16[32,1280]{1,0:T(8,128)(2,1)S(1)} collective-permute-done((f16[32,1280]{1,0:T(8,128)(2,1)S(1)}, f16[32,1280]{1,0:T(8,128)(2,1)S(1)}, u32[]{:S(2)}, u32[]{:S(2)}) %collective-permute-start.12) | collective-permute-done | bytes 81952 | tf_op jit(solution)/shard_map/ppermute | solution.py:25
  107.9 2.2 %collective-permute-done.11 = f16[32,1280]{1,0:T(8,128)(2,1)S(1)} collective-permute-done((f16[32,1280]{1,0:T(8,128)(2,1)S(1)}, f16[32,1280]{1,0:T(8,128)(2,1)S(1)}, u32[]{:S(2)}, u32[]{:S(2)}) %collective-permute-start.11) | collective-permute-done | bytes 81952 | tf_op jit(solution)/shard_map/ppermute | solution.py:25
  110.1 0.1 fusion.15
  110.2 3.1 %collective-permute-start.13 = (f16[16,1280]{1,0:T(8,128)(2,1)S(1)}, f16[16,1280]{1,0:T(8,128)(2,1)S(1)}, u32[]{:S(2)}, u32[]{:S(2)}) collective-permute-start(f16[16,1280]{1,0:T(8,128)(2,1)S(1)} %slice_convert_fusion), channel_id=1, source_target_pairs={{0,1},{1,0},{2,3},{3,2},{4,5},{5,4},{6,7},{7,6},{8,9},{9,8},{10,11... | collective-permute-start | bytes 122888 | tf_op jit(solution)/shard_map/ppermute | solution.py:25
  113.3 3.2 %collective-permute-done.13 = f16[16,1280]{1,0:T(8,128)(2,1)S(1)} collective-permute-done((f16[16,1280]{1,0:T(8,128)(2,1)S(1)}, f16[16,1280]{1,0:T(8,128)(2,1)S(1)}, u32[]{:S(2)}, u32[]{:S(2)}) %collective-permute-start.13) | collective-permute-done | bytes 40992 | tf_op jit(solution)/shard_map/ppermute | solution.py:25
  116.6 0.6 fusion.24
  117.2 2.6 %all-to-all-done.1 = f16[32,16,1152]{2,1,0:T(8,128)(2,1)S(1)} async-done(((f16[32,16,1152]{2,1,0:T(8,128)(2,1)}), f16[32,16,1152]{2,1,0:T(8,128)(2,1)S(1)}, u32[]{:S(2)}, u32[]{:S(2)}) %all-to-all-start.1) | async-done | bytes 1179680 | tf_op jit(solution)/shard_map/all_to_all | solution.py:87
  119.7 0.2 convert_reduce_fusion
  119.9 0.2 fusion.20
  120.1 0.7 add_add_fusion.1
  120.8 0.7 add_add_fusion
  (31 shorter events, 0.4 us)
Async XLA Ops:
  0.6 21.4 %collective-permute-start = (bf16[16,1152]{1,0:T(8,128)(2,1)}, bf16[16,1152]{1,0:T(8,128)(2,1)S(1)}, u32[]{:S(2)}, u32[]{:S(2)}) collective-permute-start(bf16[16,1152]{1,0:T(8,128)(2,1)} %param.5), channel_id=1, source_target_pairs={{0,1},{1,0},{2,3},{3,2},{4,5},{5,4},{6,7},{7,6},{8,9},{9,8},{10,11... | collective-permute-start | bytes 110600 | tf_op jit(solution)/shard_map/ppermute | solution.py:25
  6.2 15.9 %copy-start = (bf16[16,1152]{1,0:T(8,128)(2,1)S(1)}, bf16[16,1152]{1,0:T(8,128)(2,1)}, u32[]{:S(2)}) copy-start(bf16[16,1152]{1,0:T(8,128)(2,1)} %param.5) | copy-start | bytes 110596
  6.2 58.7 %all-to-all-start = ((bf16[32,16,1152]{2,1,0:T(8,128)(2,1)}), bf16[32,16,1152]{2,1,0:T(8,128)(2,1)S(1)}, u32[]{:S(2)}, u32[]{:S(2)}) async-start(bf16[32,16,1152]{2,1,0:T(8,128)(2,1)} %copies.1), calls=%async_computation | async-start | bytes 2359296 | tf_op jit(solution)/shard_map/all_to_all | solution.py:49
  22.3 32.3 %collective-permute-start.3 = (bf16[32,1152]{1,0:T(8,128)(2,1)S(1)}, bf16[32,1152]{1,0:T(8,128)(2,1)S(1)}, u32[]{:S(2)}, u32[]{:S(2)}) collective-permute-start(bf16[32,1152]{1,0:T(8,128)(2,1)S(1)} %get-tuple-element.10), channel_id=1, source_target_pairs={{0,8},{2,10},{4,12},{6,14},{8,0},{10,2},{12,4},{14,6},{1,9},{3,11}... | collective-permute-start | bytes 221192 | tf_op jit(solution)/shard_map/ppermute | solution.py:25
  34.0 8.8 %collective-permute-start.2 = (bf16[32,1152]{1,0:T(8,128)(2,1)S(1)}, bf16[32,1152]{1,0:T(8,128)(2,1)S(1)}, u32[]{:S(2)}, u32[]{:S(2)}) collective-permute-start(bf16[32,1152]{1,0:T(8,128)(2,1)S(1)} %get-tuple-element.10), channel_id=1, source_target_pairs={{0,4},{2,6},{4,8},{6,10},{8,12},{10,14},{12,0},{14,2},{1,5},{3,7},... | collective-permute-start | bytes 221192 | tf_op jit(solution)/shard_map/ppermute | solution.py:25
  40.2 7.3 %collective-permute-start.1 = (bf16[32,1152]{1,0:T(8,128)(2,1)S(1)}, bf16[32,1152]{1,0:T(8,128)(2,1)S(1)}, u32[]{:S(2)}, u32[]{:S(2)}) collective-permute-start(bf16[32,1152]{1,0:T(8,128)(2,1)S(1)} %get-tuple-element.10), channel_id=1, source_target_pairs={{0,12},{2,14},{4,0},{6,2},{8,4},{10,6},{12,8},{14,10},{1,13},{3,15... | collective-permute-start | bytes 221192 | tf_op jit(solution)/shard_map/ppermute | solution.py:25
  47.5 11.5 %collective-permute-start.5 = (bf16[64,1152]{1,0:T(8,128)(2,1)S(1)}, bf16[64,1152]{1,0:T(8,128)(2,1)S(1)}, u32[]{:S(2)}, u32[]{:S(2)}) collective-permute-start(bf16[64,1152]{1,0:T(8,128)(2,1)S(1)} %get-tuple-element.27), channel_id=1, source_target_pairs={{0,2},{2,4},{4,6},{6,8},{8,10},{10,12},{12,14},{14,0},{1,3},{3,5},... | collective-permute-start | bytes 442376 | tf_op jit(solution)/shard_map/ppermute | solution.py:25
  52.0 7.0 %collective-permute-start.4 = (bf16[64,1152]{1,0:T(8,128)(2,1)S(1)}, bf16[64,1152]{1,0:T(8,128)(2,1)S(1)}, u32[]{:S(2)}, u32[]{:S(2)}) collective-permute-start(bf16[64,1152]{1,0:T(8,128)(2,1)S(1)} %get-tuple-element.28), channel_id=1, source_target_pairs={{0,14},{2,0},{4,2},{6,4},{8,6},{10,8},{12,10},{14,12},{1,15},{3,1}... | collective-permute-start | bytes 442376 | tf_op jit(solution)/shard_map/ppermute | solution.py:25
  59.1 1.9 %copy-start.2 = (bf16[512,1152]{1,0:T(8,128)(2,1)}, bf16[512,1152]{1,0:T(8,128)(2,1)S(1)}, u32[]{:S(2)}) copy-start(bf16[512,1152]{1,0:T(8,128)(2,1)S(1)} %get-tuple-element.18) | copy-start | bytes 3538948
  59.1 4.9 %collective-permute-start.6 = (bf16[256,1152]{1,0:T(8,128)(2,1)S(1)}, bf16[256,1152]{1,0:T(8,128)(2,1)S(1)}, u32[]{:S(2)}, u32[]{:S(2)}) collective-permute-start(bf16[256,1152]{1,0:T(8,128)(2,1)S(1)} %get-tuple-element.17), channel_id=1, source_target_pairs={{0,16},{16,0},{1,17},{17,1},{2,18},{18,2},{3,19},{19,3},{4,20},{20... | collective-permute-start | bytes 1769480 | tf_op jit(solution)/shard_map/ppermute | solution.py:25
  62.7 2.2 %copy-start.4 = (s32[4,128]{1,0:T(4,128)S(1)}, s32[4,128]{1,0:T(4,128)}, u32[]{:S(2)}) copy-start(s32[4,128]{1,0:T(4,128)} %pairs.1) | copy-start | bytes 6148
  68.9 2.7 %copy-start.3 = (bf16[512,1152]{1,0:T(8,128)(2,1)S(1)}, bf16[512,1152]{1,0:T(8,128)(2,1)}, u32[]{:S(2)}) copy-start(bf16[512,1152]{1,0:T(8,128)(2,1)} %constant_dynamic-update-slice_fusion.6) | copy-start | bytes 3538948
  69.0 16.9 %collective-permute-start.7 = (f16[8,32,1280]{2,1,0:T(8,128)(2,1)S(1)}, f16[8,32,1280]{2,1,0:T(8,128)(2,1)}, u32[]{:S(2)}, u32[]{:S(2)}) collective-permute-start(f16[8,32,1280]{2,1,0:T(8,128)(2,1)S(1)} %bitcast.37), channel_id=1, source_target_pairs={{0,16},{16,0},{1,17},{17,1},{2,18},{18,2},{3,19},{19,3},{4,20},{20... | collective-permute-start | bytes 1966088 | tf_op jit(solution)/shard_map/ppermute | solution.py:25
  73.7 46.0 %all-to-all-start.1 = ((f16[32,16,1152]{2,1,0:T(8,128)(2,1)}), f16[32,16,1152]{2,1,0:T(8,128)(2,1)S(1)}, u32[]{:S(2)}, u32[]{:S(2)}) async-start(f16[32,16,1152]{2,1,0:T(8,128)(2,1)} %bitcast.36), calls=%async_computation.1 | async-start | bytes 2359296 | tf_op jit(solution)/shard_map/all_to_all | solution.py:87
  87.3 10.0 %collective-permute-start.8 = (f16[2,32,1280]{2,1,0:T(8,128)(2,1)S(1)}, f16[2,32,1280]{2,1,0:T(8,128)(2,1)S(1)}, u32[]{:S(2)}, u32[]{:S(2)}) collective-permute-start(f16[2,32,1280]{2,1,0:T(8,128)(2,1)S(1)} %get-tuple-element.15), channel_id=1, source_target_pairs={{0,2},{2,4},{4,6},{6,8},{8,10},{10,12},{12,14},{14,0},{1,3},{3,5},... | collective-permute-start | bytes 491528 | tf_op jit(solution)/shard_map/ppermute | solution.py:25
  89.2 8.9 %collective-permute-start.9 = (f16[2,32,1280]{2,1,0:T(8,128)(2,1)S(1)}, f16[2,32,1280]{2,1,0:T(8,128)(2,1)S(1)}, u32[]{:S(2)}, u32[]{:S(2)}) collective-permute-start(f16[2,32,1280]{2,1,0:T(8,128)(2,1)S(1)} %get-tuple-element.16), channel_id=1, source_target_pairs={{0,14},{2,0},{4,2},{6,4},{8,6},{10,8},{12,10},{14,12},{1,15},{3,1}... | collective-permute-start | bytes 491528 | tf_op jit(solution)/shard_map/ppermute | solution.py:25
  94.4 13.5 %collective-permute-start.12 = (f16[32,1280]{1,0:T(8,128)(2,1)S(1)}, f16[32,1280]{1,0:T(8,128)(2,1)S(1)}, u32[]{:S(2)}, u32[]{:S(2)}) collective-permute-start(f16[32,1280]{1,0:T(8,128)(2,1)S(1)} %slice_bitcast_fusion), channel_id=1, source_target_pairs={{0,8},{2,10},{4,12},{6,14},{8,0},{10,2},{12,4},{14,6},{1,9},{3,11}... | collective-permute-start | bytes 245768 | tf_op jit(solution)/shard_map/ppermute | solution.py:25
  98.2 9.7 %collective-permute-start.10 = (f16[32,1280]{1,0:T(8,128)(2,1)S(1)}, f16[32,1280]{1,0:T(8,128)(2,1)S(1)}, u32[]{:S(2)}, u32[]{:S(2)}) collective-permute-start(f16[32,1280]{1,0:T(8,128)(2,1)S(1)} %get-tuple-element.13), channel_id=1, source_target_pairs={{0,4},{2,6},{4,8},{6,10},{8,12},{10,14},{12,0},{14,2},{1,5},{3,7},... | collective-permute-start | bytes 245768 | tf_op jit(solution)/shard_map/ppermute | solution.py:25
  101.2 18.7 %copy-start.1 = (bf16[16,1152]{1,0:T(8,128)(2,1)S(1)}, bf16[16,1152]{1,0:T(8,128)(2,1)}, u32[]{:S(2)}) copy-start(bf16[16,1152]{1,0:T(8,128)(2,1)} %raw_ref.1) | copy-start | bytes 110596
  101.2 8.9 %collective-permute-start.11 = (f16[32,1280]{1,0:T(8,128)(2,1)S(1)}, f16[32,1280]{1,0:T(8,128)(2,1)S(1)}, u32[]{:S(2)}, u32[]{:S(2)}) collective-permute-start(f16[32,1280]{1,0:T(8,128)(2,1)S(1)} %get-tuple-element.14), channel_id=1, source_target_pairs={{0,12},{2,14},{4,0},{6,2},{8,4},{10,6},{12,8},{14,10},{1,13},{3,15... | collective-permute-start | bytes 245768 | tf_op jit(solution)/shard_map/ppermute | solution.py:25
  110.2 6.4 %collective-permute-start.13 = (f16[16,1280]{1,0:T(8,128)(2,1)S(1)}, f16[16,1280]{1,0:T(8,128)(2,1)S(1)}, u32[]{:S(2)}, u32[]{:S(2)}) collective-permute-start(f16[16,1280]{1,0:T(8,128)(2,1)S(1)} %slice_convert_fusion), channel_id=1, source_target_pairs={{0,1},{1,0},{2,3},{3,2},{4,5},{5,4},{6,7},{7,6},{8,9},{9,8},{10,11... | collective-permute-start | bytes 122888 | tf_op jit(solution)/shard_map/ppermute | solution.py:25

commit v10 on v8

--- a/solution.py
+++ b/solution.py
@@ -12,6 +12,7 @@
 SEND_SCALE = 2.0
 LOSS_SCALE = 0.125
 WAIT_FLOPS = 100_000_000_000
+KERNEL_BYTES = 4 * 1024 * 1024
 
 
 def normalize(raw):
@@ -42,13 +43,15 @@
         out_shape=jax.ShapeDtypeStruct((lax.axis_size(axes),) + raw.shape, jnp.bfloat16),
         in_specs=[pl.BlockSpec(memory_space=pltpu.VMEM)],
         out_specs=pl.BlockSpec(memory_space=pltpu.VMEM),
+        compiler_params=pltpu.CompilerParams(vmem_limit_bytes=KERNEL_BYTES),
         name="copies",
     )(raw)
     return lax.all_to_all(copies, axes, 0, 0, tiled=True)
 
 
-def pairs_kernel(place_ref, all_ref, pairs_ref):
-    group, core, z, ylo = place_ref[0], place_ref[1], place_ref[2], place_ref[3]
+def pairs_kernel(all_ref, pairs_ref):
+    group = lax.axis_index(TEXT_GROUP)
+    core, z, ylo = [lax.axis_index(axis) for axis in IMAGE_GROUP]
     lane = lax.broadcasted_iota(jnp.int32, (1, 128), 1)
     turn = lax.rem(z, 4) * 32
     for ahead in range(2):
@@ -63,18 +66,15 @@
 
 
 def image_pairs(caption_partner_position, image_count):
-    place = jnp.stack([lax.axis_index(axes) for axes in (TEXT_GROUP,) + IMAGE_GROUP]).astype(jnp.int32)
     pairs = pl.pallas_call(
         pairs_kernel,
         out_shape=jax.ShapeDtypeStruct((image_count // 128, 128), jnp.int32),
-        in_specs=[
-            pl.BlockSpec(memory_space=pltpu.SMEM),
-            pl.BlockSpec(memory_space=pltpu.VMEM),
-        ],
+        in_specs=[pl.BlockSpec(memory_space=pltpu.VMEM)],
         out_specs=pl.BlockSpec(memory_space=pltpu.VMEM),
         cost_estimate=pl.CostEstimate(flops=WAIT_FLOPS, bytes_accessed=0, transcendentals=0),
+        compiler_params=pltpu.CompilerParams(vmem_limit_bytes=KERNEL_BYTES),
         name="pairs",
-    )(place, caption_partner_position.reshape(-1, 128))
+    )(caption_partner_position.reshape(-1, 128))
     return pairs.reshape(-1)
 
 
@@ -103,10 +103,10 @@
     own_rows, width = picture_vectors.shape
     similarity_multiplier = sharpness_factor[0]
     shift = affine_offset_array[0]
-    raw_images = jnp.concatenate([picture_vectors, shift_by(picture_vectors, "ylo", 1)])
+    near_images = jnp.concatenate([picture_vectors, shift_by(picture_vectors, "ylo", 1)])
+    near_images = normalize(near_images).astype(jnp.bfloat16)
     txt_block = gather(caption_vectors, TEXT_GROUP).reshape(-1, width)
-    raw_images = lax.all_gather(raw_images, "z", axis=0, tiled=False)
-    z_images = normalize(from_own(raw_images, "z").reshape(-1, width)).astype(jnp.bfloat16)
+    z_images = from_own(lax.all_gather(near_images, "z", axis=0, tiled=False), "z").reshape(-1, width)
     img_block = jnp.concatenate([z_images, shift_by(z_images, "core", 1)])
     image_count = img_block.shape[0]
     my_pairs = image_pairs(caption_partner_position, image_count)

time: 120 us -> 117 us (0.975)
  Pallas kernels: 3.55 us -> 1.36 us
    ppermute x9, waiting for transfers between devices: 6.67 us -> 8.34 us  [shift_by(): lax.ppermute(block, axis, [(i, (i + step) % count) for i in range(count)])]
    pallas_call x1, Pallas kernels: 1.59 us -> 0.17 us  [image_pairs(): pl.pallas_call(pairs_kernel, out_shape=jax.ShapeDtypeStruct((image_count...]
  transfers between devices with their start and end apart: 11 -> 11, of which waited for: 5 -> 6; matrix products, arithmetic and copies ran while one was open for 5% -> 4% of each run, Pallas kernels for 3% -> 1%
where the time goes in v10:
time: 117 us; the launch traced here: 116 us
  starting transfers between devices  56.9 us (49%)
  blocking collectives  35.1 us (30%)
  waiting for transfers between devices  10.6 us (9%)
  matrix products  4.65 us (4%)
  other arithmetic  4.58 us (4%)
  between operations  2.28 us (2%)
  Pallas kernels  1.36 us (1%)
    all_gather x1, blocking collectives, per_device(): lax.all_gather(near_images, 'z', axis=0, tiled=False)  35.1 us
    ppermute x9, starting transfers between devices, shift_by(): lax.ppermute(block, axis, [(i, (i + step) % count) for i in range(count)])  29.5 us
    all_to_all x1, starting transfers between devices, gather(): return lax.all_to_all(copies, axes, 0, 0, tiled=True)  15.2 us
    all_to_all x1, starting transfers between devices, scatter(): lax.all_to_all(parts.reshape(count, parts.shape[0] // count, parts.shape[...  12.2 us
    ppermute x9, waiting for transfers between devices, shift_by(): lax.ppermute(block, axis, [(i, (i + step) % count) for i in range(count)])  8.34 us
  transfers between devices with their start and end apart: 11, of which 6 were waited for; matrix products, arithmetic and copies ran while one was open for 4% of the time, Pallas kernels for 1%

profile of v10, /device:TPU:2, one launch (start us, length us, event | category | flops | bytes accessed | tf_op | source)
XLA Modules:
  0.0 116.5 jit_solution(7126398093683225498)
XLA Ops:
  0.6 3.6 %collective-permute-start = (bf16[16,1152]{1,0:T(8,128)(2,1)}, bf16[16,1152]{1,0:T(8,128)(2,1)S(1)}, u32[]{:S(2)}, u32[]{:S(2)}) collective-permute-start(bf16[16,1152]{1,0:T(8,128)(2,1)} %param.5), channel_id=1, source_target_pairs={{0,1},{1,0},{2,3},{3,2},{4,5},{5,4},{6,7},{7,6},{8,9},{9,8},{10,11... | collective-permute-start | bytes 110600 | tf_op jit(solution)/shard_map/ppermute | solution.py:25
  4.2 0.0 copy-start
  4.2 0.8 copy-done
  5.0 1.2 %copies.1 = bf16[32,16,1152]{2,1,0:T(8,128)(2,1)} custom-call(bf16[16,1152]{1,0:T(8,128)(2,1)S(1)} %copy-done), custom_call_target="tpu_custom_call" | custom-call | tf_op jit(solution)/shard_map/copies/pallas_call | solution.py:41
  6.2 15.2 %all-to-all-start = ((bf16[32,16,1152]{2,1,0:T(8,128)(2,1)}), bf16[32,16,1152]{2,1,0:T(8,128)(2,1)S(1)}, u32[]{:S(2)}, u32[]{:S(2)}) async-start(bf16[32,16,1152]{2,1,0:T(8,128)(2,1)} %copies.1), calls=%async_computation | async-start | bytes 2359296 | tf_op jit(solution)/shard_map/all_to_all | solution.py:49
  21.4 0.0 copy-start.2
  21.5 0.0 collective-permute-done
  21.5 0.1 multiply_reduce_fusion
  21.6 0.1 multiply_convert_fusion
  21.7 35.1 %all_gather.4 = bf16[8,32,1152]{2,1,0:T(8,128)(2,1)S(1)} all-gather(bf16[1,32,1152]{2,1,0:T(8,128)(2,1)S(1)} %multiply_convert_fusion), channel_id=1, replica_groups=mesh['yhi'=4,'x'=8,'core'=2,'z'=8,'ylo'=2] {'z'}, dimensions={0}, use_global_device_ids=true | all-gather | bytes 663552 | tf_op jit(solution)/shard_map/all_gather | solution.py:109
  56.8 0.2 fusion.10
  57.0 0.0 copy-start.3
  57.1 1.9 %collective-permute-start.1 = (bf16[256,1152]{1,0:T(8,128)(2,1)S(1)}, bf16[256,1152]{1,0:T(8,128)(2,1)S(1)}, u32[]{:S(2)}, u32[]{:S(2)}) collective-permute-start(bf16[256,1152]{1,0:T(8,128)(2,1)S(1)} %bitcast.39), channel_id=1, source_target_pairs={{0,16},{16,0},{1,17},{17,1},{2,18},{18,2},{3,19},{19,3},{4,20},{20... | collective-permute-start | bytes 1769480 | tf_op jit(solution)/shard_map/ppermute | solution.py:25
  59.0 0.0 copy-done.2
  59.0 0.2 pairs.1
  60.5 0.5 collective-permute-done.1
  61.0 0.0 all-to-all-done
  61.0 0.0 copy-done.3
  61.0 1.6 %fusion.9 = (f32[512]{0:T(512)S(1)}, f32[512,512]{0,1:T(8,128)S(1)}) fusion(s32[512]{0:T(512)S(1)} %bitcast.31, s32[512]{0:T(512)S(1)} %fusion.30, f32[]{:T(128)} %bitcast.29, bf16[512,1152]{1,0:T(8,128)(2,1)S(1)} %bitcast.36, bf16[256,1152]{1,0:T(8,128)(2,1)S(1)} %collective-permute-done.1, bf16[256,1152]{1,0:T(8,128)(2,1)S(1)} %bitcast.40, f32[]{:T(128)} %bitcast.28), kind=kOutput, calls=%fused_computation.23 | convolution fusion | flops 610008576 | bytes 3414024 | tf_op jit(solution)/shard_map/dot_general | solution.py:119
  62.5 1.0 convolution_multiply_fusion.1
  63.6 0.1 broadcast_in_dim.6
  63.7 0.2 fusion.3
  63.9 2.2 %collective-permute-start.2 = (f16[8,32,1280]{2,1,0:T(8,128)(2,1)S(1)}, f16[8,32,1280]{2,1,0:T(8,128)(2,1)}, u32[]{:S(2)}, u32[]{:S(2)}) collective-permute-start(f16[8,32,1280]{2,1,0:T(8,128)(2,1)S(1)} %bitcast.38), channel_id=1, source_target_pairs={{0,16},{16,0},{1,17},{17,1},{2,18},{18,2},{3,19},{19,3},{4,20},{20... | collective-permute-start | bytes 1966088 | tf_op jit(solution)/shard_map/ppermute | solution.py:25
  66.1 2.1 %fusion = f16[512,1152]{1,0:T(8,128)(2,1)} fusion(bf16[256,1152]{1,0:T(8,128)(2,1)S(1)} %copy-done.7, bf16[256,1152]{1,0:T(8,128)(2,1)S(1)} %bitcast.41, f32[512,512]{0,1:T(8,128)S(1)} %get-tuple-element.23, s32[512]{0:T(512)S(1)} %bitcast.33, s32[512]{0:T(512)S(1)} %fusion.30), kind=kOutput, calls=%fused_computation.3 | convolution fusion | flops 609353728 | bytes 3411968 | tf_op jit(solution)/shard_map/dot_general | solution.py:128
  68.2 12.2 %all-to-all-start.1 = ((f16[32,16,1152]{2,1,0:T(8,128)(2,1)}), f16[32,16,1152]{2,1,0:T(8,128)(2,1)S(1)}, u32[]{:S(2)}, u32[]{:S(2)}) async-start(f16[32,16,1152]{2,1,0:T(8,128)(2,1)} %bitcast.35), calls=%async_computation.1 | async-start | bytes 2359296 | tf_op jit(solution)/shard_map/all_to_all | solution.py:83
  80.4 0.0 collective-permute-done.2
  80.4 1.3 %fusion.38 = (f16[8,32,1280]{2,1,0:T(8,128)(2,1)S(1)}, f32[8,32,1280]{2,1,0:T(8,128)S(1)}) fusion(f32[8,32,1280]{2,1,0:T(8,128)S(1)} %bitcast.34, f16[8,32,1280]{2,1,0:T(8,128)(2,1)} %collective-permute-done.2), kind=kLoop, calls=%fused_computation.81 | loop fusion | flops 983040 | bytes 3932160 | tf_op jit(solution)/shard_map/convert.9
  81.6 0.1 slice_bitcast_fusion
  81.8 3.5 %collective-permute-start.3 = (f16[2,32,1280]{2,1,0:T(8,128)(2,1)S(1)}, f16[2,32,1280]{2,1,0:T(8,128)(2,1)S(1)}, u32[]{:S(2)}, u32[]{:S(2)}) collective-permute-start(f16[2,32,1280]{2,1,0:T(8,128)(2,1)S(1)} %pad_maximum_fusion.4), channel_id=1, source_target_pairs={{0,2},{2,4},{4,6},{6,8},{8,10},{10,12},{12,14},{14,0},{1,3},{3,5},... | collective-permute-start | bytes 491528 | tf_op jit(solution)/shard_map/ppermute | solution.py:25
  85.3 3.5 %collective-permute-start.4 = (f16[2,32,1280]{2,1,0:T(8,128)(2,1)S(1)}, f16[2,32,1280]{2,1,0:T(8,128)(2,1)S(1)}, u32[]{:S(2)}, u32[]{:S(2)}) collective-permute-start(f16[2,32,1280]{2,1,0:T(8,128)(2,1)S(1)} %pad_maximum_fusion.5), channel_id=1, source_target_pairs={{0,14},{2,0},{4,2},{6,4},{8,6},{10,8},{12,10},{14,12},{1,15},{3,1}... | collective-permute-start | bytes 491528 | tf_op jit(solution)/shard_map/ppermute | solution.py:25
  88.9 3.7 %collective-permute-start.7 = (f16[32,1280]{1,0:T(8,128)(2,1)S(1)}, f16[32,1280]{1,0:T(8,128)(2,1)S(1)}, u32[]{:S(2)}, u32[]{:S(2)}) collective-permute-start(f16[32,1280]{1,0:T(8,128)(2,1)S(1)} %get-tuple-element.13), channel_id=1, source_target_pairs={{0,8},{2,10},{4,12},{6,14},{8,0},{10,2},{12,4},{14,6},{1,9},{3,11}... | collective-permute-start | bytes 245768 | tf_op jit(solution)/shard_map/ppermute | solution.py:25
  92.6 0.0 collective-permute-done.3
  92.7 0.2 collective-permute-done.4
  92.9 0.0 copy-start.1
  92.9 3.3 %collective-permute-start.5 = (f16[32,1280]{1,0:T(8,128)(2,1)S(1)}, f16[32,1280]{1,0:T(8,128)(2,1)S(1)}, u32[]{:S(2)}, u32[]{:S(2)}) collective-permute-start(f16[32,1280]{1,0:T(8,128)(2,1)S(1)} %get-tuple-element.11), channel_id=1, source_target_pairs={{0,4},{2,6},{4,8},{6,10},{8,12},{10,14},{12,0},{14,2},{1,5},{3,7},... | collective-permute-start | bytes 245768 | tf_op jit(solution)/shard_map/ppermute | solution.py:25
  96.3 4.6 %collective-permute-start.6 = (f16[32,1280]{1,0:T(8,128)(2,1)S(1)}, f16[32,1280]{1,0:T(8,128)(2,1)S(1)}, u32[]{:S(2)}, u32[]{:S(2)}) collective-permute-start(f16[32,1280]{1,0:T(8,128)(2,1)S(1)} %get-tuple-element.12), channel_id=1, source_target_pairs={{0,12},{2,14},{4,0},{6,2},{8,4},{10,6},{12,8},{14,10},{1,13},{3,15... | collective-permute-start | bytes 245768 | tf_op jit(solution)/shard_map/ppermute | solution.py:25
  100.9 0.0 collective-permute-done.7
  100.9 1.4 %collective-permute-done.5 = f16[32,1280]{1,0:T(8,128)(2,1)S(1)} collective-permute-done((f16[32,1280]{1,0:T(8,128)(2,1)S(1)}, f16[32,1280]{1,0:T(8,128)(2,1)S(1)}, u32[]{:S(2)}, u32[]{:S(2)}) %collective-permute-start.5) | collective-permute-done | bytes 81952 | tf_op jit(solution)/shard_map/ppermute | solution.py:25
  102.3 1.4 %collective-permute-done.6 = f16[32,1280]{1,0:T(8,128)(2,1)S(1)} collective-permute-done((f16[32,1280]{1,0:T(8,128)(2,1)S(1)}, f16[32,1280]{1,0:T(8,128)(2,1)S(1)}, u32[]{:S(2)}, u32[]{:S(2)}) %collective-permute-start.6) | collective-permute-done | bytes 81952 | tf_op jit(solution)/shard_map/ppermute | solution.py:25
  103.7 0.1 fusion.16
  103.8 3.1 %collective-permute-start.8 = (f16[16,1280]{1,0:T(8,128)(2,1)S(1)}, f16[16,1280]{1,0:T(8,128)(2,1)S(1)}, u32[]{:S(2)}, u32[]{:S(2)}) collective-permute-start(f16[16,1280]{1,0:T(8,128)(2,1)S(1)} %slice_convert_fusion), channel_id=1, source_target_pairs={{0,1},{1,0},{2,3},{3,2},{4,5},{5,4},{6,7},{7,6},{8,9},{9,8},{10,11... | collective-permute-start | bytes 122888 | tf_op jit(solution)/shard_map/ppermute | solution.py:25
  106.9 4.9 %collective-permute-done.8 = f16[16,1280]{1,0:T(8,128)(2,1)S(1)} collective-permute-done((f16[16,1280]{1,0:T(8,128)(2,1)S(1)}, f16[16,1280]{1,0:T(8,128)(2,1)S(1)}, u32[]{:S(2)}, u32[]{:S(2)}) %collective-permute-start.8) | collective-permute-done | bytes 40992 | tf_op jit(solution)/shard_map/ppermute | solution.py:25
  111.8 0.6 fusion.23
  112.4 2.2 %all-to-all-done.1 = f16[32,16,1152]{2,1,0:T(8,128)(2,1)S(1)} async-done(((f16[32,16,1152]{2,1,0:T(8,128)(2,1)}), f16[32,16,1152]{2,1,0:T(8,128)(2,1)S(1)}, u32[]{:S(2)}, u32[]{:S(2)}) %all-to-all-start.1) | async-done | bytes 1179680 | tf_op jit(solution)/shard_map/all_to_all | solution.py:83
  114.6 0.2 convert_reduce_fusion
  114.8 0.2 fusion.19
  115.0 0.7 add_add_fusion.1
  115.7 0.7 add_add_fusion
  (21 shorter events, 0.3 us)
Async XLA Ops:
  0.6 20.8 %collective-permute-start = (bf16[16,1152]{1,0:T(8,128)(2,1)}, bf16[16,1152]{1,0:T(8,128)(2,1)S(1)}, u32[]{:S(2)}, u32[]{:S(2)}) collective-permute-start(bf16[16,1152]{1,0:T(8,128)(2,1)} %param.5), channel_id=1, source_target_pairs={{0,1},{1,0},{2,3},{3,2},{4,5},{5,4},{6,7},{7,6},{8,9},{9,8},{10,11... | collective-permute-start | bytes 110600 | tf_op jit(solution)/shard_map/ppermute | solution.py:25
  4.2 0.8 copy-start
  6.2 15.3 %copy-start.5 = (bf16[16,1152]{1,0:T(8,128)(2,1)S(1)}, bf16[16,1152]{1,0:T(8,128)(2,1)}, u32[]{:S(2)}) copy-start(bf16[16,1152]{1,0:T(8,128)(2,1)} %param.5) | copy-start | bytes 110596
  6.2 54.8 %all-to-all-start = ((bf16[32,16,1152]{2,1,0:T(8,128)(2,1)}), bf16[32,16,1152]{2,1,0:T(8,128)(2,1)S(1)}, u32[]{:S(2)}, u32[]{:S(2)}) async-start(bf16[32,16,1152]{2,1,0:T(8,128)(2,1)} %copies.1), calls=%async_computation | async-start | bytes 2359296 | tf_op jit(solution)/shard_map/all_to_all | solution.py:49
  21.4 37.5 %copy-start.2 = (s32[16384]{0:T(1024)S(1)}, s32[16384]{0:T(1024)}, u32[]{:S(2)}) copy-start(s32[16384]{0:T(1024)} %param.7) | copy-start | bytes 196612
  57.0 3.9 %copy-start.3 = (bf16[8,32,1152]{2,1,0:T(8,128)(2,1)}, bf16[8,32,1152]{2,1,0:T(8,128)(2,1)S(1)}, u32[]{:S(2)}) copy-start(bf16[8,32,1152]{2,1,0:T(8,128)(2,1)S(1)} %fusion.10) | copy-start | bytes 1769476
  57.1 3.9 %collective-permute-start.1 = (bf16[256,1152]{1,0:T(8,128)(2,1)S(1)}, bf16[256,1152]{1,0:T(8,128)(2,1)S(1)}, u32[]{:S(2)}, u32[]{:S(2)}) collective-permute-start(bf16[256,1152]{1,0:T(8,128)(2,1)S(1)} %bitcast.39), channel_id=1, source_target_pairs={{0,16},{16,0},{1,17},{17,1},{2,18},{18,2},{3,19},{19,3},{4,20},{20... | collective-permute-start | bytes 1769480 | tf_op jit(solution)/shard_map/ppermute | solution.py:25
  61.0 1.6 %copy-start.6 = (bf16[256,1152]{1,0:T(8,128)(2,1)}, bf16[256,1152]{1,0:T(8,128)(2,1)S(1)}, u32[]{:S(2)}) copy-start(bf16[256,1152]{1,0:T(8,128)(2,1)S(1)} %collective-permute-done.1) | copy-start | bytes 1769476
  63.7 2.4 %copy-start.4 = (bf16[8,32,1152]{2,1,0:T(8,128)(2,1)S(1)}, bf16[8,32,1152]{2,1,0:T(8,128)(2,1)}, u32[]{:S(2)}) copy-start(bf16[8,32,1152]{2,1,0:T(8,128)(2,1)} %copy-done.3) | copy-start | bytes 1769476
  63.7 2.4 %copy-start.7 = (bf16[256,1152]{1,0:T(8,128)(2,1)S(1)}, bf16[256,1152]{1,0:T(8,128)(2,1)}, u32[]{:S(2)}) copy-start(bf16[256,1152]{1,0:T(8,128)(2,1)} %copy-done.6) | copy-start | bytes 1769476
  63.9 16.5 %collective-permute-start.2 = (f16[8,32,1280]{2,1,0:T(8,128)(2,1)S(1)}, f16[8,32,1280]{2,1,0:T(8,128)(2,1)}, u32[]{:S(2)}, u32[]{:S(2)}) collective-permute-start(f16[8,32,1280]{2,1,0:T(8,128)(2,1)S(1)} %bitcast.38), channel_id=1, source_target_pairs={{0,16},{16,0},{1,17},{17,1},{2,18},{18,2},{3,19},{19,3},{4,20},{20... | collective-permute-start | bytes 1966088 | tf_op jit(solution)/shard_map/ppermute | solution.py:25
  68.2 46.5 %all-to-all-start.1 = ((f16[32,16,1152]{2,1,0:T(8,128)(2,1)}), f16[32,16,1152]{2,1,0:T(8,128)(2,1)S(1)}, u32[]{:S(2)}, u32[]{:S(2)}) async-start(f16[32,16,1152]{2,1,0:T(8,128)(2,1)} %bitcast.35), calls=%async_computation.1 | async-start | bytes 2359296 | tf_op jit(solution)/shard_map/all_to_all | solution.py:83
  81.8 10.9 %collective-permute-start.3 = (f16[2,32,1280]{2,1,0:T(8,128)(2,1)S(1)}, f16[2,32,1280]{2,1,0:T(8,128)(2,1)S(1)}, u32[]{:S(2)}, u32[]{:S(2)}) collective-permute-start(f16[2,32,1280]{2,1,0:T(8,128)(2,1)S(1)} %pad_maximum_fusion.4), channel_id=1, source_target_pairs={{0,2},{2,4},{4,6},{6,8},{8,10},{10,12},{12,14},{14,0},{1,3},{3,5},... | collective-permute-start | bytes 491528 | tf_op jit(solution)/shard_map/ppermute | solution.py:25
  85.3 7.5 %collective-permute-start.4 = (f16[2,32,1280]{2,1,0:T(8,128)(2,1)S(1)}, f16[2,32,1280]{2,1,0:T(8,128)(2,1)S(1)}, u32[]{:S(2)}, u32[]{:S(2)}) collective-permute-start(f16[2,32,1280]{2,1,0:T(8,128)(2,1)S(1)} %pad_maximum_fusion.5), channel_id=1, source_target_pairs={{0,14},{2,0},{4,2},{6,4},{8,6},{10,8},{12,10},{14,12},{1,15},{3,1}... | collective-permute-start | bytes 491528 | tf_op jit(solution)/shard_map/ppermute | solution.py:25
  88.9 12.0 %collective-permute-start.7 = (f16[32,1280]{1,0:T(8,128)(2,1)S(1)}, f16[32,1280]{1,0:T(8,128)(2,1)S(1)}, u32[]{:S(2)}, u32[]{:S(2)}) collective-permute-start(f16[32,1280]{1,0:T(8,128)(2,1)S(1)} %get-tuple-element.13), channel_id=1, source_target_pairs={{0,8},{2,10},{4,12},{6,14},{8,0},{10,2},{12,4},{14,6},{1,9},{3,11}... | collective-permute-start | bytes 245768 | tf_op jit(solution)/shard_map/ppermute | solution.py:25
  92.9 21.9 %copy-start.1 = (bf16[16,1152]{1,0:T(8,128)(2,1)S(1)}, bf16[16,1152]{1,0:T(8,128)(2,1)}, u32[]{:S(2)}) copy-start(bf16[16,1152]{1,0:T(8,128)(2,1)} %raw_ref.1) | copy-start | bytes 110596
  92.9 9.4 %collective-permute-start.5 = (f16[32,1280]{1,0:T(8,128)(2,1)S(1)}, f16[32,1280]{1,0:T(8,128)(2,1)S(1)}, u32[]{:S(2)}, u32[]{:S(2)}) collective-permute-start(f16[32,1280]{1,0:T(8,128)(2,1)S(1)} %get-tuple-element.11), channel_id=1, source_target_pairs={{0,4},{2,6},{4,8},{6,10},{8,12},{10,14},{12,0},{14,2},{1,5},{3,7},... | collective-permute-start | bytes 245768 | tf_op jit(solution)/shard_map/ppermute | solution.py:25
  96.3 7.5 %collective-permute-start.6 = (f16[32,1280]{1,0:T(8,128)(2,1)S(1)}, f16[32,1280]{1,0:T(8,128)(2,1)S(1)}, u32[]{:S(2)}, u32[]{:S(2)}) collective-permute-start(f16[32,1280]{1,0:T(8,128)(2,1)S(1)} %get-tuple-element.12), channel_id=1, source_target_pairs={{0,12},{2,14},{4,0},{6,2},{8,4},{10,6},{12,8},{14,10},{1,13},{3,15... | collective-permute-start | bytes 245768 | tf_op jit(solution)/shard_map/ppermute | solution.py:25
  103.8 7.9 %collective-permute-start.8 = (f16[16,1280]{1,0:T(8,128)(2,1)S(1)}, f16[16,1280]{1,0:T(8,128)(2,1)S(1)}, u32[]{:S(2)}, u32[]{:S(2)}) collective-permute-start(f16[16,1280]{1,0:T(8,128)(2,1)S(1)} %slice_convert_fusion), channel_id=1, source_target_pairs={{0,1},{1,0},{2,3},{3,2},{4,5},{5,4},{6,7},{7,6},{8,9},{9,8},{10,11... | collective-permute-start | bytes 122888 | tf_op jit(solution)/shard_map/ppermute | solution.py:25

commit v11 on v10

--- a/solution.py
+++ b/solution.py
@@ -129,11 +129,16 @@
         slope, img_block, (((0,), (0,)), ((), ())), preferred_element_type=jnp.float32
     )
     txt_terms = scatter(half(SEND_SCALE * txt_part), TEXT_GROUP)
-    img_part = SEND_SCALE * jnp.dot(slope, txt_block, preferred_element_type=jnp.float32)
-    img_part = jnp.concatenate(
-        [img_part, jnp.broadcast_to(loss[:, None] * LOSS_SCALE, (image_count, 128))], axis=1
-    ).reshape(2, 8, 2 * own_rows, width + 128)
-    total = img_part[0] + full(shift_by(half(img_part[1]), "core", 1))
+    half_count = image_count // 2
+
+    def image_part(rows):
+        terms = SEND_SCALE * jnp.dot(slope[rows], txt_block, preferred_element_type=jnp.float32)
+        losses = jnp.broadcast_to(loss[rows, None] * LOSS_SCALE, (half_count, 128))
+        return jnp.concatenate([terms, losses], axis=1)
+
+    came = shift_by(half(image_part(slice(half_count, image_count))), "core", 1)
+    total = image_part(slice(0, half_count)) + full(came)
+    total = total.reshape(8, 2 * own_rows, width + 128)
     far = shift_by(half(total[4]), "z", 4)
     ahead = full(shift_by(half(jnp.stack([total[1], total[3]])), "z", 1))
     back = full(shift_by(half(jnp.stack([total[7], total[5]])), "z", -1))

time: 117 us -> 117 us (level)
  waiting for transfers between devices: 10.6 us -> 8.88 us
  transfers between devices with their start and end apart: 11 -> 11, of which waited for: 6 -> 6; matrix products, arithmetic and copies ran while one was open for 4% -> 5% of each run, Pallas kernels for 1% -> 1%
where the time goes in v11:
time: 117 us; the launch traced here: 116 us
  starting transfers between devices  56.8 us (49%)
  blocking collectives  35.1 us (30%)
  waiting for transfers between devices  8.88 us (8%)
  matrix products  5.68 us (5%)
  other arithmetic  4.56 us (4%)
  between operations  2.28 us (2%)
  Pallas kernels  1.36 us (1%)
    all_gather x1, blocking collectives, per_device(): lax.all_gather(near_images, 'z', axis=0, tiled=False)  35.1 us
    ppermute x9, starting transfers between devices, shift_by(): lax.ppermute(block, axis, [(i, (i + step) % count) for i in range(count)])  29.4 us
    all_to_all x1, starting transfers between devices, gather(): return lax.all_to_all(copies, axes, 0, 0, tiled=True)  15.2 us
    all_to_all x1, starting transfers between devices, scatter(): lax.all_to_all(parts.reshape(count, parts.shape[0] // count, parts.shape[...  12.2 us
    ppermute x9, waiting for transfers between devices, shift_by(): lax.ppermute(block, axis, [(i, (i + step) % count) for i in range(count)])  7.25 us
  transfers between devices with their start and end apart: 11, of which 6 were waited for; matrix products, arithmetic and copies ran while one was open for 5% of the time, Pallas kernels for 1%

profile of v11, /device:TPU:2, one launch (start us, length us, event | category | flops | bytes accessed | tf_op | source)
XLA Modules:
  0.0 115.7 jit_solution(1553882160712668482)
XLA Ops:
  0.6 3.6 %collective-permute-start = (bf16[16,1152]{1,0:T(8,128)(2,1)}, bf16[16,1152]{1,0:T(8,128)(2,1)S(1)}, u32[]{:S(2)}, u32[]{:S(2)}) collective-permute-start(bf16[16,1152]{1,0:T(8,128)(2,1)} %param.5), channel_id=1, source_target_pairs={{0,1},{1,0},{2,3},{3,2},{4,5},{5,4},{6,7},{7,6},{8,9},{9,8},{10,11... | collective-permute-start | bytes 110600 | tf_op jit(solution)/shard_map/ppermute | solution.py:25
  4.2 0.0 copy-start
  4.2 0.8 copy-done
  5.0 1.2 %copies.1 = bf16[32,16,1152]{2,1,0:T(8,128)(2,1)} custom-call(bf16[16,1152]{1,0:T(8,128)(2,1)S(1)} %copy-done), custom_call_target="tpu_custom_call" | custom-call | tf_op jit(solution)/shard_map/copies/pallas_call | solution.py:41
  6.2 15.2 %all-to-all-start = ((bf16[32,16,1152]{2,1,0:T(8,128)(2,1)}), bf16[32,16,1152]{2,1,0:T(8,128)(2,1)S(1)}, u32[]{:S(2)}, u32[]{:S(2)}) async-start(bf16[32,16,1152]{2,1,0:T(8,128)(2,1)} %copies.1), calls=%async_computation | async-start | bytes 2359296 | tf_op jit(solution)/shard_map/all_to_all | solution.py:49
  21.4 0.0 copy-start.2
  21.5 0.0 collective-permute-done
  21.5 0.1 multiply_reduce_fusion
  21.6 0.1 multiply_convert_fusion
  21.7 35.1 %all_gather.4 = bf16[8,32,1152]{2,1,0:T(8,128)(2,1)S(1)} all-gather(bf16[1,32,1152]{2,1,0:T(8,128)(2,1)S(1)} %multiply_convert_fusion), channel_id=1, replica_groups=mesh['yhi'=4,'x'=8,'core'=2,'z'=8,'ylo'=2] {'z'}, dimensions={0}, use_global_device_ids=true | all-gather | bytes 663552 | tf_op jit(solution)/shard_map/all_gather | solution.py:109
  56.8 0.2 fusion.9
  57.1 1.9 %collective-permute-start.1 = (bf16[256,1152]{1,0:T(8,128)(2,1)S(1)}, bf16[256,1152]{1,0:T(8,128)(2,1)S(1)}, u32[]{:S(2)}, u32[]{:S(2)}) collective-permute-start(bf16[256,1152]{1,0:T(8,128)(2,1)S(1)} %bitcast.57), channel_id=1, source_target_pairs={{0,16},{16,0},{1,17},{17,1},{2,18},{18,2},{3,19},{19,3},{4,20},{20... | collective-permute-start | bytes 1769480 | tf_op jit(solution)/shard_map/ppermute | solution.py:25
  59.0 0.2 pairs.1
  60.5 0.5 collective-permute-done.1
  61.0 0.0 all-to-all-done
  61.0 1.8 %fusion.4 = (bf16[512,512]{0,1:T(8,128)(2,1)S(1)}, f32[512]{0:T(512)S(1)}) fusion(s32[512]{0:T(512)S(1)} %bitcast.53, s32[512]{0:T(512)S(1)} %fusion.32, f32[]{:T(128)} %bitcast.51, bf16[512,1152]{1,0:T(8,128)(2,1)S(1)} %bitcast.54, bf16[256,1152]{1,0:T(8,128)(2,1)S(1)} %collective-permute-done.1, bf16[256,1152]{1,0:T(8,128)(2,1)S(1)} %bitcast.58, f32[]{:T(128)} %bitcast.50), kind=kOutput, calls=%fused_computation.16 | convolution fusion | flops 611581440 | bytes 2889736 | tf_op jit(solution)/shard_map/dot_general | solution.py:119
  62.8 0.5 fusion.1
  63.3 0.0 copy-start.6
  63.3 0.1 broadcast_in_dim.9
  63.4 0.2 pad_maximum_fusion.3
  63.6 2.0 %collective-permute-start.2 = (f16[256,1280]{1,0:T(8,128)(2,1)S(1)}, f16[256,1280]{1,0:T(8,128)(2,1)}, u32[]{:S(2)}, u32[]{:S(2)}) collective-permute-start(f16[256,1280]{1,0:T(8,128)(2,1)S(1)} %pad_maximum_fusion.3), channel_id=1, source_target_pairs={{0,16},{16,0},{1,17},{17,1},{2,18},{18,2},{3,19},{19,3},{4,20},{20... | collective-permute-start | bytes 1966088 | tf_op jit(solution)/shard_map/ppermute | solution.py:25
  65.7 1.9 %fusion = f16[512,1152]{1,0:T(8,128)(2,1)} fusion(bf16[512,512]{0,1:T(8,128)(2,1)S(1)} %get-tuple-element.11, bf16[256,1152]{1,0:T(8,128)(2,1)S(1)} %copy-done.6, bf16[256,1152]{1,0:T(8,128)(2,1)S(1)} %bitcast.59), kind=kOutput, calls=%fused_computation.2 | convolution fusion | flops 607518720 | bytes 2883584 | tf_op jit(solution)/shard_map/dot_general | solution.py:128
  67.5 12.2 %all-to-all-start.1 = ((f16[32,16,1152]{2,1,0:T(8,128)(2,1)}), f16[32,16,1152]{2,1,0:T(8,128)(2,1)S(1)}, u32[]{:S(2)}, u32[]{:S(2)}) async-start(f16[32,16,1152]{2,1,0:T(8,128)(2,1)} %bitcast.16), calls=%async_computation.1 | async-start | bytes 2359296 | tf_op jit(solution)/shard_map/all_to_all | solution.py:83
  79.7 1.5 %convolution_multiply_fusion.2 = f32[256,1152]{1,0:T(8,128)S(1)} fusion(bf16[512,1152]{1,0:T(8,128)(2,1)S(1)} %bitcast.56, bf16[512,512]{0,1:T(8,128)(2,1)} %copy-done.4), kind=kOutput, calls=%fused_computation.4 | convolution fusion | flops 302284800 | bytes 2621440 | tf_op jit(solution)/shard_map/dot_general | solution.py:135
  81.2 0.0 collective-permute-done.2
  81.2 0.1 broadcast_in_dim.8
  81.3 1.2 %fusion.38 = (f16[256,1280]{1,0:T(8,128)(2,1)S(1)}, f32[256,1280]{1,0:T(8,128)S(1)}) fusion(f16[256,1280]{1,0:T(8,128)(2,1)} %collective-permute-done.2, f32[256,128]{1,0:T(8,128)S(1)} %broadcast_in_dim.8, f32[256,1152]{1,0:T(8,128)S(1)} %convolution_multiply_fusion.2), kind=kLoop, calls=%fused_computation.86 | loop fusion | flops 1310720 | bytes 3932160 | tf_op jit(solution)/shard_map/convert.13
  82.6 0.1 fusion.39
  82.7 3.5 %collective-permute-start.3 = (f16[2,32,1280]{2,1,0:T(8,128)(2,1)S(1)}, f16[2,32,1280]{2,1,0:T(8,128)(2,1)S(1)}, u32[]{:S(2)}, u32[]{:S(2)}) collective-permute-start(f16[2,32,1280]{2,1,0:T(8,128)(2,1)S(1)} %pad_maximum_fusion.4), channel_id=1, source_target_pairs={{0,2},{2,4},{4,6},{6,8},{8,10},{10,12},{12,14},{14,0},{1,3},{3,5},... | collective-permute-start | bytes 491528 | tf_op jit(solution)/shard_map/ppermute | solution.py:25
  86.3 3.5 %collective-permute-start.4 = (f16[2,32,1280]{2,1,0:T(8,128)(2,1)S(1)}, f16[2,32,1280]{2,1,0:T(8,128)(2,1)S(1)}, u32[]{:S(2)}, u32[]{:S(2)}) collective-permute-start(f16[2,32,1280]{2,1,0:T(8,128)(2,1)S(1)} %pad_maximum_fusion.5), channel_id=1, source_target_pairs={{0,14},{2,0},{4,2},{6,4},{8,6},{10,8},{12,10},{14,12},{1,15},{3,1}... | collective-permute-start | bytes 491528 | tf_op jit(solution)/shard_map/ppermute | solution.py:25
  89.8 3.7 %collective-permute-start.7 = (f16[32,1280]{1,0:T(8,128)(2,1)S(1)}, f16[32,1280]{1,0:T(8,128)(2,1)S(1)}, u32[]{:S(2)}, u32[]{:S(2)}) collective-permute-start(f16[32,1280]{1,0:T(8,128)(2,1)S(1)} %get-tuple-element.13), channel_id=1, source_target_pairs={{0,8},{2,10},{4,12},{6,14},{8,0},{10,2},{12,4},{14,6},{1,9},{3,11}... | collective-permute-start | bytes 245768 | tf_op jit(solution)/shard_map/ppermute | solution.py:25
  93.6 0.0 collective-permute-done.3
  93.6 0.2 collective-permute-done.4
  93.9 3.3 %collective-permute-start.5 = (f16[32,1280]{1,0:T(8,128)(2,1)S(1)}, f16[32,1280]{1,0:T(8,128)(2,1)S(1)}, u32[]{:S(2)}, u32[]{:S(2)}) collective-permute-start(f16[32,1280]{1,0:T(8,128)(2,1)S(1)} %get-tuple-element.9), channel_id=1, source_target_pairs={{0,4},{2,6},{4,8},{6,10},{8,12},{10,14},{12,0},{14,2},{1,5},{3,7},... | collective-permute-start | bytes 245768 | tf_op jit(solution)/shard_map/ppermute | solution.py:25
  97.3 0.0 copy-start.1
  97.3 4.6 %collective-permute-start.6 = (f16[32,1280]{1,0:T(8,128)(2,1)S(1)}, f16[32,1280]{1,0:T(8,128)(2,1)S(1)}, u32[]{:S(2)}, u32[]{:S(2)}) collective-permute-start(f16[32,1280]{1,0:T(8,128)(2,1)S(1)} %get-tuple-element.10), channel_id=1, source_target_pairs={{0,12},{2,14},{4,0},{6,2},{8,4},{10,6},{12,8},{14,10},{1,13},{3,15... | collective-permute-start | bytes 245768 | tf_op jit(solution)/shard_map/ppermute | solution.py:25
  101.9 0.0 collective-permute-done.7
  101.9 1.4 %collective-permute-done.5 = f16[32,1280]{1,0:T(8,128)(2,1)S(1)} collective-permute-done((f16[32,1280]{1,0:T(8,128)(2,1)S(1)}, f16[32,1280]{1,0:T(8,128)(2,1)S(1)}, u32[]{:S(2)}, u32[]{:S(2)}) %collective-permute-start.5) | collective-permute-done | bytes 81952 | tf_op jit(solution)/shard_map/ppermute | solution.py:25
  103.3 1.4 %collective-permute-done.6 = f16[32,1280]{1,0:T(8,128)(2,1)S(1)} collective-permute-done((f16[32,1280]{1,0:T(8,128)(2,1)S(1)}, f16[32,1280]{1,0:T(8,128)(2,1)S(1)}, u32[]{:S(2)}, u32[]{:S(2)}) %collective-permute-start.6) | collective-permute-done | bytes 81952 | tf_op jit(solution)/shard_map/ppermute | solution.py:25
  104.7 0.1 fusion.19
  104.8 3.1 %collective-permute-start.8 = (f16[16,1280]{1,0:T(8,128)(2,1)S(1)}, f16[16,1280]{1,0:T(8,128)(2,1)S(1)}, u32[]{:S(2)}, u32[]{:S(2)}) collective-permute-start(f16[16,1280]{1,0:T(8,128)(2,1)S(1)} %slice_convert_fusion), channel_id=1, source_target_pairs={{0,1},{1,0},{2,3},{3,2},{4,5},{5,4},{6,7},{7,6},{8,9},{9,8},{10,11... | collective-permute-start | bytes 122888 | tf_op jit(solution)/shard_map/ppermute | solution.py:25
  107.9 3.8 %collective-permute-done.8 = f16[16,1280]{1,0:T(8,128)(2,1)S(1)} collective-permute-done((f16[16,1280]{1,0:T(8,128)(2,1)S(1)}, f16[16,1280]{1,0:T(8,128)(2,1)S(1)}, u32[]{:S(2)}, u32[]{:S(2)}) %collective-permute-start.8) | collective-permute-done | bytes 40992 | tf_op jit(solution)/shard_map/ppermute | solution.py:25
  111.7 0.6 fusion.25
  112.3 1.6 %all-to-all-done.1 = f16[32,16,1152]{2,1,0:T(8,128)(2,1)S(1)} async-done(((f16[32,16,1152]{2,1,0:T(8,128)(2,1)}), f16[32,16,1152]{2,1,0:T(8,128)(2,1)S(1)}, u32[]{:S(2)}, u32[]{:S(2)}) %all-to-all-start.1) | async-done | bytes 1179680 | tf_op jit(solution)/shard_map/all_to_all | solution.py:83
  113.9 0.2 convert_reduce_fusion
  114.1 0.2 fusion.21
  114.3 0.7 add_add_fusion.1
  115.0 0.7 add_add_fusion
  (21 shorter events, 0.3 us)
Async XLA Ops:
  0.6 20.8 %collective-permute-start = (bf16[16,1152]{1,0:T(8,128)(2,1)}, bf16[16,1152]{1,0:T(8,128)(2,1)S(1)}, u32[]{:S(2)}, u32[]{:S(2)}) collective-permute-start(bf16[16,1152]{1,0:T(8,128)(2,1)} %param.5), channel_id=1, source_target_pairs={{0,1},{1,0},{2,3},{3,2},{4,5},{5,4},{6,7},{7,6},{8,9},{9,8},{10,11... | collective-permute-start | bytes 110600 | tf_op jit(solution)/shard_map/ppermute | solution.py:25
  4.2 0.8 copy-start
  6.2 15.3 %copy-start.3 = (bf16[16,1152]{1,0:T(8,128)(2,1)S(1)}, bf16[16,1152]{1,0:T(8,128)(2,1)}, u32[]{:S(2)}) copy-start(bf16[16,1152]{1,0:T(8,128)(2,1)} %param.5) | copy-start | bytes 110596
  6.2 54.7 %all-to-all-start = ((bf16[32,16,1152]{2,1,0:T(8,128)(2,1)}), bf16[32,16,1152]{2,1,0:T(8,128)(2,1)S(1)}, u32[]{:S(2)}, u32[]{:S(2)}) async-start(bf16[32,16,1152]{2,1,0:T(8,128)(2,1)} %copies.1), calls=%async_computation | async-start | bytes 2359296 | tf_op jit(solution)/shard_map/all_to_all | solution.py:49
  21.4 37.5 %copy-start.2 = (s32[16384]{0:T(1024)S(1)}, s32[16384]{0:T(1024)}, u32[]{:S(2)}) copy-start(s32[16384]{0:T(1024)} %param.7) | copy-start | bytes 196612
  57.1 3.9 %collective-permute-start.1 = (bf16[256,1152]{1,0:T(8,128)(2,1)S(1)}, bf16[256,1152]{1,0:T(8,128)(2,1)S(1)}, u32[]{:S(2)}, u32[]{:S(2)}) collective-permute-start(bf16[256,1152]{1,0:T(8,128)(2,1)S(1)} %bitcast.57), channel_id=1, source_target_pairs={{0,16},{16,0},{1,17},{17,1},{2,18},{18,2},{3,19},{19,3},{4,20},{20... | collective-permute-start | bytes 1769480 | tf_op jit(solution)/shard_map/ppermute | solution.py:25
  61.0 1.8 %copy-start.5 = (bf16[256,1152]{1,0:T(8,128)(2,1)}, bf16[256,1152]{1,0:T(8,128)(2,1)S(1)}, u32[]{:S(2)}) copy-start(bf16[256,1152]{1,0:T(8,128)(2,1)S(1)} %collective-permute-done.1) | copy-start | bytes 1769476
  62.7 2.9 %copy-start.4 = (bf16[512,512]{0,1:T(8,128)(2,1)}, bf16[512,512]{0,1:T(8,128)(2,1)S(1)}, u32[]{:S(2)}) copy-start(bf16[512,512]{0,1:T(8,128)(2,1)S(1)} %get-tuple-element.11) | copy-start | bytes 1572868
  63.3 2.3 %copy-start.6 = (bf16[256,1152]{1,0:T(8,128)(2,1)S(1)}, bf16[256,1152]{1,0:T(8,128)(2,1)}, u32[]{:S(2)}) copy-start(bf16[256,1152]{1,0:T(8,128)(2,1)} %copy-done.5) | copy-start | bytes 1769476
  63.6 17.6 %collective-permute-start.2 = (f16[256,1280]{1,0:T(8,128)(2,1)S(1)}, f16[256,1280]{1,0:T(8,128)(2,1)}, u32[]{:S(2)}, u32[]{:S(2)}) collective-permute-start(f16[256,1280]{1,0:T(8,128)(2,1)S(1)} %pad_maximum_fusion.3), channel_id=1, source_target_pairs={{0,16},{16,0},{1,17},{17,1},{2,18},{18,2},{3,19},{19,3},{4,20},{20... | collective-permute-start | bytes 1966088 | tf_op jit(solution)/shard_map/ppermute | solution.py:25
  67.5 46.4 %all-to-all-start.1 = ((f16[32,16,1152]{2,1,0:T(8,128)(2,1)}), f16[32,16,1152]{2,1,0:T(8,128)(2,1)S(1)}, u32[]{:S(2)}, u32[]{:S(2)}) async-start(f16[32,16,1152]{2,1,0:T(8,128)(2,1)} %bitcast.16), calls=%async_computation.1 | async-start | bytes 2359296 | tf_op jit(solution)/shard_map/all_to_all | solution.py:83
  82.7 10.9 %collective-permute-start.3 = (f16[2,32,1280]{2,1,0:T(8,128)(2,1)S(1)}, f16[2,32,1280]{2,1,0:T(8,128)(2,1)S(1)}, u32[]{:S(2)}, u32[]{:S(2)}) collective-permute-start(f16[2,32,1280]{2,1,0:T(8,128)(2,1)S(1)} %pad_maximum_fusion.4), channel_id=1, source_target_pairs={{0,2},{2,4},{4,6},{6,8},{8,10},{10,12},{12,14},{14,0},{1,3},{3,5},... | collective-permute-start | bytes 491528 | tf_op jit(solution)/shard_map/ppermute | solution.py:25
  86.3 7.5 %collective-permute-start.4 = (f16[2,32,1280]{2,1,0:T(8,128)(2,1)S(1)}, f16[2,32,1280]{2,1,0:T(8,128)(2,1)S(1)}, u32[]{:S(2)}, u32[]{:S(2)}) collective-permute-start(f16[2,32,1280]{2,1,0:T(8,128)(2,1)S(1)} %pad_maximum_fusion.5), channel_id=1, source_target_pairs={{0,14},{2,0},{4,2},{6,4},{8,6},{10,8},{12,10},{14,12},{1,15},{3,1}... | collective-permute-start | bytes 491528 | tf_op jit(solution)/shard_map/ppermute | solution.py:25
  89.8 12.0 %collective-permute-start.7 = (f16[32,1280]{1,0:T(8,128)(2,1)S(1)}, f16[32,1280]{1,0:T(8,128)(2,1)S(1)}, u32[]{:S(2)}, u32[]{:S(2)}) collective-permute-start(f16[32,1280]{1,0:T(8,128)(2,1)S(1)} %get-tuple-element.13), channel_id=1, source_target_pairs={{0,8},{2,10},{4,12},{6,14},{8,0},{10,2},{12,4},{14,6},{1,9},{3,11}... | collective-permute-start | bytes 245768 | tf_op jit(solution)/shard_map/ppermute | solution.py:25
  93.9 9.4 %collective-permute-start.5 = (f16[32,1280]{1,0:T(8,128)(2,1)S(1)}, f16[32,1280]{1,0:T(8,128)(2,1)S(1)}, u32[]{:S(2)}, u32[]{:S(2)}) collective-permute-start(f16[32,1280]{1,0:T(8,128)(2,1)S(1)} %get-tuple-element.9), channel_id=1, source_target_pairs={{0,4},{2,6},{4,8},{6,10},{8,12},{10,14},{12,0},{14,2},{1,5},{3,7},... | collective-permute-start | bytes 245768 | tf_op jit(solution)/shard_map/ppermute | solution.py:25
  97.3 16.9 %copy-start.1 = (bf16[16,1152]{1,0:T(8,128)(2,1)S(1)}, bf16[16,1152]{1,0:T(8,128)(2,1)}, u32[]{:S(2)}) copy-start(bf16[16,1152]{1,0:T(8,128)(2,1)} %raw_ref.1) | copy-start | bytes 110596
  97.3 7.4 %collective-permute-start.6 = (f16[32,1280]{1,0:T(8,128)(2,1)S(1)}, f16[32,1280]{1,0:T(8,128)(2,1)S(1)}, u32[]{:S(2)}, u32[]{:S(2)}) collective-permute-start(f16[32,1280]{1,0:T(8,128)(2,1)S(1)} %get-tuple-element.10), channel_id=1, source_target_pairs={{0,12},{2,14},{4,0},{6,2},{8,4},{10,6},{12,8},{14,10},{1,13},{3,15... | collective-permute-start | bytes 245768 | tf_op jit(solution)/shard_map/ppermute | solution.py:25
  104.8 6.9 %collective-permute-start.8 = (f16[16,1280]{1,0:T(8,128)(2,1)S(1)}, f16[16,1280]{1,0:T(8,128)(2,1)S(1)}, u32[]{:S(2)}, u32[]{:S(2)}) collective-permute-start(f16[16,1280]{1,0:T(8,128)(2,1)S(1)} %slice_convert_fusion), channel_id=1, source_target_pairs={{0,1},{1,0},{2,3},{3,2},{4,5},{5,4},{6,7},{7,6},{8,9},{9,8},{10,11... | collective-permute-start | bytes 122888 | tf_op jit(solution)/shard_map/ppermute | solution.py:25

commit v12 on v10

--- a/solution.py
+++ b/solution.py
@@ -49,7 +49,7 @@
     return lax.all_to_all(copies, axes, 0, 0, tiled=True)
 
 
-def pairs_kernel(all_ref, pairs_ref):
+def pairs_kernel(all_ref, after_ref, *pairs_refs):
     group = lax.axis_index(TEXT_GROUP)
     core, z, ylo = [lax.axis_index(axis) for axis in IMAGE_GROUP]
     lane = lax.broadcasted_iota(jnp.int32, (1, 128), 1)
@@ -61,21 +61,21 @@
             row = all_ref[pl.ds(first + lax.rem(z // 4 + late, 2), 1), :]
             swapped = jnp.where(lane % 32 < 16, pltpu.roll(row, 112, 1), pltpu.roll(row, 16, 1))
             rows.append(pltpu.roll(jnp.where(ylo == 0, row, swapped), lax.rem(128 - turn, 128), 1))
-        pairs_ref[2 * ahead : 2 * ahead + 1, :] = jnp.where(lane + turn < 128, rows[0], rows[1])
-        pairs_ref[2 * ahead + 1 : 2 * ahead + 2, :] = jnp.where(lane + turn < 128, rows[1], rows[0])
+        pairs_refs[ahead][0:1, :] = jnp.where(lane + turn < 128, rows[0], rows[1])
+        pairs_refs[ahead][1:2, :] = jnp.where(lane + turn < 128, rows[1], rows[0])
 
 
-def image_pairs(caption_partner_position, image_count):
+def image_pairs(caption_partner_position, core_images, after):
     pairs = pl.pallas_call(
         pairs_kernel,
-        out_shape=jax.ShapeDtypeStruct((image_count // 128, 128), jnp.int32),
-        in_specs=[pl.BlockSpec(memory_space=pltpu.VMEM)],
-        out_specs=pl.BlockSpec(memory_space=pltpu.VMEM),
+        out_shape=[jax.ShapeDtypeStruct((core_images // 128, 128), jnp.int32)] * 2,
+        in_specs=[pl.BlockSpec(memory_space=pltpu.VMEM), pl.BlockSpec(memory_space=pl.ANY)],
+        out_specs=[pl.BlockSpec(memory_space=pltpu.VMEM)] * 2,
         cost_estimate=pl.CostEstimate(flops=WAIT_FLOPS, bytes_accessed=0, transcendentals=0),
         compiler_params=pltpu.CompilerParams(vmem_limit_bytes=KERNEL_BYTES),
         name="pairs",
-    )(caption_partner_position.reshape(-1, 128))
-    return pairs.reshape(-1)
+    )(caption_partner_position.reshape(-1, 128), after)
+    return [own_or_other.reshape(-1) for own_or_other in pairs]
 
 
 def scatter(parts, axes):
@@ -107,33 +107,44 @@
     near_images = normalize(near_images).astype(jnp.bfloat16)
     txt_block = gather(caption_vectors, TEXT_GROUP).reshape(-1, width)
     z_images = from_own(lax.all_gather(near_images, "z", axis=0, tiled=False), "z").reshape(-1, width)
-    img_block = jnp.concatenate([z_images, shift_by(z_images, "core", 1)])
-    image_count = img_block.shape[0]
-    my_pairs = image_pairs(caption_partner_position, image_count)
+    other_images = shift_by(z_images, "core", 1)
+    image_count = 2 * z_images.shape[0]
+    own_pairs, other_pairs = image_pairs(caption_partner_position, image_count // 2, z_images[:16, :128])
     column = jnp.arange(txt_block.shape[0], dtype=jnp.int32)
     text_ids = (
         column // own_rows * image_count + lax.axis_index(IMAGE_GROUP) * own_rows + column % own_rows
     )
-    logits = (
-        similarity_multiplier
-        * lax.dot_general(
-            img_block, txt_block, (((1,), (1,)), ((), ())), preferred_element_type=jnp.float32
+
+    def compare(images, partners):
+        logits = (
+            similarity_multiplier
+            * lax.dot_general(
+                images, txt_block, (((1,), (1,)), ((), ())), preferred_element_type=jnp.float32
+            )
+            + shift
         )
-        + shift
-    )
-    positive = (my_pairs[:, None] == text_ids[None, :]).astype(jnp.float32)
-    sign = 2.0 * positive - 1.0
-    loss = jnp.sum(jax.nn.softplus(-sign * logits), axis=1)
-    slope = (jax.nn.sigmoid(logits) - positive).astype(jnp.bfloat16)
-    txt_part = lax.dot_general(
-        slope, img_block, (((0,), (0,)), ((), ())), preferred_element_type=jnp.float32
-    )
+        positive = (partners[:, None] == text_ids[None, :]).astype(jnp.float32)
+        sign = 2.0 * positive - 1.0
+        loss = jnp.sum(jax.nn.softplus(-sign * logits), axis=1)
+        return loss, (jax.nn.sigmoid(logits) - positive).astype(jnp.bfloat16)
+
+    def image_part(loss, slope):
+        terms = SEND_SCALE * jnp.dot(slope, txt_block, preferred_element_type=jnp.float32)
+        losses = jnp.broadcast_to(loss[:, None] * LOSS_SCALE, (loss.shape[0], 128))
+        return jnp.concatenate([terms, losses], axis=1)
+
+    def text_part(slope, images):
+        return lax.dot_general(
+            slope, images, (((0,), (0,)), ((), ())), preferred_element_type=jnp.float32
+        )
+
+    own_loss, own_slope = compare(z_images, own_pairs)
+    other_loss, other_slope = compare(other_images, other_pairs)
+    txt_part = text_part(own_slope, z_images) + text_part(other_slope, other_images)
     txt_terms = scatter(half(SEND_SCALE * txt_part), TEXT_GROUP)
-    img_part = SEND_SCALE * jnp.dot(slope, txt_block, preferred_element_type=jnp.float32)
-    img_part = jnp.concatenate(
-        [img_part, jnp.broadcast_to(loss[:, None] * LOSS_SCALE, (image_count, 128))], axis=1
-    ).reshape(2, 8, 2 * own_rows, width + 128)
-    total = img_part[0] + full(shift_by(half(img_part[1]), "core", 1))
+    came = shift_by(half(image_part(other_loss, other_slope)), "core", 1)
+    total = image_part(own_loss, own_slope) + full(came)
+    total = total.reshape(8, 2 * own_rows, width + 128)
     far = shift_by(half(total[4]), "z", 4)
     ahead = full(shift_by(half(jnp.stack([total[1], total[3]])), "z", 1))
     back = full(shift_by(half(jnp.stack([total[7], total[5]])), "z", -1))

time: 117 us -> 117 us (level)
  waiting for transfers between devices: 10.6 us -> 9.42 us
    dot_general x3 -> x6, matrix products: 4.65 us -> 5.37 us  [the longest x2 2.32 us: text_part(): lax.dot_general(slope, images, (((0,), (0,)), ((), ())), preferred_elemen...]
  transfers between devices with their start and end apart: 11 -> 11, of which waited for: 6 -> 6; matrix products, arithmetic and copies ran while one was open for 4% -> 5% of each run, Pallas kernels for 1% -> 1%
where the time goes in v12:
time: 117 us; the launch traced here: 116 us
  starting transfers between devices  57.1 us (49%)
  blocking collectives  35 us (30%)
  waiting for transfers between devices  9.42 us (8%)
  matrix products  5.37 us (5%)
  other arithmetic  4.62 us (4%)
  between operations  2.32 us (2%)
  Pallas kernels  1.35 us (1%)
    all_gather x1, blocking collectives, per_device(): lax.all_gather(near_images, 'z', axis=0, tiled=False)  35 us
    ppermute x9, starting transfers between devices, shift_by(): lax.ppermute(block, axis, [(i, (i + step) % count) for i in range(count)])  29.7 us
    all_to_all x1, starting transfers between devices, gather(): return lax.all_to_all(copies, axes, 0, 0, tiled=True)  15.2 us
    all_to_all x1, starting transfers between devices, scatter(): lax.all_to_all(parts.reshape(count, parts.shape[0] // count, parts.shape[...  12.1 us
    ppermute x9, waiting for transfers between devices, shift_by(): lax.ppermute(block, axis, [(i, (i + step) % count) for i in range(count)])  7.75 us
  transfers between devices with their start and end apart: 11, of which 6 were waited for; matrix products, arithmetic and copies ran while one was open for 5% of the time, Pallas kernels for 1%

profile of v12, /device:TPU:2, one launch (start us, length us, event | category | flops | bytes accessed | tf_op | source)
XLA Modules:
  0.0 116.2 jit_solution(7394696522238229849)
XLA Ops:
  0.6 3.6 %collective-permute-start = (bf16[16,1152]{1,0:T(8,128)(2,1)}, bf16[16,1152]{1,0:T(8,128)(2,1)S(1)}, u32[]{:S(2)}, u32[]{:S(2)}) collective-permute-start(bf16[16,1152]{1,0:T(8,128)(2,1)} %param.5), channel_id=1, source_target_pairs={{0,1},{1,0},{2,3},{3,2},{4,5},{5,4},{6,7},{7,6},{8,9},{9,8},{10,11... | collective-permute-start | bytes 110600 | tf_op jit(solution)/shard_map/ppermute | solution.py:25
  4.2 0.0 copy-start
  4.2 0.8 copy-done
  5.0 1.2 %copies.1 = bf16[32,16,1152]{2,1,0:T(8,128)(2,1)} custom-call(bf16[16,1152]{1,0:T(8,128)(2,1)S(1)} %copy-done), custom_call_target="tpu_custom_call" | custom-call | tf_op jit(solution)/shard_map/copies/pallas_call | solution.py:41
  6.2 15.2 %all-to-all-start = ((bf16[32,16,1152]{2,1,0:T(8,128)(2,1)}), bf16[32,16,1152]{2,1,0:T(8,128)(2,1)S(1)}, u32[]{:S(2)}, u32[]{:S(2)}) async-start(bf16[32,16,1152]{2,1,0:T(8,128)(2,1)} %copies.1), calls=%async_computation | async-start | bytes 2359296 | tf_op jit(solution)/shard_map/all_to_all | solution.py:49
  21.4 0.0 copy-start.2
  22.8 0.0 collective-permute-done
  22.8 0.1 multiply_reduce_fusion
  22.9 0.1 multiply_convert_fusion
  23.0 35.0 %all_gather.4 = bf16[8,32,1152]{2,1,0:T(8,128)(2,1)S(1)} all-gather(bf16[1,32,1152]{2,1,0:T(8,128)(2,1)S(1)} %multiply_convert_fusion), channel_id=1, replica_groups=mesh['yhi'=4,'x'=8,'core'=2,'z'=8,'ylo'=2] {'z'}, dimensions={0}, use_global_device_ids=true | all-gather | bytes 663552 | tf_op jit(solution)/shard_map/all_gather | solution.py:109
  58.0 0.2 fusion.5
  58.3 1.9 %collective-permute-start.1 = (bf16[256,1152]{1,0:T(8,128)(2,1)S(1)}, bf16[256,1152]{1,0:T(8,128)(2,1)S(1)}, u32[]{:S(2)}, u32[]{:S(2)}) collective-permute-start(bf16[256,1152]{1,0:T(8,128)(2,1)S(1)} %bitcast.67), channel_id=1, source_target_pairs={{0,16},{16,0},{1,17},{17,1},{2,18},{18,2},{3,19},{19,3},{4,20},{20... | collective-permute-start | bytes 1769480 | tf_op jit(solution)/shard_map/ppermute | solution.py:25
  60.2 0.2 pairs.1
  60.4 0.5 fusion.4
  61.0 0.6 fusion.44
  61.6 0.6 collective-permute-done.1
  62.2 1.3 %fusion.17 = (f32[256]{0:T(256)S(1)}, f32[256]{0:T(256)S(1)}, f32[256,512]{1,0:T(8,128)S(1)}) fusion(s32[512]{0:T(512)S(1)} %fusion.38, s32[256]{0:T(256)S(1)} %bitcast.63, f32[256,512]{1,0:T(8,128)S(1)} %fusion.4, s32[256]{0:T(256)S(1)} %bitcast.60, f32[]{:T(128)} %bitcast.58, bf16[256,1152]{1,0:T(8,128)(2,1)S(1)} %collective-permute-done.1, ...), kind=kOutput, calls=%fused_computation.33 | convolution fusion | flops 305397248 | bytes 2824200 | tf_op jit(solution)/shard_map/dot_general | solution.py:121
  63.5 0.6 fusion.2
  64.1 0.1 broadcast_in_dim.9
  64.2 0.2 pad_maximum_fusion
  64.4 2.0 %collective-permute-start.2 = (f16[256,1280]{1,0:T(8,128)(2,1)S(1)}, f16[256,1280]{1,0:T(8,128)(2,1)}, u32[]{:S(2)}, u32[]{:S(2)}) collective-permute-start(f16[256,1280]{1,0:T(8,128)(2,1)S(1)} %pad_maximum_fusion), channel_id=1, source_target_pairs={{0,16},{16,0},{1,17},{17,1},{2,18},{18,2},{3,19},{19,3},{4,20},{20... | collective-permute-start | bytes 1966088 | tf_op jit(solution)/shard_map/ppermute | solution.py:25
  66.4 1.7 %fusion.1 = f16[512,1152]{1,0:T(8,128)(2,1)} fusion(f32[512,1152]{1,0:T(8,128)S(1)} %fusion.44, bf16[256,1152]{1,0:T(8,128)(2,1)S(1)} %copy-done.6, f32[256,512]{1,0:T(8,128)S(1)} %get-tuple-element.26, s32[512]{0:T(512)S(1)} %fusion.38, s32[256]{0:T(256)S(1)} %bitcast.65), kind=kOutput, calls=%fused_computation.2 | convolution fusion | flops 304676864 | bytes 4656128 | tf_op jit(solution)/shard_map/dot_general | solution.py:137
  68.1 12.1 %all-to-all-start.1 = ((f16[32,16,1152]{2,1,0:T(8,128)(2,1)}), f16[32,16,1152]{2,1,0:T(8,128)(2,1)S(1)}, u32[]{:S(2)}, u32[]{:S(2)}) async-start(f16[32,16,1152]{2,1,0:T(8,128)(2,1)} %bitcast.74), calls=%async_computation.1 | async-start | bytes 2359296 | tf_op jit(solution)/shard_map/all_to_all | solution.py:83
  80.3 0.6 convolution_multiply_fusion.1
  80.9 0.0 collective-permute-done.2
  80.9 0.1 broadcast_in_dim.8
  81.0 1.3 %fusion.47 = (f16[256,1280]{1,0:T(8,128)(2,1)S(1)}, f32[256,1280]{1,0:T(8,128)S(1)}) fusion(f16[256,1280]{1,0:T(8,128)(2,1)} %collective-permute-done.2, f32[256,128]{1,0:T(8,128)S(1)} %broadcast_in_dim.8, f32[256,1152]{1,0:T(8,128)S(1)} %convolution_multiply_fusion.1), kind=kLoop, calls=%fused_computation.94 | loop fusion | flops 1310720 | bytes 3932160 | tf_op jit(solution)/shard_map/convert.13
  82.3 0.1 fusion.48
  82.4 3.7 %collective-permute-start.3 = (f16[2,32,1280]{2,1,0:T(8,128)(2,1)S(1)}, f16[2,32,1280]{2,1,0:T(8,128)(2,1)S(1)}, u32[]{:S(2)}, u32[]{:S(2)}) collective-permute-start(f16[2,32,1280]{2,1,0:T(8,128)(2,1)S(1)} %pad_maximum_fusion.1), channel_id=1, source_target_pairs={{0,2},{2,4},{4,6},{6,8},{8,10},{10,12},{12,14},{14,0},{1,3},{3,5},... | collective-permute-start | bytes 491528 | tf_op jit(solution)/shard_map/ppermute | solution.py:25
  86.2 3.3 %collective-permute-start.4 = (f16[2,32,1280]{2,1,0:T(8,128)(2,1)S(1)}, f16[2,32,1280]{2,1,0:T(8,128)(2,1)S(1)}, u32[]{:S(2)}, u32[]{:S(2)}) collective-permute-start(f16[2,32,1280]{2,1,0:T(8,128)(2,1)S(1)} %pad_maximum_fusion.2), channel_id=1, source_target_pairs={{0,14},{2,0},{4,2},{6,4},{8,6},{10,8},{12,10},{14,12},{1,15},{3,1}... | collective-permute-start | bytes 491528 | tf_op jit(solution)/shard_map/ppermute | solution.py:25
  89.5 3.9 %collective-permute-start.7 = (f16[32,1280]{1,0:T(8,128)(2,1)S(1)}, f16[32,1280]{1,0:T(8,128)(2,1)S(1)}, u32[]{:S(2)}, u32[]{:S(2)}) collective-permute-start(f16[32,1280]{1,0:T(8,128)(2,1)S(1)} %get-tuple-element.17), channel_id=1, source_target_pairs={{0,8},{2,10},{4,12},{6,14},{8,0},{10,2},{12,4},{14,6},{1,9},{3,11}... | collective-permute-start | bytes 245768 | tf_op jit(solution)/shard_map/ppermute | solution.py:25
  93.5 0.2 collective-permute-done.4
  93.7 3.3 %collective-permute-start.5 = (f16[32,1280]{1,0:T(8,128)(2,1)S(1)}, f16[32,1280]{1,0:T(8,128)(2,1)S(1)}, u32[]{:S(2)}, u32[]{:S(2)}) collective-permute-start(f16[32,1280]{1,0:T(8,128)(2,1)S(1)} %get-tuple-element.15), channel_id=1, source_target_pairs={{0,4},{2,6},{4,8},{6,10},{8,12},{10,14},{12,0},{14,2},{1,5},{3,7},... | collective-permute-start | bytes 245768 | tf_op jit(solution)/shard_map/ppermute | solution.py:25
  97.1 0.0 copy-start.1
  97.1 0.0 copy-start.4
  97.1 4.8 %collective-permute-start.6 = (f16[32,1280]{1,0:T(8,128)(2,1)S(1)}, f16[32,1280]{1,0:T(8,128)(2,1)S(1)}, u32[]{:S(2)}, u32[]{:S(2)}) collective-permute-start(f16[32,1280]{1,0:T(8,128)(2,1)S(1)} %get-tuple-element.16), channel_id=1, source_target_pairs={{0,12},{2,14},{4,0},{6,2},{8,4},{10,6},{12,8},{14,10},{1,13},{3,15... | collective-permute-start | bytes 245768 | tf_op jit(solution)/shard_map/ppermute | solution.py:25
  101.9 0.0 collective-permute-done.7
  101.9 1.3 %collective-permute-done.5 = f16[32,1280]{1,0:T(8,128)(2,1)S(1)} collective-permute-done((f16[32,1280]{1,0:T(8,128)(2,1)S(1)}, f16[32,1280]{1,0:T(8,128)(2,1)S(1)}, u32[]{:S(2)}, u32[]{:S(2)}) %collective-permute-start.5) | collective-permute-done | bytes 81952 | tf_op jit(solution)/shard_map/ppermute | solution.py:25
  103.2 1.5 %collective-permute-done.6 = f16[32,1280]{1,0:T(8,128)(2,1)S(1)} collective-permute-done((f16[32,1280]{1,0:T(8,128)(2,1)S(1)}, f16[32,1280]{1,0:T(8,128)(2,1)S(1)}, u32[]{:S(2)}, u32[]{:S(2)}) %collective-permute-start.6) | collective-permute-done | bytes 81952 | tf_op jit(solution)/shard_map/ppermute | solution.py:25
  104.7 0.1 fusion.25
  104.8 3.1 %collective-permute-start.8 = (f16[16,1280]{1,0:T(8,128)(2,1)S(1)}, f16[16,1280]{1,0:T(8,128)(2,1)S(1)}, u32[]{:S(2)}, u32[]{:S(2)}) collective-permute-start(f16[16,1280]{1,0:T(8,128)(2,1)S(1)} %slice_convert_fusion), channel_id=1, source_target_pairs={{0,1},{1,0},{2,3},{3,2},{4,5},{5,4},{6,7},{7,6},{8,9},{9,8},{10,11... | collective-permute-start | bytes 122888 | tf_op jit(solution)/shard_map/ppermute | solution.py:25
  108.0 4.1 %collective-permute-done.8 = f16[16,1280]{1,0:T(8,128)(2,1)S(1)} collective-permute-done((f16[16,1280]{1,0:T(8,128)(2,1)S(1)}, f16[16,1280]{1,0:T(8,128)(2,1)S(1)}, u32[]{:S(2)}, u32[]{:S(2)}) %collective-permute-start.8) | collective-permute-done | bytes 40992 | tf_op jit(solution)/shard_map/ppermute | solution.py:25
  112.1 0.6 fusion.31
  112.7 1.7 %all-to-all-done.1 = f16[32,16,1152]{2,1,0:T(8,128)(2,1)S(1)} async-done(((f16[32,16,1152]{2,1,0:T(8,128)(2,1)}), f16[32,16,1152]{2,1,0:T(8,128)(2,1)S(1)}, u32[]{:S(2)}, u32[]{:S(2)}) %all-to-all-start.1) | async-done | bytes 1179680 | tf_op jit(solution)/shard_map/all_to_all | solution.py:83
  114.4 0.2 convert_reduce_fusion
  114.6 0.2 fusion.27
  114.8 0.7 add_add_fusion.1
  115.5 0.7 add_add_fusion
  (25 shorter events, 0.3 us)
Async XLA Ops:
  0.6 22.2 %collective-permute-start = (bf16[16,1152]{1,0:T(8,128)(2,1)}, bf16[16,1152]{1,0:T(8,128)(2,1)S(1)}, u32[]{:S(2)}, u32[]{:S(2)}) collective-permute-start(bf16[16,1152]{1,0:T(8,128)(2,1)} %param.5), channel_id=1, source_target_pairs={{0,1},{1,0},{2,3},{3,2},{4,5},{5,4},{6,7},{7,6},{8,9},{9,8},{10,11... | collective-permute-start | bytes 110600 | tf_op jit(solution)/shard_map/ppermute | solution.py:25
  4.2 0.8 copy-start
  6.2 16.6 %copy-start.3 = (bf16[16,1152]{1,0:T(8,128)(2,1)S(1)}, bf16[16,1152]{1,0:T(8,128)(2,1)}, u32[]{:S(2)}) copy-start(bf16[16,1152]{1,0:T(8,128)(2,1)} %param.5) | copy-start | bytes 110596
  6.2 54.2 %all-to-all-start = ((bf16[32,16,1152]{2,1,0:T(8,128)(2,1)}), bf16[32,16,1152]{2,1,0:T(8,128)(2,1)S(1)}, u32[]{:S(2)}, u32[]{:S(2)}) async-start(bf16[32,16,1152]{2,1,0:T(8,128)(2,1)} %copies.1), calls=%async_computation | async-start | bytes 2359296 | tf_op jit(solution)/shard_map/all_to_all | solution.py:49
  21.4 38.8 %copy-start.2 = (s32[16384]{0:T(1024)S(1)}, s32[16384]{0:T(1024)}, u32[]{:S(2)}) copy-start(s32[16384]{0:T(1024)} %param.7) | copy-start | bytes 196612
  58.3 3.9 %collective-permute-start.1 = (bf16[256,1152]{1,0:T(8,128)(2,1)S(1)}, bf16[256,1152]{1,0:T(8,128)(2,1)S(1)}, u32[]{:S(2)}, u32[]{:S(2)}) collective-permute-start(bf16[256,1152]{1,0:T(8,128)(2,1)S(1)} %bitcast.67), channel_id=1, source_target_pairs={{0,16},{16,0},{1,17},{17,1},{2,18},{18,2},{3,19},{19,3},{4,20},{20... | collective-permute-start | bytes 1769480 | tf_op jit(solution)/shard_map/ppermute | solution.py:25
  62.2 1.3 %copy-start.5 = (bf16[256,1152]{1,0:T(8,128)(2,1)}, bf16[256,1152]{1,0:T(8,128)(2,1)S(1)}, u32[]{:S(2)}) copy-start(bf16[256,1152]{1,0:T(8,128)(2,1)S(1)} %collective-permute-done.1) | copy-start | bytes 1769476
  64.1 2.3 %copy-start.6 = (bf16[256,1152]{1,0:T(8,128)(2,1)S(1)}, bf16[256,1152]{1,0:T(8,128)(2,1)}, u32[]{:S(2)}) copy-start(bf16[256,1152]{1,0:T(8,128)(2,1)} %copy-done.5) | copy-start | bytes 1769476
  64.4 16.5 %collective-permute-start.2 = (f16[256,1280]{1,0:T(8,128)(2,1)S(1)}, f16[256,1280]{1,0:T(8,128)(2,1)}, u32[]{:S(2)}, u32[]{:S(2)}) collective-permute-start(f16[256,1280]{1,0:T(8,128)(2,1)S(1)} %pad_maximum_fusion), channel_id=1, source_target_pairs={{0,16},{16,0},{1,17},{17,1},{2,18},{18,2},{3,19},{19,3},{4,20},{20... | collective-permute-start | bytes 1966088 | tf_op jit(solution)/shard_map/ppermute | solution.py:25
  68.1 46.3 %all-to-all-start.1 = ((f16[32,16,1152]{2,1,0:T(8,128)(2,1)}), f16[32,16,1152]{2,1,0:T(8,128)(2,1)S(1)}, u32[]{:S(2)}, u32[]{:S(2)}) async-start(f16[32,16,1152]{2,1,0:T(8,128)(2,1)} %bitcast.74), calls=%async_computation.1 | async-start | bytes 2359296 | tf_op jit(solution)/shard_map/all_to_all | solution.py:83
  82.4 11.0 %collective-permute-start.3 = (f16[2,32,1280]{2,1,0:T(8,128)(2,1)S(1)}, f16[2,32,1280]{2,1,0:T(8,128)(2,1)S(1)}, u32[]{:S(2)}, u32[]{:S(2)}) collective-permute-start(f16[2,32,1280]{2,1,0:T(8,128)(2,1)S(1)} %pad_maximum_fusion.1), channel_id=1, source_target_pairs={{0,2},{2,4},{4,6},{6,8},{8,10},{10,12},{12,14},{14,0},{1,3},{3,5},... | collective-permute-start | bytes 491528 | tf_op jit(solution)/shard_map/ppermute | solution.py:25
  86.2 7.5 %collective-permute-start.4 = (f16[2,32,1280]{2,1,0:T(8,128)(2,1)S(1)}, f16[2,32,1280]{2,1,0:T(8,128)(2,1)S(1)}, u32[]{:S(2)}, u32[]{:S(2)}) collective-permute-start(f16[2,32,1280]{2,1,0:T(8,128)(2,1)S(1)} %pad_maximum_fusion.2), channel_id=1, source_target_pairs={{0,14},{2,0},{4,2},{6,4},{8,6},{10,8},{12,10},{14,12},{1,15},{3,1}... | collective-permute-start | bytes 491528 | tf_op jit(solution)/shard_map/ppermute | solution.py:25
  89.5 12.4 %collective-permute-start.7 = (f16[32,1280]{1,0:T(8,128)(2,1)S(1)}, f16[32,1280]{1,0:T(8,128)(2,1)S(1)}, u32[]{:S(2)}, u32[]{:S(2)}) collective-permute-start(f16[32,1280]{1,0:T(8,128)(2,1)S(1)} %get-tuple-element.17), channel_id=1, source_target_pairs={{0,8},{2,10},{4,12},{6,14},{8,0},{10,2},{12,4},{14,6},{1,9},{3,11}... | collective-permute-start | bytes 245768 | tf_op jit(solution)/shard_map/ppermute | solution.py:25
  93.7 9.5 %collective-permute-start.5 = (f16[32,1280]{1,0:T(8,128)(2,1)S(1)}, f16[32,1280]{1,0:T(8,128)(2,1)S(1)}, u32[]{:S(2)}, u32[]{:S(2)}) collective-permute-start(f16[32,1280]{1,0:T(8,128)(2,1)S(1)} %get-tuple-element.15), channel_id=1, source_target_pairs={{0,4},{2,6},{4,8},{6,10},{8,12},{10,14},{12,0},{14,2},{1,5},{3,7},... | collective-permute-start | bytes 245768 | tf_op jit(solution)/shard_map/ppermute | solution.py:25
  97.1 17.5 %copy-start.1 = (bf16[16,1152]{1,0:T(8,128)(2,1)S(1)}, bf16[16,1152]{1,0:T(8,128)(2,1)}, u32[]{:S(2)}) copy-start(bf16[16,1152]{1,0:T(8,128)(2,1)} %raw_ref.1) | copy-start | bytes 110596
  97.1 17.5 %copy-start.4 = (bf16[16,1152]{1,0:T(8,128)(2,1)S(1)}, bf16[16,1152]{1,0:T(8,128)(2,1)}, u32[]{:S(2)}) copy-start(bf16[16,1152]{1,0:T(8,128)(2,1)} %param.5) | copy-start | bytes 110596
  97.1 7.6 %collective-permute-start.6 = (f16[32,1280]{1,0:T(8,128)(2,1)S(1)}, f16[32,1280]{1,0:T(8,128)(2,1)S(1)}, u32[]{:S(2)}, u32[]{:S(2)}) collective-permute-start(f16[32,1280]{1,0:T(8,128)(2,1)S(1)} %get-tuple-element.16), channel_id=1, source_target_pairs={{0,12},{2,14},{4,0},{6,2},{8,4},{10,6},{12,8},{14,10},{1,13},{3,15... | collective-permute-start | bytes 245768 | tf_op jit(solution)/shard_map/ppermute | solution.py:25
  104.8 7.3 %collective-permute-start.8 = (f16[16,1280]{1,0:T(8,128)(2,1)S(1)}, f16[16,1280]{1,0:T(8,128)(2,1)S(1)}, u32[]{:S(2)}, u32[]{:S(2)}) collective-permute-start(f16[16,1280]{1,0:T(8,128)(2,1)S(1)} %slice_convert_fusion), channel_id=1, source_target_pairs={{0,1},{1,0},{2,3},{3,2},{4,5},{5,4},{6,7},{7,6},{8,9},{9,8},{10,11... | collective-permute-start | bytes 122888 | tf_op jit(solution)/shard_map/ppermute | solution.py:25

commit v13 on v12

--- a/solution.py
+++ b/solution.py
@@ -49,7 +49,12 @@
     return lax.all_to_all(copies, axes, 0, 0, tiled=True)
 
 
-def pairs_kernel(all_ref, after_ref, *pairs_refs):
+def pairs_kernel(all_ref, after_ref, own_ref, other_ref, texts_ref):
+    pairs_refs = (own_ref, other_ref)
+    text = lax.broadcasted_iota(jnp.int32, texts_ref.shape, 0) * 128
+    text = text + lax.broadcasted_iota(jnp.int32, texts_ref.shape, 1)
+    owner_rows = own_ref.shape[0] * 2 * 128
+    texts_ref[...] = text // 16 * owner_rows + lax.axis_index(IMAGE_GROUP) * 16 + text % 16
     group = lax.axis_index(TEXT_GROUP)
     core, z, ylo = [lax.axis_index(axis) for axis in IMAGE_GROUP]
     lane = lax.broadcasted_iota(jnp.int32, (1, 128), 1)
@@ -65,17 +70,18 @@
         pairs_refs[ahead][1:2, :] = jnp.where(lane + turn < 128, rows[1], rows[0])
 
 
-def image_pairs(caption_partner_position, core_images, after):
+def image_pairs(caption_partner_position, core_images, text_count, after):
     pairs = pl.pallas_call(
         pairs_kernel,
-        out_shape=[jax.ShapeDtypeStruct((core_images // 128, 128), jnp.int32)] * 2,
+        out_shape=[jax.ShapeDtypeStruct((core_images // 128, 128), jnp.int32)] * 2
+        + [jax.ShapeDtypeStruct((text_count // 128, 128), jnp.int32)],
         in_specs=[pl.BlockSpec(memory_space=pltpu.VMEM), pl.BlockSpec(memory_space=pl.ANY)],
-        out_specs=[pl.BlockSpec(memory_space=pltpu.VMEM)] * 2,
+        out_specs=[pl.BlockSpec(memory_space=pltpu.VMEM)] * 3,
         cost_estimate=pl.CostEstimate(flops=WAIT_FLOPS, bytes_accessed=0, transcendentals=0),
         compiler_params=pltpu.CompilerParams(vmem_limit_bytes=KERNEL_BYTES),
         name="pairs",
     )(caption_partner_position.reshape(-1, 128), after)
-    return [own_or_other.reshape(-1) for own_or_other in pairs]
+    return [indices.reshape(-1) for indices in pairs]
 
 
 def scatter(parts, axes):
@@ -109,10 +115,8 @@
     z_images = from_own(lax.all_gather(near_images, "z", axis=0, tiled=False), "z").reshape(-1, width)
     other_images = shift_by(z_images, "core", 1)
     image_count = 2 * z_images.shape[0]
-    own_pairs, other_pairs = image_pairs(caption_partner_position, image_count // 2, z_images[:16, :128])
-    column = jnp.arange(txt_block.shape[0], dtype=jnp.int32)
-    text_ids = (
-        column // own_rows * image_count + lax.axis_index(IMAGE_GROUP) * own_rows + column % own_rows
+    own_pairs, other_pairs, text_ids = image_pairs(
+        caption_partner_position, image_count // 2, txt_block.shape[0], z_images[:16, :128]
     )
 
     def compare(images, partners):

time: 117 us -> 117 us (level)
  no operation moved by 1% of the time
where the time goes in v13:
time: 117 us; the launch traced here: 116 us
  starting transfers between devices  57.1 us (49%)
  blocking collectives  35 us (30%)
  waiting for transfers between devices  9.42 us (8%)
  matrix products  5.36 us (5%)
  other arithmetic  4.62 us (4%)
  between operations  2.31 us (2%)
  Pallas kernels  1.35 us (1%)
    all_gather x1, blocking collectives, per_device(): lax.all_gather(near_images, 'z', axis=0, tiled=False)  35 us
    ppermute x9, starting transfers between devices, shift_by(): lax.ppermute(block, axis, [(i, (i + step) % count) for i in range(count)])  29.7 us
    all_to_all x1, starting transfers between devices, gather(): return lax.all_to_all(copies, axes, 0, 0, tiled=True)  15.2 us
    all_to_all x1, starting transfers between devices, scatter(): lax.all_to_all(parts.reshape(count, parts.shape[0] // count, parts.shape[...  12.1 us
    ppermute x9, waiting for transfers between devices, shift_by(): lax.ppermute(block, axis, [(i, (i + step) % count) for i in range(count)])  7.67 us
  transfers between devices with their start and end apart: 11, of which 6 were waited for; matrix products, arithmetic and copies ran while one was open for 5% of the time, Pallas kernels for 1%

profile of v13, /device:TPU:2, one launch (start us, length us, event | category | flops | bytes accessed | tf_op | source)
XLA Modules:
  0.0 116.2 jit_solution(5226235459678168663)
XLA Ops:
  0.6 3.6 %collective-permute-start = (bf16[16,1152]{1,0:T(8,128)(2,1)}, bf16[16,1152]{1,0:T(8,128)(2,1)S(1)}, u32[]{:S(2)}, u32[]{:S(2)}) collective-permute-start(bf16[16,1152]{1,0:T(8,128)(2,1)} %param.5), channel_id=1, source_target_pairs={{0,1},{1,0},{2,3},{3,2},{4,5},{5,4},{6,7},{7,6},{8,9},{9,8},{10,11... | collective-permute-start | bytes 110600 | tf_op jit(solution)/shard_map/ppermute | solution.py:25
  4.2 0.0 copy-start
  4.2 0.8 copy-done
  5.0 1.2 %copies.1 = bf16[32,16,1152]{2,1,0:T(8,128)(2,1)} custom-call(bf16[16,1152]{1,0:T(8,128)(2,1)S(1)} %copy-done), custom_call_target="tpu_custom_call" | custom-call | tf_op jit(solution)/shard_map/copies/pallas_call | solution.py:41
  6.2 15.2 %all-to-all-start = ((bf16[32,16,1152]{2,1,0:T(8,128)(2,1)}), bf16[32,16,1152]{2,1,0:T(8,128)(2,1)S(1)}, u32[]{:S(2)}, u32[]{:S(2)}) async-start(bf16[32,16,1152]{2,1,0:T(8,128)(2,1)} %copies.1), calls=%async_computation | async-start | bytes 2359296 | tf_op jit(solution)/shard_map/all_to_all | solution.py:49
  21.4 0.0 copy-start.2
  22.8 0.0 collective-permute-done
  22.8 0.1 multiply_reduce_fusion
  22.9 0.1 multiply_convert_fusion
  23.0 35.0 %all_gather.4 = bf16[8,32,1152]{2,1,0:T(8,128)(2,1)S(1)} all-gather(bf16[1,32,1152]{2,1,0:T(8,128)(2,1)S(1)} %multiply_convert_fusion), channel_id=1, replica_groups=mesh['yhi'=4,'x'=8,'core'=2,'z'=8,'ylo'=2] {'z'}, dimensions={0}, use_global_device_ids=true | all-gather | bytes 663552 | tf_op jit(solution)/shard_map/all_gather | solution.py:115
  58.0 0.2 fusion.5
  58.3 1.9 %collective-permute-start.1 = (bf16[256,1152]{1,0:T(8,128)(2,1)S(1)}, bf16[256,1152]{1,0:T(8,128)(2,1)S(1)}, u32[]{:S(2)}, u32[]{:S(2)}) collective-permute-start(bf16[256,1152]{1,0:T(8,128)(2,1)S(1)} %bitcast.73), channel_id=1, source_target_pairs={{0,16},{16,0},{1,17},{17,1},{2,18},{18,2},{3,19},{19,3},{4,20},{20... | collective-permute-start | bytes 1769480 | tf_op jit(solution)/shard_map/ppermute | solution.py:25
  60.2 0.2 pairs.1
  60.4 0.6 fusion.4
  60.9 0.6 fusion.34
  61.6 0.6 collective-permute-done.1
  62.2 1.3 %fusion.17 = (f32[256]{0:T(256)S(1)}, f32[256]{0:T(256)S(1)}, f32[256,512]{1,0:T(8,128)S(1)}) fusion(s32[512]{0:T(512)S(1)} %bitcast.61, s32[256]{0:T(256)S(1)} %bitcast.69, f32[256,512]{1,0:T(8,128)S(1)} %fusion.4, s32[256]{0:T(256)S(1)} %bitcast.66, f32[]{:T(128)} %bitcast.59, bf16[256,1152]{1,0:T(8,128)(2,1)S(1)} %collective-permute-done.1, ...), kind=kOutput, calls=%fused_computation.33 | convolution fusion | flops 305397248 | bytes 2824200 | tf_op jit(solution)/shard_map/dot_general | solution.py:125
  63.5 0.6 fusion.2
  64.1 0.1 broadcast_in_dim.9
  64.2 0.2 pad_maximum_fusion
  64.4 2.1 %collective-permute-start.2 = (f16[256,1280]{1,0:T(8,128)(2,1)S(1)}, f16[256,1280]{1,0:T(8,128)(2,1)}, u32[]{:S(2)}, u32[]{:S(2)}) collective-permute-start(f16[256,1280]{1,0:T(8,128)(2,1)S(1)} %pad_maximum_fusion), channel_id=1, source_target_pairs={{0,16},{16,0},{1,17},{17,1},{2,18},{18,2},{3,19},{19,3},{4,20},{20... | collective-permute-start | bytes 1966088 | tf_op jit(solution)/shard_map/ppermute | solution.py:25
  66.4 1.7 %fusion.1 = f16[512,1152]{1,0:T(8,128)(2,1)} fusion(f32[512,1152]{1,0:T(8,128)S(1)} %fusion.34, bf16[256,1152]{1,0:T(8,128)(2,1)S(1)} %copy-done.6, f32[256,512]{1,0:T(8,128)S(1)} %get-tuple-element.28, s32[512]{0:T(512)S(1)} %bitcast.63, s32[256]{0:T(256)S(1)} %bitcast.71), kind=kOutput, calls=%fused_computation.2 | convolution fusion | flops 304676864 | bytes 4656128 | tf_op jit(solution)/shard_map/dot_general | solution.py:141
  68.1 12.1 %all-to-all-start.1 = ((f16[32,16,1152]{2,1,0:T(8,128)(2,1)}), f16[32,16,1152]{2,1,0:T(8,128)(2,1)S(1)}, u32[]{:S(2)}, u32[]{:S(2)}) async-start(f16[32,16,1152]{2,1,0:T(8,128)(2,1)} %bitcast.80), calls=%async_computation.1 | async-start | bytes 2359296 | tf_op jit(solution)/shard_map/all_to_all | solution.py:89
  80.2 0.6 convolution_multiply_fusion.1
  80.9 0.1 broadcast_in_dim.8
  81.0 1.3 %fusion.37 = (f16[256,1280]{1,0:T(8,128)(2,1)S(1)}, f32[256,1280]{1,0:T(8,128)S(1)}) fusion(f16[256,1280]{1,0:T(8,128)(2,1)} %collective-permute-done.2, f32[256,128]{1,0:T(8,128)S(1)} %broadcast_in_dim.8, f32[256,1152]{1,0:T(8,128)S(1)} %convolution_multiply_fusion.1), kind=kLoop, calls=%fused_computation.80 | loop fusion | flops 1310720 | bytes 3932160 | tf_op jit(solution)/shard_map/convert.13
  82.2 0.1 fusion.38
  82.4 3.7 %collective-permute-start.3 = (f16[2,32,1280]{2,1,0:T(8,128)(2,1)S(1)}, f16[2,32,1280]{2,1,0:T(8,128)(2,1)S(1)}, u32[]{:S(2)}, u32[]{:S(2)}) collective-permute-start(f16[2,32,1280]{2,1,0:T(8,128)(2,1)S(1)} %pad_maximum_fusion.1), channel_id=1, source_target_pairs={{0,2},{2,4},{4,6},{6,8},{8,10},{10,12},{12,14},{14,0},{1,3},{3,5},... | collective-permute-start | bytes 491528 | tf_op jit(solution)/shard_map/ppermute | solution.py:25
  86.1 3.3 %collective-permute-start.4 = (f16[2,32,1280]{2,1,0:T(8,128)(2,1)S(1)}, f16[2,32,1280]{2,1,0:T(8,128)(2,1)S(1)}, u32[]{:S(2)}, u32[]{:S(2)}) collective-permute-start(f16[2,32,1280]{2,1,0:T(8,128)(2,1)S(1)} %pad_maximum_fusion.2), channel_id=1, source_target_pairs={{0,14},{2,0},{4,2},{6,4},{8,6},{10,8},{12,10},{14,12},{1,15},{3,1}... | collective-permute-start | bytes 491528 | tf_op jit(solution)/shard_map/ppermute | solution.py:25
  89.5 3.9 %collective-permute-start.7 = (f16[32,1280]{1,0:T(8,128)(2,1)S(1)}, f16[32,1280]{1,0:T(8,128)(2,1)S(1)}, u32[]{:S(2)}, u32[]{:S(2)}) collective-permute-start(f16[32,1280]{1,0:T(8,128)(2,1)S(1)} %get-tuple-element.19), channel_id=1, source_target_pairs={{0,8},{2,10},{4,12},{6,14},{8,0},{10,2},{12,4},{14,6},{1,9},{3,11}... | collective-permute-start | bytes 245768 | tf_op jit(solution)/shard_map/ppermute | solution.py:25
  93.4 0.0 collective-permute-done.3
  93.4 0.2 collective-permute-done.4
  93.7 3.3 %collective-permute-start.5 = (f16[32,1280]{1,0:T(8,128)(2,1)S(1)}, f16[32,1280]{1,0:T(8,128)(2,1)S(1)}, u32[]{:S(2)}, u32[]{:S(2)}) collective-permute-start(f16[32,1280]{1,0:T(8,128)(2,1)S(1)} %get-tuple-element.17), channel_id=1, source_target_pairs={{0,4},{2,6},{4,8},{6,10},{8,12},{10,14},{12,0},{14,2},{1,5},{3,7},... | collective-permute-start | bytes 245768 | tf_op jit(solution)/shard_map/ppermute | solution.py:25
  97.1 0.0 copy-start.1
  97.1 0.0 copy-start.4
  97.1 4.8 %collective-permute-start.6 = (f16[32,1280]{1,0:T(8,128)(2,1)S(1)}, f16[32,1280]{1,0:T(8,128)(2,1)S(1)}, u32[]{:S(2)}, u32[]{:S(2)}) collective-permute-start(f16[32,1280]{1,0:T(8,128)(2,1)S(1)} %get-tuple-element.18), channel_id=1, source_target_pairs={{0,12},{2,14},{4,0},{6,2},{8,4},{10,6},{12,8},{14,10},{1,13},{3,15... | collective-permute-start | bytes 245768 | tf_op jit(solution)/shard_map/ppermute | solution.py:25
  101.9 0.0 collective-permute-done.7
  101.9 1.3 %collective-permute-done.5 = f16[32,1280]{1,0:T(8,128)(2,1)S(1)} collective-permute-done((f16[32,1280]{1,0:T(8,128)(2,1)S(1)}, f16[32,1280]{1,0:T(8,128)(2,1)S(1)}, u32[]{:S(2)}, u32[]{:S(2)}) %collective-permute-start.5) | collective-permute-done | bytes 81952 | tf_op jit(solution)/shard_map/ppermute | solution.py:25
  103.2 1.5 %collective-permute-done.6 = f16[32,1280]{1,0:T(8,128)(2,1)S(1)} collective-permute-done((f16[32,1280]{1,0:T(8,128)(2,1)S(1)}, f16[32,1280]{1,0:T(8,128)(2,1)S(1)}, u32[]{:S(2)}, u32[]{:S(2)}) %collective-permute-start.6) | collective-permute-done | bytes 81952 | tf_op jit(solution)/shard_map/ppermute | solution.py:25
  104.7 0.1 fusion.25
  104.8 3.1 %collective-permute-start.8 = (f16[16,1280]{1,0:T(8,128)(2,1)S(1)}, f16[16,1280]{1,0:T(8,128)(2,1)S(1)}, u32[]{:S(2)}, u32[]{:S(2)}) collective-permute-start(f16[16,1280]{1,0:T(8,128)(2,1)S(1)} %slice_convert_fusion), channel_id=1, source_target_pairs={{0,1},{1,0},{2,3},{3,2},{4,5},{5,4},{6,7},{7,6},{8,9},{9,8},{10,11... | collective-permute-start | bytes 122888 | tf_op jit(solution)/shard_map/ppermute | solution.py:25
  107.9 4.0 %collective-permute-done.8 = f16[16,1280]{1,0:T(8,128)(2,1)S(1)} collective-permute-done((f16[16,1280]{1,0:T(8,128)(2,1)S(1)}, f16[16,1280]{1,0:T(8,128)(2,1)S(1)}, u32[]{:S(2)}, u32[]{:S(2)}) %collective-permute-start.8) | collective-permute-done | bytes 40992 | tf_op jit(solution)/shard_map/ppermute | solution.py:25
  112.0 0.6 fusion.31
  112.6 1.7 %all-to-all-done.1 = f16[32,16,1152]{2,1,0:T(8,128)(2,1)S(1)} async-done(((f16[32,16,1152]{2,1,0:T(8,128)(2,1)}), f16[32,16,1152]{2,1,0:T(8,128)(2,1)S(1)}, u32[]{:S(2)}, u32[]{:S(2)}) %all-to-all-start.1) | async-done | bytes 1179680 | tf_op jit(solution)/shard_map/all_to_all | solution.py:89
  114.4 0.2 convert_reduce_fusion
  114.6 0.2 fusion.27
  114.8 0.7 add_add_fusion.1
  115.5 0.7 add_add_fusion
  (24 shorter events, 0.3 us)
Async XLA Ops:
  0.6 22.1 %collective-permute-start = (bf16[16,1152]{1,0:T(8,128)(2,1)}, bf16[16,1152]{1,0:T(8,128)(2,1)S(1)}, u32[]{:S(2)}, u32[]{:S(2)}) collective-permute-start(bf16[16,1152]{1,0:T(8,128)(2,1)} %param.5), channel_id=1, source_target_pairs={{0,1},{1,0},{2,3},{3,2},{4,5},{5,4},{6,7},{7,6},{8,9},{9,8},{10,11... | collective-permute-start | bytes 110600 | tf_op jit(solution)/shard_map/ppermute | solution.py:25
  4.2 0.8 copy-start
  6.2 16.6 %copy-start.3 = (bf16[16,1152]{1,0:T(8,128)(2,1)S(1)}, bf16[16,1152]{1,0:T(8,128)(2,1)}, u32[]{:S(2)}) copy-start(bf16[16,1152]{1,0:T(8,128)(2,1)} %param.5) | copy-start | bytes 110596
  6.2 54.2 %all-to-all-start = ((bf16[32,16,1152]{2,1,0:T(8,128)(2,1)}), bf16[32,16,1152]{2,1,0:T(8,128)(2,1)S(1)}, u32[]{:S(2)}, u32[]{:S(2)}) async-start(bf16[32,16,1152]{2,1,0:T(8,128)(2,1)} %copies.1), calls=%async_computation | async-start | bytes 2359296 | tf_op jit(solution)/shard_map/all_to_all | solution.py:49
  21.4 38.8 %copy-start.2 = (s32[16384]{0:T(1024)S(1)}, s32[16384]{0:T(1024)}, u32[]{:S(2)}) copy-start(s32[16384]{0:T(1024)} %param.7) | copy-start | bytes 196612
  58.3 3.9 %collective-permute-start.1 = (bf16[256,1152]{1,0:T(8,128)(2,1)S(1)}, bf16[256,1152]{1,0:T(8,128)(2,1)S(1)}, u32[]{:S(2)}, u32[]{:S(2)}) collective-permute-start(bf16[256,1152]{1,0:T(8,128)(2,1)S(1)} %bitcast.73), channel_id=1, source_target_pairs={{0,16},{16,0},{1,17},{17,1},{2,18},{18,2},{3,19},{19,3},{4,20},{20... | collective-permute-start | bytes 1769480 | tf_op jit(solution)/shard_map/ppermute | solution.py:25
  62.2 1.3 %copy-start.5 = (bf16[256,1152]{1,0:T(8,128)(2,1)}, bf16[256,1152]{1,0:T(8,128)(2,1)S(1)}, u32[]{:S(2)}) copy-start(bf16[256,1152]{1,0:T(8,128)(2,1)S(1)} %collective-permute-done.1) | copy-start | bytes 1769476
  64.1 2.3 %copy-start.6 = (bf16[256,1152]{1,0:T(8,128)(2,1)S(1)}, bf16[256,1152]{1,0:T(8,128)(2,1)}, u32[]{:S(2)}) copy-start(bf16[256,1152]{1,0:T(8,128)(2,1)} %copy-done.5) | copy-start | bytes 1769476
  64.4 16.5 %collective-permute-start.2 = (f16[256,1280]{1,0:T(8,128)(2,1)S(1)}, f16[256,1280]{1,0:T(8,128)(2,1)}, u32[]{:S(2)}, u32[]{:S(2)}) collective-permute-start(f16[256,1280]{1,0:T(8,128)(2,1)S(1)} %pad_maximum_fusion), channel_id=1, source_target_pairs={{0,16},{16,0},{1,17},{17,1},{2,18},{18,2},{3,19},{19,3},{4,20},{20... | collective-permute-start | bytes 1966088 | tf_op jit(solution)/shard_map/ppermute | solution.py:25
  68.1 46.3 %all-to-all-start.1 = ((f16[32,16,1152]{2,1,0:T(8,128)(2,1)}), f16[32,16,1152]{2,1,0:T(8,128)(2,1)S(1)}, u32[]{:S(2)}, u32[]{:S(2)}) async-start(f16[32,16,1152]{2,1,0:T(8,128)(2,1)} %bitcast.80), calls=%async_computation.1 | async-start | bytes 2359296 | tf_op jit(solution)/shard_map/all_to_all | solution.py:89
  82.4 11.0 %collective-permute-start.3 = (f16[2,32,1280]{2,1,0:T(8,128)(2,1)S(1)}, f16[2,32,1280]{2,1,0:T(8,128)(2,1)S(1)}, u32[]{:S(2)}, u32[]{:S(2)}) collective-permute-start(f16[2,32,1280]{2,1,0:T(8,128)(2,1)S(1)} %pad_maximum_fusion.1), channel_id=1, source_target_pairs={{0,2},{2,4},{4,6},{6,8},{8,10},{10,12},{12,14},{14,0},{1,3},{3,5},... | collective-permute-start | bytes 491528 | tf_op jit(solution)/shard_map/ppermute | solution.py:25
  86.1 7.5 %collective-permute-start.4 = (f16[2,32,1280]{2,1,0:T(8,128)(2,1)S(1)}, f16[2,32,1280]{2,1,0:T(8,128)(2,1)S(1)}, u32[]{:S(2)}, u32[]{:S(2)}) collective-permute-start(f16[2,32,1280]{2,1,0:T(8,128)(2,1)S(1)} %pad_maximum_fusion.2), channel_id=1, source_target_pairs={{0,14},{2,0},{4,2},{6,4},{8,6},{10,8},{12,10},{14,12},{1,15},{3,1}... | collective-permute-start | bytes 491528 | tf_op jit(solution)/shard_map/ppermute | solution.py:25
  89.5 12.4 %collective-permute-start.7 = (f16[32,1280]{1,0:T(8,128)(2,1)S(1)}, f16[32,1280]{1,0:T(8,128)(2,1)S(1)}, u32[]{:S(2)}, u32[]{:S(2)}) collective-permute-start(f16[32,1280]{1,0:T(8,128)(2,1)S(1)} %get-tuple-element.19), channel_id=1, source_target_pairs={{0,8},{2,10},{4,12},{6,14},{8,0},{10,2},{12,4},{14,6},{1,9},{3,11}... | collective-permute-start | bytes 245768 | tf_op jit(solution)/shard_map/ppermute | solution.py:25
  93.7 9.4 %collective-permute-start.5 = (f16[32,1280]{1,0:T(8,128)(2,1)S(1)}, f16[32,1280]{1,0:T(8,128)(2,1)S(1)}, u32[]{:S(2)}, u32[]{:S(2)}) collective-permute-start(f16[32,1280]{1,0:T(8,128)(2,1)S(1)} %get-tuple-element.17), channel_id=1, source_target_pairs={{0,4},{2,6},{4,8},{6,10},{8,12},{10,14},{12,0},{14,2},{1,5},{3,7},... | collective-permute-start | bytes 245768 | tf_op jit(solution)/shard_map/ppermute | solution.py:25
  97.1 17.5 %copy-start.1 = (bf16[16,1152]{1,0:T(8,128)(2,1)S(1)}, bf16[16,1152]{1,0:T(8,128)(2,1)}, u32[]{:S(2)}) copy-start(bf16[16,1152]{1,0:T(8,128)(2,1)} %raw_ref.1) | copy-start | bytes 110596
  97.1 17.5 %copy-start.4 = (bf16[16,1152]{1,0:T(8,128)(2,1)S(1)}, bf16[16,1152]{1,0:T(8,128)(2,1)}, u32[]{:S(2)}) copy-start(bf16[16,1152]{1,0:T(8,128)(2,1)} %param.5) | copy-start | bytes 110596
  97.1 7.6 %collective-permute-start.6 = (f16[32,1280]{1,0:T(8,128)(2,1)S(1)}, f16[32,1280]{1,0:T(8,128)(2,1)S(1)}, u32[]{:S(2)}, u32[]{:S(2)}) collective-permute-start(f16[32,1280]{1,0:T(8,128)(2,1)S(1)} %get-tuple-element.18), channel_id=1, source_target_pairs={{0,12},{2,14},{4,0},{6,2},{8,4},{10,6},{12,8},{14,10},{1,13},{3,15... | collective-permute-start | bytes 245768 | tf_op jit(solution)/shard_map/ppermute | solution.py:25
  104.8 7.2 %collective-permute-start.8 = (f16[16,1280]{1,0:T(8,128)(2,1)S(1)}, f16[16,1280]{1,0:T(8,128)(2,1)S(1)}, u32[]{:S(2)}, u32[]{:S(2)}) collective-permute-start(f16[16,1280]{1,0:T(8,128)(2,1)S(1)} %slice_convert_fusion), channel_id=1, source_target_pairs={{0,1},{1,0},{2,3},{3,2},{4,5},{5,4},{6,7},{7,6},{8,9},{9,8},{10,11... | collective-permute-start | bytes 122888 | tf_op jit(solution)/shard_map/ppermute | solution.py:25
